TPU v7x, 32 devices: a whole 2x2x4 slice. The times are simulated.
32 devices in a mesh: head: 1, seq: 32 (over z, y, x, core).
Axes of the slice: x: 2, y: 2, z: 4, core: 2. Of those that a mesh axis runs over, the one named last changes fastest.
Arguments:
- queries: bfloat16 [8192, 4096], P('seq', 'head'), may hold values from -6 to 6
- keys: bfloat16 [8192, 4096], P('seq', 'head'), may hold values from -6 to 6
- values: bfloat16 [8192, 4096], P('seq', 'head'), may hold values from -6 to 6
- token_rates: float32 [16, 8192], P('head', 'seq'), may hold values from 0.05 to 1
- w_gate: bfloat16 [16, 256, 512], P('head'), may hold values from -6 to 6
- w_up: bfloat16 [16, 256, 512], P('head'), may hold values from -6 to 6
- w_down: bfloat16 [16, 512, 256], P('head'), may hold values from -6 to 6
Outputs:
- applied: bfloat16 [8192, 4096], P('seq', 'head')
- step_gate: bfloat16 [16, 256, 512], P('head')
- step_up: bfloat16 [16, 256, 512], P('head')
- step_down: bfloat16 [16, 256, 512], P('head')
All inputs are finite; a program needn't handle non-finite values.
Results may differ from a plain program's by a relative error of at most 0.035.
Values may be sent and summed in bfloat16 or wider, within the bound.
No kernel may reach another device: no remote copies, remote signals or barrier semaphores. Data moves between devices by JAX's collectives and lax.ppermute only.
A program may use at most 192 MiB of HBM per device.

v0:
```python
import math

import jax
import jax.numpy as jnp
from jax import lax
from jax.sharding import PartitionSpec as P

NS_STEPS = 5


def newton_batch(xmat, width):
    for step in range(NS_STEPS):
        amat = jnp.einsum("mdf,mef->mde", xmat, xmat, preferred_element_type=jnp.float32).astype(
            jnp.bfloat16
        )
        square = jnp.einsum("mde,mef->mdf", amat, amat, preferred_element_type=jnp.float32)
        bmat = (-4.775 * amat.astype(jnp.float32) + 2.0315 * square).astype(jnp.bfloat16)
        nxt = 3.4445 * xmat.astype(jnp.float32) + jnp.einsum(
            "mde,mef->mdf", bmat, xmat, preferred_element_type=jnp.float32
        )
        if step == NS_STEPS - 1:
            nxt = nxt * (0.2 * math.sqrt(width))
        xmat = nxt.astype(jnp.bfloat16)
    return xmat


def per_device(queries, keys, values, token_rates, w_gate, w_up, w_down):
    head_count, head_size, hidden = w_gate.shape
    tokens = queries.shape[0]
    scale_one = head_size ** (-0.5)
    scale_two = hidden ** (-0.5)
    qpart = queries.reshape(tokens, head_count, head_size)
    kpart = keys.reshape(tokens, head_count, head_size)
    vpart = values.reshape(tokens, head_count, head_size)
    gq = scale_one * jnp.einsum("thd,hdf->htf", qpart, w_gate, preferred_element_type=jnp.float32)
    uq = scale_one * jnp.einsum("thd,hdf->htf", qpart, w_up, preferred_element_type=jnp.float32)
    hq = (jax.nn.silu(gq) * uq).astype(jnp.bfloat16)
    applied = (
        scale_two * jnp.einsum("htf,hfd->thd", hq, w_down, preferred_element_type=jnp.float32)
    ).astype(jnp.bfloat16)
    applied = applied.reshape(tokens, head_count * head_size)
    gk = scale_one * jnp.einsum("thd,hdf->htf", kpart, w_gate, preferred_element_type=jnp.float32)
    uk = scale_one * jnp.einsum("thd,hdf->htf", kpart, w_up, preferred_element_type=jnp.float32)
    hk = (jax.nn.silu(gk) * uk).astype(jnp.bfloat16)
    vrate = (jnp.transpose(token_rates)[:, :, None] * vpart.astype(jnp.float32)).astype(
        jnp.bfloat16
    )
    gdown = -scale_two * jnp.einsum("thd,htf->hdf", vrate, hk, preferred_element_type=jnp.float32)
    dhid = -scale_two * jnp.einsum(
        "thd,hfd->htf", vrate, w_down, preferred_element_type=jnp.float32
    )
    sig = jax.nn.sigmoid(gk)
    dgate = (dhid * uk * sig * (1.0 + gk * (1.0 - sig))).astype(jnp.bfloat16)
    dup = (dhid * jax.nn.silu(gk)).astype(jnp.bfloat16)
    ggate = scale_one * jnp.einsum("thd,htf->hdf", kpart, dgate, preferred_element_type=jnp.float32)
    gup = scale_one * jnp.einsum("thd,htf->hdf", kpart, dup, preferred_element_type=jnp.float32)
    stacked = jnp.stack([ggate, gup, gdown], axis=1)
    total = lax.psum(stacked, "seq")
    norms = jnp.sqrt(jnp.sum(total * total, axis=(2, 3)))
    xmat = (total / (norms[:, :, None, None] + 1e-07)).astype(jnp.bfloat16)
    result = newton_batch(xmat.reshape(head_count * 3, head_size, hidden), hidden)
    result = result.reshape(head_count, 3, head_size, hidden)
    return (applied, result[:, 0], result[:, 1], result[:, 2])


def solution(mesh):
    in_specs = (
        P("seq", "head"),
        P("seq", "head"),
        P("seq", "head"),
        P("head", "seq"),
        P("head", None, None),
        P("head", None, None),
        P("head", None, None),
    )
    out_specs = (
        P("seq", "head"),
        P("head", None, None),
        P("head", None, None),
        P("head", None, None),
    )
    return jax.shard_map(
        per_device, mesh=mesh, in_specs=in_specs, out_specs=out_specs, check_vma=False
    )
```

profile of v0, /device:TPU:0, one launch (start us, length us, event | category | flops | bytes accessed | tf_op | source)
XLA Modules:
  0.0 704.0 jit_solution(1460333214064800515)
XLA Ops:
  7.2 4.3 copy.50
  16.2 5.3 fusion.43
  25.4 4.7 fusion.60
  30.1 10.2 %multiply_bitcast_fusion = f32[16,1,256,512]{3,2,0,1:T(8,128)} fusion(f32[16,256,512]{2,1,0:T(8,128)} %fusion.43, f32[16,256,512]{2,1,0:T(8,128)S(1)} %fusion.41, f32[256,16,256]{0,2,1:T(8,128)S(1)} %bitcast.82, f32[256,16]{0,1:T(8,128)S(1)} %bitcast.92), kind=kOutput, calls=%fused_computation.13 | convolution fusion | flops 1094713344 | bytes 29376512 | tf_op jit(solution)/shard_map/thd,htf->hdf/dot_general | solution.py:48
  40.4 10.6 %multiply_bitcast_fusion.2 = f32[16,1,256,512]{3,2,0,1:T(8,128)} fusion(f32[16,256,512]{2,1,0:T(8,128)S(1)} %fusion.41, f32[16,256,512]{2,1,0:T(8,128)} %fusion.43, f32[16,256,512]{2,1,0:T(8,128)} %fusion.60, bf16[32,16,8,256]{3,2,1,0:T(8,128)(2,1)S(1)} %bitcast.86), kind=kOutput, calls=%fused_computation.17 | convolution fusion | flops 1103101952 | bytes 35651584 | tf_op jit(solution)/shard_map/thd,htf->hdf/dot_general | solution.py:55
  51.0 12.4 %multiply_bitcast_fusion.1 = f32[16,1,256,512]{3,2,0,1:T(8,128)} fusion(f32[16,256,512]{2,1,0:T(8,128)} %fusion.60, bf16[32,16,8,256]{3,2,1,0:T(8,128)(2,1)S(1)} %bitcast.87, f32[16,256,512]{2,1,0:T(8,128)} %copy-done.3), kind=kOutput, calls=%fused_computation.15 | convolution fusion | flops 1092616192 | bytes 27262976 | tf_op jit(solution)/shard_map/thd,htf->hdf/dot_general | solution.py:56
  63.5 18.0 %pad_maximum_fusion = f32[16,3,256,512]{3,2,0,1:T(8,128)} fusion(f32[16,1,256,512]{3,2,0,1:T(8,128)} %multiply_bitcast_fusion, f32[16,1,256,512]{3,2,0,1:T(8,128)} %multiply_bitcast_fusion.1, f32[16,1,256,512]{3,2,0,1:T(8,128)} %multiply_bitcast_fusion.2), kind=kLoop, calls=%fused_computation | loop fusion | flops 12582912 | bytes 50331648 | tf_op jit(solution)/shard_map/stack | solution.py:57
  83.0 6.7 fusion.47
  89.7 12.0 %multiply_convert_fusion.8 = bf16[16,256,256]{1,2,0:T(8,128)(2,1)} fusion(bf16[16,512,256]{2,1,0:T(8,128)(2,1)} %param.13, f32[16,256,512]{2,1,0:T(8,128)} %fusion.47, bf16[16,256,512]{2,1,0:T(8,128)(2,1)} %param.12, bf16[32,16,8,256]{3,2,1,0:T(8,128)(2,1)S(1)} %bitcast.89), kind=kOutput, calls=%fused_computation.39 | convolution fusion | flops 2166358016 | bytes 20971520 | tf_op jit(solution)/shard_map/htf,hfd->thd/dot_general | solution.py:39
  105.8 368.6 %all-reduce.2.cloned.1.call-done = f32[16,3,256,512]{3,2,0,1:T(8,128)} async-done(((f32[16,3,256,512]{3,2,0,1:T(8,128)}), f32[16,3,256,512]{3,2,0,1:T(8,128)}) %all-reduce.2.cloned.1.call-update) | async-done | bytes 25165840 | tf_op jit(solution)/shard_map/psum | solution.py:58
  474.4 10.5 %multiply_reduce_fusion = f32[16,3]{0,1:T(4,128)S(1)} fusion(f32[16,3,256,512]{3,2,0,1:T(8,128)} %all-reduce.2.cloned.1.call-done), kind=kLoop, calls=%fused_computation.7 | loop fusion | flops 12582864 | bytes 25166016 | tf_op jit(solution)/shard_map/reduce_sum | solution.py:59
  484.9 4.9 copy-done
  493.7 5.6 copy.39
  499.3 13.8 %fusion.81 = bf16[48,256,256]{2,1,0:T(8,128)(2,1)} fusion(bf16[48,256,512]{2,1,0:T(8,128)(2,1)} %bitcast.79), kind=kOutput, calls=%fused_computation.91 | convolution fusion | flops 3221225472 | bytes 18874368 | tf_op jit(solution)/shard_map/mdf,mef->mde/dot_general | solution.py:13
  513.1 23.8 %add_convert_fusion.3 = bf16[48,256,512]{2,1,0:T(8,128)(2,1)} fusion(bf16[48,256,512]{2,1,0:T(8,128)(2,1)} %bitcast.80, bf16[48,256,256]{2,1,0:T(8,128)(2,1)} %fusion.81), kind=kOutput, calls=%fused_computation.5 | convolution fusion | flops 4872732672 | bytes 31457280 | tf_op jit(solution)/shard_map/mde,mef->mdf/dot_general | solution.py:18
  536.9 13.3 %fusion.82 = bf16[48,256,256]{2,1,0:T(8,128)(2,1)} fusion(bf16[48,256,512]{2,1,0:T(8,128)(2,1)} %add_convert_fusion.3), kind=kOutput, calls=%fused_computation.92 | convolution fusion | flops 3221225472 | bytes 18874368 | tf_op jit(solution)/shard_map/mdf,mef->mde/dot_general | solution.py:13
  550.1 24.0 %add_convert_fusion.2 = bf16[48,256,512]{2,1,0:T(8,128)(2,1)} fusion(bf16[48,256,512]{2,1,0:T(8,128)(2,1)} %add_convert_fusion.3, bf16[48,256,256]{2,1,0:T(8,128)(2,1)} %fusion.82), kind=kOutput, calls=%fused_computation.4 | convolution fusion | flops 4872732672 | bytes 31457280 | tf_op jit(solution)/shard_map/mde,mef->mdf/dot_general | solution.py:18
  574.2 13.6 %fusion.83 = bf16[48,256,256]{2,1,0:T(8,128)(2,1)} fusion(bf16[48,256,512]{2,1,0:T(8,128)(2,1)} %add_convert_fusion.2), kind=kOutput, calls=%fused_computation.93 | convolution fusion | flops 3221225472 | bytes 18874368 | tf_op jit(solution)/shard_map/mdf,mef->mde/dot_general | solution.py:13
  587.8 23.8 %add_convert_fusion.1 = bf16[48,256,512]{2,1,0:T(8,128)(2,1)} fusion(bf16[48,256,512]{2,1,0:T(8,128)(2,1)} %add_convert_fusion.2, bf16[48,256,256]{2,1,0:T(8,128)(2,1)} %fusion.83), kind=kOutput, calls=%fused_computation.3 | convolution fusion | flops 4872732672 | bytes 31457280 | tf_op jit(solution)/shard_map/mde,mef->mdf/dot_general | solution.py:18
  611.5 13.5 %fusion.84 = bf16[48,256,256]{2,1,0:T(8,128)(2,1)} fusion(bf16[48,256,512]{2,1,0:T(8,128)(2,1)} %add_convert_fusion.1), kind=kOutput, calls=%fused_computation.94 | convolution fusion | flops 3221225472 | bytes 18874368 | tf_op jit(solution)/shard_map/mdf,mef->mde/dot_general | solution.py:13
  625.1 24.0 %add_convert_fusion = bf16[48,256,512]{2,1,0:T(8,128)(2,1)} fusion(bf16[48,256,512]{2,1,0:T(8,128)(2,1)} %add_convert_fusion.1, bf16[48,256,256]{2,1,0:T(8,128)(2,1)} %fusion.84), kind=kOutput, calls=%fused_computation.2 | convolution fusion | flops 4872732672 | bytes 31457280 | tf_op jit(solution)/shard_map/mde,mef->mdf/dot_general | solution.py:18
  649.1 13.6 %fusion.85 = bf16[48,256,256]{2,1,0:T(8,128)(2,1)} fusion(bf16[48,256,512]{2,1,0:T(8,128)(2,1)} %add_convert_fusion), kind=kOutput, calls=%fused_computation.95 | convolution fusion | flops 3221225472 | bytes 18874368 | tf_op jit(solution)/shard_map/mdf,mef->mde/dot_general | solution.py:13
  662.7 24.9 %multiply_convert_fusion = bf16[48,256,512]{2,1,0:T(8,128)(2,1)} fusion(bf16[48,256,512]{2,1,0:T(8,128)(2,1)} %add_convert_fusion, bf16[48,256,256]{2,1,0:T(8,128)(2,1)} %fusion.85), kind=kOutput, calls=%fused_computation.1 | convolution fusion | flops 4879024128 | bytes 31457280 | tf_op jit(solution)/shard_map/mde,mef->mdf/dot_general | solution.py:18
  687.5 9.1 %slice_bitcast_fusion = (bf16[16,256,512]{2,1,0:T(8,128)(2,1)}, bf16[16,256,512]{2,1,0:T(8,128)(2,1)}, bf16[16,256,512]{2,1,0:T(8,128)(2,1)}) fusion(bf16[16,3,256,512]{3,2,1,0:T(8,128)(2,1)} %bitcast.83), kind=kLoop, calls=%fused_computation.34 | loop fusion | bytes 25165824 | tf_op jit(solution)/shard_map/squeeze | solution.py:63
  (21 shorter events, 18.2 us)
Async XLA Ops:
  7.2 467.2 %all-reduce.2.cloned.1.call-start = ((), (), s32[]{:S(2)}) async-start(), calls=%async_computation | async-start | bytes 50331648 | tf_op jit(solution)/shard_map/psum | solution.py:58
  11.5 4.2 copy-start.2
  11.5 4.7 copy-start.5
  16.2 24.2 %copy-start.3 = (f32[16,256,512]{2,1,0:T(8,128)}, f32[16,256,512]{2,1,0:T(8,128)S(1)}, u32[]{:S(2)}) copy-start(f32[16,256,512]{2,1,0:T(8,128)S(1)} %fusion.41) | copy-start | bytes 25165828
  16.2 5.3 copy-start.1
  16.2 9.3 %copy-start.4 = (bf16[16,512,256]{2,1,0:T(8,128)(2,1)S(1)}, bf16[16,512,256]{2,1,0:T(8,128)(2,1)}, u32[]{:S(2)}) copy-start(bf16[16,512,256]{2,1,0:T(8,128)(2,1)} %param.13) | copy-start | bytes 12582916
  16.2 9.3 %copy-start.7 = (f32[16,256]{1,0:T(8,128)S(1)}, f32[16,256]{1,0:T(8,128)}, u32[]{:S(2)}) copy-start(f32[16,256]{1,0:T(8,128)} %param.10) | copy-start | bytes 49156
  81.4 1.6 copy-start.6
  474.4 15.4 %copy-start = (f32[16,3,256,512]{3,2,0,1:T(8,128)S(1)}, f32[16,3,256,512]{3,2,0,1:T(8,128)}, u32[]{:S(2)}) copy-start(f32[16,3,256,512]{3,2,0,1:T(8,128)} %all-reduce.2.cloned.1.call-done) | copy-start | bytes 75497472
Sparse Core Ops, SparseCore 0:
  81.6 392.7 all-reduce.1
where the time goes:
time: 712 us; the launch traced here: 704 us
  waiting for transfers between devices  369 us (52%)
  matrix products  254 us (36%)
  local copies, waits for them, and re-layouts  34.1 us (5%)
  other arithmetic  32.3 us (5%)
  between operations  14.5 us (2%)
    psum x1, waiting for transfers between devices, per_device(): total = lax.psum(stacked, 'seq')  369 us
    dot_general x5, matrix products, newton_batch(): jnp.einsum('mde,mef->mdf', bmat, xmat, preferred_element_type=jnp.float32)  120 us
    dot_general x5, matrix products, newton_batch(): jnp.einsum('mdf,mef->mde', xmat, xmat, preferred_element_type=jnp.float32)  67.8 us
    another operation x1, other arithmetic, per_device(): stacked = jnp.stack([ggate, gup, gdown], axis=1)  18 us
    unnamed x17, local copies, waits for them, and re-layouts  15 us
  transfers between devices with their start and end apart: 1, of which 1 were waited for; matrix products, arithmetic and copies ran while one was open for 3% of the time, Pallas kernels for 0%

commit v1 on v0

v1 whole, which is shorter than its diff:
```python
import functools
import math

import jax
import jax.numpy as jnp
from jax import lax
from jax.experimental import pallas as pl
from jax.experimental.pallas import tpu as pltpu
from jax.sharding import PartitionSpec as P

NS_STEPS = 5
BF = jnp.bfloat16
F32 = jnp.float32
VMEM_BYTES = 48 * 1024 * 1024
ANY = pl.BlockSpec(memory_space=pl.ANY)
SMEM = pl.BlockSpec(memory_space=pltpu.SMEM)

NZ = 4
PLANE = 8
DEVICES = NZ * PLANE


def newton_batch(xmat, width):
    for step in range(NS_STEPS):
        amat = jnp.einsum("mdf,mef->mde", xmat, xmat, preferred_element_type=F32).astype(BF)
        square = jnp.einsum("mde,mef->mdf", amat, amat, preferred_element_type=F32)
        bmat = (-4.775 * amat.astype(F32) + 2.0315 * square).astype(BF)
        nxt = 3.4445 * xmat.astype(F32) + jnp.einsum(
            "mde,mef->mdf", bmat, xmat, preferred_element_type=F32
        )
        if step == NS_STEPS - 1:
            nxt = nxt * (0.2 * math.sqrt(width))
        xmat = nxt.astype(BF)
    return xmat


def per_device_plain(queries, keys, values, token_rates, w_gate, w_up, w_down):
    head_count, head_size, hidden = w_gate.shape
    tokens = queries.shape[0]
    scale_one = head_size ** (-0.5)
    scale_two = hidden ** (-0.5)
    qpart = queries.reshape(tokens, head_count, head_size)
    kpart = keys.reshape(tokens, head_count, head_size)
    vpart = values.reshape(tokens, head_count, head_size)
    gq = scale_one * jnp.einsum("thd,hdf->htf", qpart, w_gate, preferred_element_type=F32)
    uq = scale_one * jnp.einsum("thd,hdf->htf", qpart, w_up, preferred_element_type=F32)
    hq = (jax.nn.silu(gq) * uq).astype(BF)
    applied = (
        scale_two * jnp.einsum("htf,hfd->thd", hq, w_down, preferred_element_type=F32)
    ).astype(BF)
    applied = applied.reshape(tokens, head_count * head_size)
    gk = scale_one * jnp.einsum("thd,hdf->htf", kpart, w_gate, preferred_element_type=F32)
    uk = scale_one * jnp.einsum("thd,hdf->htf", kpart, w_up, preferred_element_type=F32)
    hk = (jax.nn.silu(gk) * uk).astype(BF)
    vrate = (jnp.transpose(token_rates)[:, :, None] * vpart.astype(F32)).astype(BF)
    gdown = -scale_two * jnp.einsum("thd,htf->hdf", vrate, hk, preferred_element_type=F32)
    dhid = -scale_two * jnp.einsum("thd,hfd->htf", vrate, w_down, preferred_element_type=F32)
    sig = jax.nn.sigmoid(gk)
    dgate = (dhid * uk * sig * (1.0 + gk * (1.0 - sig))).astype(BF)
    dup = (dhid * jax.nn.silu(gk)).astype(BF)
    ggate = scale_one * jnp.einsum("thd,htf->hdf", kpart, dgate, preferred_element_type=F32)
    gup = scale_one * jnp.einsum("thd,htf->hdf", kpart, dup, preferred_element_type=F32)
    total = lax.psum(jnp.stack([ggate, gup, gdown], axis=1), "seq")
    norms = jnp.sqrt(jnp.sum(total * total, axis=(2, 3)))
    xmat = (total / (norms[:, :, None, None] + 1e-07)).astype(BF)
    result = newton_batch(xmat.reshape(head_count * 3, head_size, hidden), hidden)
    result = result.reshape(head_count, 3, head_size, hidden)
    return (applied, result[:, 0], result[:, 1], result[:, 2])


def sigmoid(x):
    return 0.5 * jnp.tanh(0.5 * x) + 0.5


def dot(a, b, dims=((1,), (0,))):
    return lax.dot_general(a, b, (dims, ((), ())), preferred_element_type=F32)


def applied_kernel(scale_one, scale_two, q_ref, wg_ref, wu_ref, wd_ref, out_ref):
    q = q_ref[...]
    gq = scale_one * dot(q, wg_ref[0])
    hq = (gq * sigmoid(gq) * (scale_one * dot(q, wu_ref[0]))).astype(BF)
    out_ref[...] = (scale_two * dot(hq, wd_ref[0])).astype(BF)


def apply_queries(queries, w_gate, w_up, w_down):
    heads, size, hidden = w_gate.shape
    tokens = queries.shape[0]
    return pl.pallas_call(
        functools.partial(applied_kernel, size**-0.5, hidden**-0.5),
        grid=(heads,),
        out_shape=jax.ShapeDtypeStruct(queries.shape, BF),
        in_specs=[
            pl.BlockSpec((tokens, size), lambda h: (0, h)),
            pl.BlockSpec((1, size, hidden), lambda h: (h, 0, 0)),
            pl.BlockSpec((1, size, hidden), lambda h: (h, 0, 0)),
            pl.BlockSpec((1, hidden, size), lambda h: (h, 0, 0)),
        ],
        out_specs=pl.BlockSpec((tokens, size), lambda h: (0, h)),
        compiler_params=pltpu.CompilerParams(vmem_limit_bytes=VMEM_BYTES),
        cost_estimate=pl.CostEstimate(
            flops=6 * heads * tokens * size * hidden,
            bytes_accessed=4 * queries.size + 6 * w_gate.size,
            transcendentals=heads * tokens * hidden,
        ),
        name="apply_queries",
    )(queries, w_gate, w_up, w_down)


def pack_kernel(size, where_ref, k_ref, v_ref, rate_ref, *rest):
    outs, packed, sem = rest[:PLANE], rest[PLANE], rest[PLANE + 1]
    rates = jnp.transpose(rate_ref[...])
    for head in range(PLANE):
        cols = slice(head * size, (head + 1) * size)
        packed[head, 0] = k_ref[:, cols]
        packed[head, 1] = (rates[:, head : head + 1] * v_ref[:, cols].astype(F32)).astype(BF)
    mine = where_ref[0]
    copies = [
        pltpu.make_async_copy(packed.at[mine ^ d], outs[d], sem.at[d]) for d in range(PLANE)
    ]
    for copy in copies:
        copy.start()
    for copy in copies:
        copy.wait()


def pack_tokens(where, keys, values, rates, group, size):
    tokens = keys.shape[0]
    cols = PLANE * size
    return pl.pallas_call(
        functools.partial(pack_kernel, size),
        grid=(1,),
        out_shape=[jax.ShapeDtypeStruct((2, tokens, size), BF)] * PLANE,
        in_specs=[
            SMEM,
            pl.BlockSpec((tokens, cols), lambda i: (0, group)),
            pl.BlockSpec((tokens, cols), lambda i: (0, group)),
            pl.BlockSpec((PLANE, tokens), lambda i: (group, 0)),
        ],
        out_specs=[ANY] * PLANE,
        scratch_shapes=[
            pltpu.VMEM((PLANE, 2, tokens, size), BF),
            pltpu.SemaphoreType.DMA((PLANE,)),
        ],
        compiler_params=pltpu.CompilerParams(vmem_limit_bytes=VMEM_BYTES),
        cost_estimate=pl.CostEstimate(
            flops=tokens * cols, bytes_accessed=8 * tokens * cols, transcendentals=0
        ),
        name="pack_tokens",
    )(where, keys, values, rates)


def grads_kernel(scale_one, scale_two, where_ref, wg_ref, wu_ref, wd_ref, *rest):
    blocks, rest = rest[:PLANE], rest[PLANE:]
    outs, (held, total, final, sem) = rest[:NZ], rest[NZ:]
    copies = [
        pltpu.make_async_copy(blocks[b], held.at[b], sem.at[b]) for b in range(PLANE)
    ]
    for copy in copies:
        copy.start()
    wg, wu = wg_ref[0], wu_ref[0]
    wdt = jnp.transpose(wd_ref[0])
    for copy in copies:
        copy.wait()

    def step(b, carry):
        k, vr = held[b, 0], held[b, 1]
        gk = scale_one * dot(k, wg)
        uk = dot(k, wu)
        dh = dot(vr, wdt)
        sig = sigmoid(gk)
        act = gk * sig
        hk = (act * uk).astype(BF)
        dg = (dh * uk * (sig + act * (1.0 - sig))).astype(BF)
        du = (dh * act).astype(BF)
        kt, vt = jnp.transpose(k), jnp.transpose(vr)
        parts = (dot(kt, dg), dot(kt, du), dot(vt, hk))

        @pl.when(b == 0)
        def _():
            for i in range(3):
                total[i] = parts[i]

        @pl.when(b > 0)
        def _():
            for i in range(3):
                total[i] += parts[i]

        return carry

    lax.fori_loop(0, PLANE, step, 0)
    both = -scale_one * scale_two
    down = (both * total[2]).astype(BF)
    final[0] = (both * scale_one * total[0]).astype(BF)
    final[1] = down
    final[2] = (both * total[1]).astype(BF)
    final[3] = down
    own_z = where_ref[1]
    copies = [pltpu.make_async_copy(final.at[own_z ^ r], outs[r], sem.at[r]) for r in range(NZ)]
    for copy in copies:
        copy.start()
    for copy in copies:
        copy.wait()


def head_grads(where, blocks, w_gate, w_up, w_down, group):
    _, size, hidden = w_gate.shape
    tokens = blocks[0].shape[1]
    rows = tokens * PLANE
    pick = lambda i, where: (group * PLANE + where[0], 0, 0)
    return pl.pallas_call(
        functools.partial(grads_kernel, size**-0.5, hidden**-0.5),
        out_shape=[jax.ShapeDtypeStruct((size, hidden), BF)] * NZ,
        grid_spec=pltpu.PrefetchScalarGridSpec(
            num_scalar_prefetch=1,
            grid=(1,),
            in_specs=[
                pl.BlockSpec((1, size, hidden), pick),
                pl.BlockSpec((1, size, hidden), pick),
                pl.BlockSpec((1, hidden, size), pick),
            ]
            + [ANY] * PLANE,
            out_specs=[ANY] * NZ,
            scratch_shapes=[
                pltpu.VMEM((PLANE, 2, tokens, size), BF),
                pltpu.VMEM((3, size, hidden), F32),
                pltpu.VMEM((NZ, size, hidden), BF),
                pltpu.SemaphoreType.DMA((PLANE,)),
            ],
        ),
        compiler_params=pltpu.CompilerParams(vmem_limit_bytes=VMEM_BYTES),
        cost_estimate=pl.CostEstimate(
            flops=12 * rows * size * hidden,
            bytes_accessed=4 * rows * size + 14 * size * hidden,
            transcendentals=rows * hidden,
        ),
        name="head_grads",
    )(where, w_gate, w_up, w_down, *blocks)


def newton_kernel(a_ref, b_ref, c_ref, d_ref, out_ref):
    width = out_ref.shape[1]
    grad = (a_ref[...].astype(F32) + b_ref[...].astype(F32)) + (
        c_ref[...].astype(F32) + d_ref[...].astype(F32)
    )
    norm = jnp.sqrt(jnp.sum(grad * grad))
    x = (grad / (norm + 1e-07)).astype(BF)
    for step in range(NS_STEPS):
        a = dot(x, x, ((1,), (1,))).astype(BF)
        b = (-4.775 * a.astype(F32) + 2.0315 * dot(a, a)).astype(BF)
        nxt = 3.4445 * x.astype(F32) + dot(b, x)
        if step == NS_STEPS - 1:
            nxt = nxt * (0.2 * math.sqrt(width))
        x = nxt.astype(BF)
    out_ref[...] = x


def newton(parts):
    size, hidden = parts[0].shape
    return pl.pallas_call(
        newton_kernel,
        out_shape=jax.ShapeDtypeStruct((size, hidden), BF),
        compiler_params=pltpu.CompilerParams(vmem_limit_bytes=VMEM_BYTES),
        cost_estimate=pl.CostEstimate(
            flops=NS_STEPS * (4 * size * size * hidden + 2 * size**3),
            bytes_accessed=10 * size * hidden,
            transcendentals=0,
        ),
        name="newton_schulz",
    )(*parts)


def place_kernel(first, group, slot, size, where_ref, *rest):
    own, sibling = rest[:4], rest[4:8]
    gate, up, down, sem = rest[-4:]
    z, y, x, core = (where_ref[i] for i in range(1, 5))
    source_z = z ^ slot
    cut = 3 * size // 4
    tail = size - cut
    half = size // 2

    def put(m0, blocks_zero, blocks_one):
        zero_at = ((y, x), (y ^ 1, x), (y, x ^ 1), (y ^ 1, x ^ 1))
        one_at = ((y, x), (y, x ^ 1), (y ^ 1, x), (y ^ 1, x ^ 1))
        copies = []
        for at, block in zip(zero_at, blocks_zero):
            head = group * PLANE + at[0] * 4 + at[1] * 2 + source_z // 2
            copies.append((block, m0.at[head, pl.ds(0, cut)]))
        for at, block in zip(one_at, blocks_one):
            head = group * PLANE + at[0] * 4 + at[1] * 2 + source_z // 2
            rows = pl.ds(pl.multiple_of(lax.rem(source_z, 2) * half, half), half)
            copies.append((block.at[pl.ds(0, tail)], m0.at[head, pl.ds(cut, tail)]))
            copies.append((block.at[pl.ds(tail, half)], down.at[head, rows]))
        copies = [pltpu.make_async_copy(a, b, sem.at[i]) for i, (a, b) in enumerate(copies)]
        for copy in copies:
            copy.start()
        for copy in copies:
            copy.wait()

    for parity, m0 in ((0, gate), (1, up)):
        for side in range(2):

            @pl.when((lax.rem(source_z, 2) == parity) & (core == side))
            def _():
                pair = (own, sibling) if side == 0 else (sibling, own)
                put(m0, *pair)


def place(where, own, sibling, steps, shape, group, slot):
    size = shape[1]
    first = steps is None
    arrays = () if first else steps
    return pl.pallas_call(
        functools.partial(place_kernel, first, group, slot, size),
        out_shape=[jax.ShapeDtypeStruct(shape, BF)] * 3,
        in_specs=[SMEM] + [ANY] * (8 + len(arrays)),
        out_specs=[ANY] * 3,
        scratch_shapes=[pltpu.SemaphoreType.DMA((12,))],
        input_output_aliases={} if first else {9 + i: i for i in range(3)},
        compiler_params=pltpu.CompilerParams(vmem_limit_bytes=VMEM_BYTES),
        cost_estimate=pl.CostEstimate(
            flops=0, bytes_accessed=4 * 8 * own[0].size, transcendentals=0
        ),
        name="place_steps",
    )(where, *own, *sibling, *arrays)


def permutation(target):
    pairs = []
    for i in range(DEVICES):
        z, y, x, core = target(i // 8, i // 4 % 2, i // 2 % 2, i % 2)
        pairs.append((i, ((z * 2 + y) * 2 + x) * 2 + core))
    return pairs


PLANE_MOVES = [
    permutation(lambda z, y, x, c, d=d: (z, y ^ (d >> 2), x ^ (d >> 1 & 1), c ^ (d & 1)))
    for d in range(PLANE)
]
REDUCE_MOVES = [
    permutation(lambda z, y, x, c, r=r: (2 * c + ((z ^ r) >> 1), y, x, (z ^ r) & 1))
    for r in range(NZ)
]
Z_MOVES = [permutation(lambda z, y, x, c, s=s: (z ^ s, y, x, c)) for s in range(NZ)]
FIRST_MOVE = permutation(lambda z, y, x, c: (z, y ^ (1 - c), x ^ c, c))
SECOND_MOVE = permutation(lambda z, y, x, c: (z, y ^ c, x ^ (1 - c), c))
CORE_MOVE = PLANE_MOVES[1]


def move(array, pairs):
    return lax.ppermute(array, "seq", pairs)


def after(array, *others):
    return lax.optimization_barrier((array, *others))[0]


def per_device_fast(queries, keys, values, token_rates, w_gate, w_up, w_down):
    heads, size, hidden = w_gate.shape
    groups = heads // PLANE
    index = lax.axis_index("seq")
    z, core = index // 8, index % 2
    where = jnp.stack([index % 8, z, index // 4 % 2, index // 2 % 2, core]).astype(jnp.int32)

    applied = apply_queries(queries, w_gate, w_up, w_down)

    received = []
    for group in range(groups):
        blocks = pack_tokens(where, keys, values, token_rates, group, size)
        if group:
            blocks = lax.optimization_barrier((*blocks, received[-1][1]))[:PLANE]
        received.append([blocks[0]] + [move(blocks[d], PLANE_MOVES[d]) for d in range(1, PLANE)])

    steps = None
    cut = 3 * size // 4
    for group in range(groups):
        parts = head_grads(where, received[group], w_gate, w_up, w_down, group)
        parts = [move(parts[r], REDUCE_MOVES[r]) for r in range(NZ)]
        xmat = newton(parts)
        tail = move(xmat[cut:], CORE_MOVE)
        part = lax.dynamic_slice_in_dim(xmat, z % 2 * (size // 2), size // 2, 0)
        payload = jnp.where(core == 0, xmat[:cut], jnp.concatenate([tail, part], 0))
        slots = [payload]
        for s in range(1, NZ):
            slots.append(move(after(payload, slots[-1]), Z_MOVES[s]))
        for s in range(NZ):
            one = move(slots[s], FIRST_MOVE)
            two = move(slots[s], SECOND_MOVE)
            three = move(one, SECOND_MOVE)
            own = [slots[s], one, two, three]
            sibling = [move(b, CORE_MOVE) for b in own]
            steps = place(where, own, sibling, steps, w_gate.shape, group, s)
    return (applied, *steps)


def solution(mesh):
    in_specs = (
        P("seq", "head"),
        P("seq", "head"),
        P("seq", "head"),
        P("head", "seq"),
        P("head", None, None),
        P("head", None, None),
        P("head", None, None),
    )
    out_specs = (
        P("seq", "head"),
        P("head", None, None),
        P("head", None, None),
        P("head", None, None),
    )
    sizes = mesh.shape

    def per_device(*args):
        heads = args[4].shape[0]
        fast = sizes["seq"] == DEVICES and heads % PLANE == 0
        return (per_device_fast if fast else per_device_plain)(*args)

    return jax.shard_map(
        per_device, mesh=mesh, in_specs=in_specs, out_specs=out_specs, check_vma=False
    )
```

time: 712 us -> 251 us (0.35); the launches traced: 704 us -> 250 us
  waiting for transfers between devices: 369 us -> 111 us
  matrix products: 254 us -> 0 us
  starting transfers between devices: 0.04 us -> 75.6 us
  Pallas kernels: 0 us -> 59.9 us
  other arithmetic: 32.3 us -> 0.1 us
  local copies, waits for them, and re-layouts: 34.1 us -> 2.44 us
  between operations: 14.5 us -> 1.25 us
    psum x1 -> x0, waiting for transfers between devices: 369 us -> none  [per_device(): total = lax.psum(stacked, 'seq')]
    dot_general x18 -> x0, matrix products: 254 us -> none  [the longest x5 120 us: newton_batch(): jnp.einsum('mde,mef->mdf', bmat, xmat, preferred_element_type=jnp.float32)]
    ppermute x0 -> x86, waiting for transfers between devices: none -> 111 us  [move(): return lax.ppermute(array, 'seq', pairs)]
    ppermute x0 -> x86, starting transfers between devices: none -> 75.6 us  [move(): return lax.ppermute(array, 'seq', pairs)]
    pallas_call x0 -> x15, Pallas kernels: none -> 59.9 us  [the longest x2 19.5 us: head_grads(): pl.pallas_call(functools.partial(grads_kernel, size ** (-0.5), hidden **...]
    another operation x1 -> x0, other arithmetic: 18 us -> none  [per_device(): stacked = jnp.stack([ggate, gup, gdown], axis=1)]
    unnamed x17 -> x10, local copies, waits for them, and re-layouts: 15 us -> 2.32 us
    reduce_sum x1 -> x0, other arithmetic: 10.5 us -> none  [per_device(): norms = jnp.sqrt(jnp.sum(total * total, axis=(2, 3)))]
  transfers between devices with their start and end apart: 1 -> 86, of which waited for: 1 -> 23; matrix products, arithmetic and copies ran while one was open for 3% -> 0% of each run, Pallas kernels for 0% -> 18%
where the time goes in v1:
time: 251 us; the launch traced here: 250 us
  waiting for transfers between devices  111 us (44%)
  starting transfers between devices  75.6 us (30%)
  Pallas kernels  59.9 us (24%)
    ppermute x86, waiting for transfers between devices, move(): return lax.ppermute(array, 'seq', pairs)  111 us
    ppermute x86, starting transfers between devices, move(): return lax.ppermute(array, 'seq', pairs)  75.6 us
    pallas_call x2, Pallas kernels, head_grads(): pl.pallas_call(functools.partial(grads_kernel, size ** (-0.5), hidden **...  19.5 us
    pallas_call x1, Pallas kernels, apply_queries(): pl.pallas_call(functools.partial(applied_kernel, size ** (-0.5), hidden *...  14.9 us
    pallas_call x8, Pallas kernels, place(): pl.pallas_call(functools.partial(place_kernel, first, group, slot, size),...  14.6 us
    pallas_call x2, Pallas kernels, newton(): pl.pallas_call(newton_kernel, out_shape=jax.ShapeDtypeStruct((size, hidde...  6.82 us
  transfers between devices with their start and end apart: 86, of which 23 were waited for; matrix products, arithmetic and copies ran while one was open for 0% of the time, Pallas kernels for 18%

profile of v1, /device:TPU:0, one launch (start us, length us, event | category | flops | bytes accessed | tf_op | source)
XLA Modules:
  0.0 250.4 jit_solution(14147280787838552177)
XLA Ops:
  12.7 2.7 %collective-permute-done.44.rest_2_ = bf16[2,256,256]{2,1,0:T(8,128)(2,1)S(1)} collective-permute-done((bf16[2,256,256]{2,1,0:T(8,128)(2,1)S(1)}, bf16[2,256,256]{2,1,0:T(8,128)(2,1)S(1)}, u32[]{:S(2)}, u32[]{:S(2)}) %collective-permute-start.44) | collective-permute-done | bytes 262176 | tf_op jit(solution)/shard_map/ppermute | solution.py:351
  17.1 3.4 %collective-permute-done.45.rest_3_ = bf16[2,256,256]{2,1,0:T(8,128)(2,1)S(1)} collective-permute-done((bf16[2,256,256]{2,1,0:T(8,128)(2,1)S(1)}, bf16[2,256,256]{2,1,0:T(8,128)(2,1)S(1)}, u32[]{:S(2)}, u32[]{:S(2)}) %collective-permute-start.45) | collective-permute-done | bytes 262176 | tf_op jit(solution)/shard_map/ppermute | solution.py:351
  20.5 12.5 %collective-permute-done.47.rest_5_ = bf16[2,256,256]{2,1,0:T(8,128)(2,1)S(1)} collective-permute-done((bf16[2,256,256]{2,1,0:T(8,128)(2,1)S(1)}, bf16[2,256,256]{2,1,0:T(8,128)(2,1)S(1)}, u32[]{:S(2)}, u32[]{:S(2)}) %collective-permute-start.47) | collective-permute-done | bytes 262176 | tf_op jit(solution)/shard_map/ppermute | solution.py:351
  33.0 9.8 %head_grads.3 = (bf16[256,512]{1,0:T(8,128)(2,1)S(1)}, bf16[256,512]{1,0:T(8,128)(2,1)S(1)}, bf16[256,512]{1,0:T(8,128)(2,1)S(1)}, bf16[256,512]{1,0:T(8,128)(2,1)S(1)}) custom-call(s32[5]{0:T(128)S(1)} %stack.23.where_ref, bf16[16,256,512]{2,1,0:T(8,128)(2,1)} %wg_ref.5, bf16[16,256,512]{2,1,0:T(8,128)(2,1)} %wu_ref.5, bf16[16,512,256]{2,1,0:T(8,128)(2,1)} %wd_ref.5, ...), custom_call_target="tpu_custom_call" | custom-call | flops 3221225472 | bytes 3932160 | tf_op jit(solution)/shard_map/head_grads/pallas_call | solution.py:211
  43.5 4.4 %collective-permute-start.51 = (bf16[256,512]{1,0:T(8,128)(2,1)S(1)}, bf16[256,512]{1,0:T(8,128)(2,1)S(1)}, u32[]{:S(2)}, u32[]{:S(2)}) collective-permute-start(bf16[256,512]{1,0:T(8,128)(2,1)S(1)} %get-tuple-element.98), channel_id=1, source_target_pairs={{0,1},{1,17},{2,3},{3,19},{4,5},{5,21},{6,7},{7,23},{8,0},{9,16},{... | collective-permute-start | bytes 786440 | tf_op jit(solution)/shard_map/ppermute | solution.py:351
  47.9 3.5 %collective-permute-start.53 = (bf16[256,512]{1,0:T(8,128)(2,1)S(1)}, bf16[256,512]{1,0:T(8,128)(2,1)S(1)}, u32[]{:S(2)}, u32[]{:S(2)}) collective-permute-start(bf16[256,512]{1,0:T(8,128)(2,1)S(1)} %get-tuple-element.100), channel_id=1, source_target_pairs={{0,9},{1,25},{2,11},{3,27},{4,13},{5,29},{6,15},{7,31},{8,8},{9,24... | collective-permute-start | bytes 786440 | tf_op jit(solution)/shard_map/ppermute | solution.py:351
  56.0 13.4 %collective-permute-done.52.c_ref = bf16[256,512]{1,0:T(8,128)(2,1)S(1)} collective-permute-done((bf16[256,512]{1,0:T(8,128)(2,1)S(1)}, bf16[256,512]{1,0:T(8,128)(2,1)S(1)}, u32[]{:S(2)}, u32[]{:S(2)}) %collective-permute-start.52) | collective-permute-done | bytes 262176 | tf_op jit(solution)/shard_map/ppermute | solution.py:351
  69.3 3.4 %newton_schulz.3 = bf16[256,512]{1,0:T(8,128)(2,1)S(1)} custom-call(bf16[256,512]{1,0:T(8,128)(2,1)S(1)} %collective-permute-done.50.a_ref, bf16[256,512]{1,0:T(8,128)(2,1)S(1)} %collective-permute-done.51.b_ref, bf16[256,512]{1,0:T(8,128)(2,1)S(1)} %collective-permute-done.52.c_ref, bf16[256,512]{1,0:T(8,128)(2,1)S(1)} %collective-permute-done.53.d_ref), custom_call_target="tpu_custom_call" | custom-call | flops 838860800 | bytes 1310720 | tf_op jit(solution)/shard_map/newton_schulz/pallas_call | solution.py:260
  72.8 2.7 %collective-permute-start.54 = (bf16[64,512]{1,0:T(8,128)(2,1)S(1)}, bf16[64,512]{1,0:T(8,128)(2,1)S(1)}, u32[]{:S(2)}, u32[]{:S(2)}) collective-permute-start(bf16[64,512]{1,0:T(8,128)(2,1)S(1)} %slice.19), channel_id=1, source_target_pairs={{0,1},{1,0},{2,3},{3,2},{4,5},{5,4},{6,7},{7,6},{8,9},{9,8},{10,11... | collective-permute-start | bytes 196616 | tf_op jit(solution)/shard_map/ppermute | solution.py:351
  85.3 11.7 %collective-permute-done.4.rest_4_ = bf16[2,256,256]{2,1,0:T(8,128)(2,1)S(1)} collective-permute-done((bf16[2,256,256]{2,1,0:T(8,128)(2,1)S(1)}, bf16[2,256,256]{2,1,0:T(8,128)(2,1)S(1)}, u32[]{:S(2)}, u32[]{:S(2)}) %collective-permute-start.4) | collective-permute-done | bytes 262176 | tf_op jit(solution)/shard_map/ppermute | solution.py:351
  97.0 4.7 %collective-permute-done.5.rest_5_ = bf16[2,256,256]{2,1,0:T(8,128)(2,1)S(1)} collective-permute-done((bf16[2,256,256]{2,1,0:T(8,128)(2,1)S(1)}, bf16[2,256,256]{2,1,0:T(8,128)(2,1)S(1)}, u32[]{:S(2)}, u32[]{:S(2)}) %collective-permute-start.5) | collective-permute-done | bytes 262176 | tf_op jit(solution)/shard_map/ppermute | solution.py:351
  101.7 9.7 %head_grads.2 = (bf16[256,512]{1,0:T(8,128)(2,1)S(1)}, bf16[256,512]{1,0:T(8,128)(2,1)S(1)}, bf16[256,512]{1,0:T(8,128)(2,1)S(1)}, bf16[256,512]{1,0:T(8,128)(2,1)S(1)}) custom-call(s32[5]{0:T(128)S(1)} %stack.23.where_ref, bf16[16,256,512]{2,1,0:T(8,128)(2,1)} %wg_ref.5, bf16[16,256,512]{2,1,0:T(8,128)(2,1)} %wu_ref.5, bf16[16,512,256]{2,1,0:T(8,128)(2,1)} %wd_ref.5, ...), custom_call_target="tpu_custom_call" | custom-call | flops 3221225472 | bytes 3932160 | tf_op jit(solution)/shard_map/head_grads/pallas_call | solution.py:211
  111.5 4.2 %collective-permute-start.11 = (bf16[256,512]{1,0:T(8,128)(2,1)S(1)}, bf16[256,512]{1,0:T(8,128)(2,1)S(1)}, u32[]{:S(2)}, u32[]{:S(2)}) collective-permute-start(bf16[256,512]{1,0:T(8,128)(2,1)S(1)} %get-tuple-element.86), channel_id=1, source_target_pairs={{0,9},{1,25},{2,11},{3,27},{4,13},{5,29},{6,15},{7,31},{8,8},{9,24... | collective-permute-start | bytes 786440 | tf_op jit(solution)/shard_map/ppermute | solution.py:351
  116.4 3.6 %collective-permute-start.9 = (bf16[256,512]{1,0:T(8,128)(2,1)S(1)}, bf16[256,512]{1,0:T(8,128)(2,1)S(1)}, u32[]{:S(2)}, u32[]{:S(2)}) collective-permute-start(bf16[256,512]{1,0:T(8,128)(2,1)S(1)} %get-tuple-element.84), channel_id=1, source_target_pairs={{0,1},{1,17},{2,3},{3,19},{4,5},{5,21},{6,7},{7,23},{8,0},{9,16},{... | collective-permute-start | bytes 786440 | tf_op jit(solution)/shard_map/ppermute | solution.py:351
  120.1 16.9 %collective-permute-done.55.rest_0_ = bf16[192,512]{1,0:T(8,128)(2,1)S(1)} collective-permute-done((bf16[192,512]{1,0:T(8,128)(2,1)S(1)}, bf16[192,512]{1,0:T(8,128)(2,1)S(1)}, u32[]{:S(2)}, u32[]{:S(2)}) %collective-permute-start.55) | collective-permute-done | bytes 196640 | tf_op jit(solution)/shard_map/ppermute | solution.py:351
  139.1 3.4 %newton_schulz.2 = bf16[256,512]{1,0:T(8,128)(2,1)S(1)} custom-call(bf16[256,512]{1,0:T(8,128)(2,1)S(1)} %collective-permute-done.8.a_ref, bf16[256,512]{1,0:T(8,128)(2,1)S(1)} %collective-permute-done.9.b_ref, bf16[256,512]{1,0:T(8,128)(2,1)S(1)} %collective-permute-done.10.c_ref, bf16[256,512]{1,0:T(8,128)(2,1)S(1)} %collective-permute-done.11.d_ref), custom_call_target="tpu_custom_call" | custom-call | flops 838860800 | bytes 1310720 | tf_op jit(solution)/shard_map/newton_schulz/pallas_call | solution.py:260
  152.1 4.9 %collective-permute-done.56.rest_0_ = bf16[192,512]{1,0:T(8,128)(2,1)S(1)} collective-permute-done((bf16[192,512]{1,0:T(8,128)(2,1)S(1)}, bf16[192,512]{1,0:T(8,128)(2,1)S(1)}, u32[]{:S(2)}, u32[]{:S(2)}) %collective-permute-start.56) | collective-permute-done | bytes 196640 | tf_op jit(solution)/shard_map/ppermute | solution.py:351
  178.5 7.5 %collective-permute-done.14.rest_0_ = bf16[192,512]{1,0:T(8,128)(2,1)S(1)} collective-permute-done((bf16[192,512]{1,0:T(8,128)(2,1)S(1)}, bf16[192,512]{1,0:T(8,128)(2,1)S(1)}, u32[]{:S(2)}, u32[]{:S(2)}) %collective-permute-start.14) | collective-permute-done | bytes 196640 | tf_op jit(solution)/shard_map/ppermute | solution.py:351
  189.4 4.4 %collective-permute-done.58.rest_1_ = bf16[192,512]{1,0:T(8,128)(2,1)S(1)} collective-permute-done((bf16[192,512]{1,0:T(8,128)(2,1)S(1)}, bf16[192,512]{1,0:T(8,128)(2,1)S(1)}, u32[]{:S(2)}, u32[]{:S(2)}) %collective-permute-start.58) | collective-permute-done | bytes 196640 | tf_op jit(solution)/shard_map/ppermute | solution.py:351
  198.4 3.2 %collective-permute-done.23.rest_1_ = bf16[192,512]{1,0:T(8,128)(2,1)S(1)} collective-permute-done((bf16[192,512]{1,0:T(8,128)(2,1)S(1)}, bf16[192,512]{1,0:T(8,128)(2,1)S(1)}, u32[]{:S(2)}, u32[]{:S(2)}) %collective-permute-start.23) | collective-permute-done | bytes 196640 | tf_op jit(solution)/shard_map/ppermute | solution.py:351
  203.2 2.7 %collective-permute-done.15.rest_0_ = bf16[192,512]{1,0:T(8,128)(2,1)S(1)} collective-permute-done((bf16[192,512]{1,0:T(8,128)(2,1)S(1)}, bf16[192,512]{1,0:T(8,128)(2,1)S(1)}, u32[]{:S(2)}, u32[]{:S(2)}) %collective-permute-start.15) | collective-permute-done | bytes 196640 | tf_op jit(solution)/shard_map/ppermute | solution.py:351
  209.9 3.4 %collective-permute-done.25.rest_3_ = bf16[192,512]{1,0:T(8,128)(2,1)S(1)} collective-permute-done((bf16[192,512]{1,0:T(8,128)(2,1)S(1)}, bf16[192,512]{1,0:T(8,128)(2,1)S(1)}, u32[]{:S(2)}, u32[]{:S(2)}) %collective-permute-start.25) | collective-permute-done | bytes 196640 | tf_op jit(solution)/shard_map/ppermute | solution.py:351
  216.4 4.2 %collective-permute-done.18.rest_3_ = bf16[192,512]{1,0:T(8,128)(2,1)S(1)} collective-permute-done((bf16[192,512]{1,0:T(8,128)(2,1)S(1)}, bf16[192,512]{1,0:T(8,128)(2,1)S(1)}, u32[]{:S(2)}, u32[]{:S(2)}) %collective-permute-start.18) | collective-permute-done | bytes 196640 | tf_op jit(solution)/shard_map/ppermute | solution.py:351
  220.6 14.9 %apply_queries.1 = bf16[256,4096]{1,0:T(8,128)(2,1)} custom-call(bf16[256,4096]{1,0:T(8,128)(2,1)S(1)} %copy-done.2, bf16[16,256,512]{2,1,0:T(8,128)(2,1)} %wg_ref.5, bf16[16,256,512]{2,1,0:T(8,128)(2,1)} %wu_ref.5, bf16[16,512,256]{2,1,0:T(8,128)(2,1)} %wd_ref.5), custom_call_target="tpu_custom_call" | custom-call | flops 3221225472 | bytes 16777216 | tf_op jit(solution)/shard_map/apply_queries/pallas_call | solution.py:89
  (180 shorter events, 93.9 us)
Async XLA Ops:
  10.1 22.9 %collective-permute-start.47 = (bf16[2,256,256]{2,1,0:T(8,128)(2,1)S(1)}, bf16[2,256,256]{2,1,0:T(8,128)(2,1)S(1)}, u32[]{:S(2)}, u32[]{:S(2)}) collective-permute-start(bf16[2,256,256]{2,1,0:T(8,128)(2,1)S(1)} %get-tuple-element.94), channel_id=1, source_target_pairs={{0,5},{1,4},{2,7},{3,6},{4,1},{5,0},{6,3},{7,2},{8,13},{9,12},{10,... | collective-permute-start | bytes 786440 | tf_op jit(solution)/shard_map/ppermute | solution.py:351
  10.1 22.9 %collective-permute-start.48 = (bf16[2,256,256]{2,1,0:T(8,128)(2,1)S(1)}, bf16[2,256,256]{2,1,0:T(8,128)(2,1)S(1)}, u32[]{:S(2)}, u32[]{:S(2)}) collective-permute-start(bf16[2,256,256]{2,1,0:T(8,128)(2,1)S(1)} %get-tuple-element.95), channel_id=1, source_target_pairs={{0,6},{1,7},{2,4},{3,5},{4,2},{5,3},{6,0},{7,1},{8,14},{9,15},{10,... | collective-permute-start | bytes 786440 | tf_op jit(solution)/shard_map/ppermute | solution.py:351
  15.4 17.6 %collective-permute-start.49 = (bf16[2,256,256]{2,1,0:T(8,128)(2,1)S(1)}, bf16[2,256,256]{2,1,0:T(8,128)(2,1)S(1)}, u32[]{:S(2)}, u32[]{:S(2)}) collective-permute-start(bf16[2,256,256]{2,1,0:T(8,128)(2,1)S(1)} %get-tuple-element.96), channel_id=1, source_target_pairs={{0,7},{1,6},{2,5},{3,4},{4,3},{5,2},{6,1},{7,0},{8,15},{9,14},{10,... | collective-permute-start | bytes 786440 | tf_op jit(solution)/shard_map/ppermute | solution.py:351
  43.5 12.5 %collective-permute-start.51 = (bf16[256,512]{1,0:T(8,128)(2,1)S(1)}, bf16[256,512]{1,0:T(8,128)(2,1)S(1)}, u32[]{:S(2)}, u32[]{:S(2)}) collective-permute-start(bf16[256,512]{1,0:T(8,128)(2,1)S(1)} %get-tuple-element.98), channel_id=1, source_target_pairs={{0,1},{1,17},{2,3},{3,19},{4,5},{5,21},{6,7},{7,23},{8,0},{9,16},{... | collective-permute-start | bytes 786440 | tf_op jit(solution)/shard_map/ppermute | solution.py:351
  47.9 21.5 %collective-permute-start.52 = (bf16[256,512]{1,0:T(8,128)(2,1)S(1)}, bf16[256,512]{1,0:T(8,128)(2,1)S(1)}, u32[]{:S(2)}, u32[]{:S(2)}) collective-permute-start(bf16[256,512]{1,0:T(8,128)(2,1)S(1)} %get-tuple-element.99), channel_id=1, source_target_pairs={{0,8},{1,24},{2,10},{3,26},{4,12},{5,28},{6,14},{7,30},{8,9},{9,25... | collective-permute-start | bytes 786440 | tf_op jit(solution)/shard_map/ppermute | solution.py:351
  47.9 21.5 %collective-permute-start.53 = (bf16[256,512]{1,0:T(8,128)(2,1)S(1)}, bf16[256,512]{1,0:T(8,128)(2,1)S(1)}, u32[]{:S(2)}, u32[]{:S(2)}) collective-permute-start(bf16[256,512]{1,0:T(8,128)(2,1)S(1)} %get-tuple-element.100), channel_id=1, source_target_pairs={{0,9},{1,25},{2,11},{3,27},{4,13},{5,29},{6,15},{7,31},{8,8},{9,24... | collective-permute-start | bytes 786440 | tf_op jit(solution)/shard_map/ppermute | solution.py:351
  53.5 24.7 %collective-permute-start.1 = (bf16[2,256,256]{2,1,0:T(8,128)(2,1)S(1)}, bf16[2,256,256]{2,1,0:T(8,128)(2,1)S(1)}, u32[]{:S(2)}, u32[]{:S(2)}) collective-permute-start(bf16[2,256,256]{2,1,0:T(8,128)(2,1)S(1)} %get-tuple-element.76), channel_id=1, source_target_pairs={{0,1},{1,0},{2,3},{3,2},{4,5},{5,4},{6,7},{7,6},{8,9},{9,8},{10,11... | collective-permute-start | bytes 786440 | tf_op jit(solution)/shard_map/ppermute | solution.py:351
  54.5 24.0 %collective-permute-start.2 = (bf16[2,256,256]{2,1,0:T(8,128)(2,1)S(1)}, bf16[2,256,256]{2,1,0:T(8,128)(2,1)S(1)}, u32[]{:S(2)}, u32[]{:S(2)}) collective-permute-start(bf16[2,256,256]{2,1,0:T(8,128)(2,1)S(1)} %get-tuple-element.77), channel_id=1, source_target_pairs={{0,2},{1,3},{2,0},{3,1},{4,6},{5,7},{6,4},{7,5},{8,10},{9,11},{10,... | collective-permute-start | bytes 786440 | tf_op jit(solution)/shard_map/ppermute | solution.py:351
  76.7 20.3 %collective-permute-start.4 = (bf16[2,256,256]{2,1,0:T(8,128)(2,1)S(1)}, bf16[2,256,256]{2,1,0:T(8,128)(2,1)S(1)}, u32[]{:S(2)}, u32[]{:S(2)}) collective-permute-start(bf16[2,256,256]{2,1,0:T(8,128)(2,1)S(1)} %get-tuple-element.79), channel_id=1, source_target_pairs={{0,4},{1,5},{2,6},{3,7},{4,0},{5,1},{6,2},{7,3},{8,12},{9,13},{10,... | collective-permute-start | bytes 786440 | tf_op jit(solution)/shard_map/ppermute | solution.py:351
  78.2 23.5 %collective-permute-start.5 = (bf16[2,256,256]{2,1,0:T(8,128)(2,1)S(1)}, bf16[2,256,256]{2,1,0:T(8,128)(2,1)S(1)}, u32[]{:S(2)}, u32[]{:S(2)}) collective-permute-start(bf16[2,256,256]{2,1,0:T(8,128)(2,1)S(1)} %get-tuple-element.80), channel_id=1, source_target_pairs={{0,5},{1,4},{2,7},{3,6},{4,1},{5,0},{6,3},{7,2},{8,13},{9,12},{10,... | collective-permute-start | bytes 786440 | tf_op jit(solution)/shard_map/ppermute | solution.py:351
  78.5 23.2 %collective-permute-start.6 = (bf16[2,256,256]{2,1,0:T(8,128)(2,1)S(1)}, bf16[2,256,256]{2,1,0:T(8,128)(2,1)S(1)}, u32[]{:S(2)}, u32[]{:S(2)}) collective-permute-start(bf16[2,256,256]{2,1,0:T(8,128)(2,1)S(1)} %get-tuple-element.81), channel_id=1, source_target_pairs={{0,6},{1,7},{2,4},{3,5},{4,2},{5,3},{6,0},{7,1},{8,14},{9,15},{10,... | collective-permute-start | bytes 786440 | tf_op jit(solution)/shard_map/ppermute | solution.py:351
  80.0 21.7 %collective-permute-start.7 = (bf16[2,256,256]{2,1,0:T(8,128)(2,1)S(1)}, bf16[2,256,256]{2,1,0:T(8,128)(2,1)S(1)}, u32[]{:S(2)}, u32[]{:S(2)}) collective-permute-start(bf16[2,256,256]{2,1,0:T(8,128)(2,1)S(1)} %get-tuple-element.82), channel_id=1, source_target_pairs={{0,7},{1,6},{2,5},{3,4},{4,3},{5,2},{6,1},{7,0},{8,15},{9,14},{10,... | collective-permute-start | bytes 786440 | tf_op jit(solution)/shard_map/ppermute | solution.py:351
  83.8 36.3 %collective-permute-start.79 = (bf16[192,512]{1,0:T(8,128)(2,1)S(1)}, bf16[192,512]{1,0:T(8,128)(2,1)S(1)}, u32[]{:S(2)}, u32[]{:S(2)}) collective-permute-start(bf16[192,512]{1,0:T(8,128)(2,1)S(1)} %slice_select_fusion.rest_0_), channel_id=1, source_target_pairs={{0,4},{1,3},{2,6},{3,1},{4,0},{5,7},{6,2},{7,5},{8,12},{9,11},{10,... | collective-permute-start | bytes 589832 | tf_op jit(solution)/shard_map/ppermute | solution.py:351
  111.4 26.1 %collective-permute-start.10 = (bf16[256,512]{1,0:T(8,128)(2,1)S(1)}, bf16[256,512]{1,0:T(8,128)(2,1)S(1)}, u32[]{:S(2)}, u32[]{:S(2)}) collective-permute-start(bf16[256,512]{1,0:T(8,128)(2,1)S(1)} %get-tuple-element.85), channel_id=1, source_target_pairs={{0,8},{1,24},{2,10},{3,26},{4,12},{5,28},{6,14},{7,30},{8,9},{9,25... | collective-permute-start | bytes 786440 | tf_op jit(solution)/shard_map/ppermute | solution.py:351
  111.5 26.1 %collective-permute-start.11 = (bf16[256,512]{1,0:T(8,128)(2,1)S(1)}, bf16[256,512]{1,0:T(8,128)(2,1)S(1)}, u32[]{:S(2)}, u32[]{:S(2)}) collective-permute-start(bf16[256,512]{1,0:T(8,128)(2,1)S(1)} %get-tuple-element.86), channel_id=1, source_target_pairs={{0,9},{1,25},{2,11},{3,27},{4,13},{5,29},{6,15},{7,31},{8,8},{9,24... | collective-permute-start | bytes 786440 | tf_op jit(solution)/shard_map/ppermute | solution.py:351
  115.7 23.4 %collective-permute-start.8 = (bf16[256,512]{1,0:T(8,128)(2,1)S(1)}, bf16[256,512]{1,0:T(8,128)(2,1)S(1)}, u32[]{:S(2)}, u32[]{:S(2)}) collective-permute-start(bf16[256,512]{1,0:T(8,128)(2,1)S(1)} %get-tuple-element.83), channel_id=1, source_target_pairs={{0,0},{1,16},{2,2},{3,18},{4,4},{5,20},{6,6},{7,22},{8,1},{9,17},{... | collective-permute-start | bytes 786440 | tf_op jit(solution)/shard_map/ppermute | solution.py:351
  116.4 22.7 %collective-permute-start.9 = (bf16[256,512]{1,0:T(8,128)(2,1)S(1)}, bf16[256,512]{1,0:T(8,128)(2,1)S(1)}, u32[]{:S(2)}, u32[]{:S(2)}) collective-permute-start(bf16[256,512]{1,0:T(8,128)(2,1)S(1)} %get-tuple-element.84), channel_id=1, source_target_pairs={{0,1},{1,17},{2,3},{3,19},{4,5},{5,21},{6,7},{7,23},{8,0},{9,16},{... | collective-permute-start | bytes 786440 | tf_op jit(solution)/shard_map/ppermute | solution.py:351
  120.1 16.9 %collective-permute-start.55 = (bf16[192,512]{1,0:T(8,128)(2,1)S(1)}, bf16[192,512]{1,0:T(8,128)(2,1)S(1)}, u32[]{:S(2)}, u32[]{:S(2)}) collective-permute-start(bf16[192,512]{1,0:T(8,128)(2,1)S(1)} %slice_select_fusion.rest_0_), channel_id=1, source_target_pairs={{0,8},{1,9},{2,10},{3,11},{4,12},{5,13},{6,14},{7,15},{8,0},{9,1},... | collective-permute-start | bytes 589832 | tf_op jit(solution)/shard_map/ppermute | solution.py:351
  173.6 12.4 %collective-permute-start.14 = (bf16[192,512]{1,0:T(8,128)(2,1)S(1)}, bf16[192,512]{1,0:T(8,128)(2,1)S(1)}, u32[]{:S(2)}, u32[]{:S(2)}) collective-permute-start(bf16[192,512]{1,0:T(8,128)(2,1)S(1)} %slice_select_fusion.1.rest_0_), channel_id=1, source_target_pairs={{0,16},{1,17},{2,18},{3,19},{4,20},{5,21},{6,22},{7,23},{8,24},{9,... | collective-permute-start | bytes 589832 | tf_op jit(solution)/shard_map/ppermute | solution.py:351
  215.4 33.0 %collective-permute-start.19 = (bf16[192,512]{1,0:T(8,128)(2,1)S(1)}, bf16[192,512]{1,0:T(8,128)(2,1)S(1)}, u32[]{:S(2)}, u32[]{:S(2)}) collective-permute-start(bf16[192,512]{1,0:T(8,128)(2,1)S(1)} %collective-permute-done.15.rest_0_), channel_id=1, source_target_pairs={{0,1},{1,0},{2,3},{3,2},{4,5},{5,4},{6,7},{7,6},{8,9},{9,8},{10,11... | collective-permute-start | bytes 589832 | tf_op jit(solution)/shard_map/ppermute | solution.py:351
  215.4 33.0 %collective-permute-start.20 = (bf16[192,512]{1,0:T(8,128)(2,1)S(1)}, bf16[192,512]{1,0:T(8,128)(2,1)S(1)}, u32[]{:S(2)}, u32[]{:S(2)}) collective-permute-start(bf16[192,512]{1,0:T(8,128)(2,1)S(1)} %collective-permute-done.16.rest_1_), channel_id=1, source_target_pairs={{0,1},{1,0},{2,3},{3,2},{4,5},{5,4},{6,7},{7,6},{8,9},{9,8},{10,11... | collective-permute-start | bytes 589832 | tf_op jit(solution)/shard_map/ppermute | solution.py:351
  215.9 30.6 %collective-permute-start.29 = (bf16[192,512]{1,0:T(8,128)(2,1)S(1)}, bf16[192,512]{1,0:T(8,128)(2,1)S(1)}, u32[]{:S(2)}, u32[]{:S(2)}) collective-permute-start(bf16[192,512]{1,0:T(8,128)(2,1)S(1)} %collective-permute-done.25.rest_3_), channel_id=1, source_target_pairs={{0,1},{1,0},{2,3},{3,2},{4,5},{5,4},{6,7},{7,6},{8,9},{9,8},{10,11... | collective-permute-start | bytes 589832 | tf_op jit(solution)/shard_map/ppermute | solution.py:351
  216.0 32.4 %collective-permute-start.21 = (bf16[192,512]{1,0:T(8,128)(2,1)S(1)}, bf16[192,512]{1,0:T(8,128)(2,1)S(1)}, u32[]{:S(2)}, u32[]{:S(2)}) collective-permute-start(bf16[192,512]{1,0:T(8,128)(2,1)S(1)} %collective-permute-done.17.rest_2_), channel_id=1, source_target_pairs={{0,1},{1,0},{2,3},{3,2},{4,5},{5,4},{6,7},{7,6},{8,9},{9,8},{10,11... | collective-permute-start | bytes 589832 | tf_op jit(solution)/shard_map/ppermute | solution.py:351
  220.6 27.8 %collective-permute-start.22 = (bf16[192,512]{1,0:T(8,128)(2,1)S(1)}, bf16[192,512]{1,0:T(8,128)(2,1)S(1)}, u32[]{:S(2)}, u32[]{:S(2)}) collective-permute-start(bf16[192,512]{1,0:T(8,128)(2,1)S(1)} %collective-permute-done.18.rest_3_), channel_id=1, source_target_pairs={{0,1},{1,0},{2,3},{3,2},{4,5},{5,4},{6,7},{7,6},{8,9},{9,8},{10,11... | collective-permute-start | bytes 589832 | tf_op jit(solution)/shard_map/ppermute | solution.py:351
  (67 other events, 588.0 us)

commit v2 on v0

v2 whole, which is shorter than its diff:
```python
import functools
import math

import jax
import jax.numpy as jnp
from jax import lax
from jax.experimental import pallas as pl
from jax.experimental.pallas import tpu as pltpu
from jax.sharding import PartitionSpec as P

NS_STEPS = 5
BF = jnp.bfloat16
F32 = jnp.float32
VMEM_BYTES = 60 * 1024 * 1024

def cost(us):
    return pl.CostEstimate(flops=1, bytes_accessed=int(us * 3.3e6) + 1, transcendentals=0)


COST_APPLY = cost(0)
COST_PACK = cost(0)
COST_GRADS = cost(0)
COST_ADD = cost(0)
COST_NEWTON = cost(0)
COST_PLACE = cost(0)

HBM = pl.BlockSpec(memory_space=pltpu.HBM)
ANY = pl.BlockSpec(memory_space=pl.ANY)
SMEM = pl.BlockSpec(memory_space=pltpu.SMEM)
VMEM = pl.BlockSpec(memory_space=pltpu.VMEM)

NZ = 4
PLANE = 8
DEVICES = NZ * PLANE
SENDS = 2


def newton_batch(xmat, width):
    for step in range(NS_STEPS):
        amat = jnp.einsum("mdf,mef->mde", xmat, xmat, preferred_element_type=F32).astype(BF)
        square = jnp.einsum("mde,mef->mdf", amat, amat, preferred_element_type=F32)
        bmat = (-4.775 * amat.astype(F32) + 2.0315 * square).astype(BF)
        nxt = 3.4445 * xmat.astype(F32) + jnp.einsum(
            "mde,mef->mdf", bmat, xmat, preferred_element_type=F32
        )
        if step == NS_STEPS - 1:
            nxt = nxt * (0.2 * math.sqrt(width))
        xmat = nxt.astype(BF)
    return xmat


def per_device_plain(queries, keys, values, token_rates, w_gate, w_up, w_down):
    head_count, head_size, hidden = w_gate.shape
    tokens = queries.shape[0]
    scale_one = head_size ** (-0.5)
    scale_two = hidden ** (-0.5)
    qpart = queries.reshape(tokens, head_count, head_size)
    kpart = keys.reshape(tokens, head_count, head_size)
    vpart = values.reshape(tokens, head_count, head_size)
    gq = scale_one * jnp.einsum("thd,hdf->htf", qpart, w_gate, preferred_element_type=F32)
    uq = scale_one * jnp.einsum("thd,hdf->htf", qpart, w_up, preferred_element_type=F32)
    hq = (jax.nn.silu(gq) * uq).astype(BF)
    applied = (
        scale_two * jnp.einsum("htf,hfd->thd", hq, w_down, preferred_element_type=F32)
    ).astype(BF)
    applied = applied.reshape(tokens, head_count * head_size)
    gk = scale_one * jnp.einsum("thd,hdf->htf", kpart, w_gate, preferred_element_type=F32)
    uk = scale_one * jnp.einsum("thd,hdf->htf", kpart, w_up, preferred_element_type=F32)
    hk = (jax.nn.silu(gk) * uk).astype(BF)
    vrate = (jnp.transpose(token_rates)[:, :, None] * vpart.astype(F32)).astype(BF)
    gdown = -scale_two * jnp.einsum("thd,htf->hdf", vrate, hk, preferred_element_type=F32)
    dhid = -scale_two * jnp.einsum("thd,hfd->htf", vrate, w_down, preferred_element_type=F32)
    sig = jax.nn.sigmoid(gk)
    dgate = (dhid * uk * sig * (1.0 + gk * (1.0 - sig))).astype(BF)
    dup = (dhid * jax.nn.silu(gk)).astype(BF)
    ggate = scale_one * jnp.einsum("thd,htf->hdf", kpart, dgate, preferred_element_type=F32)
    gup = scale_one * jnp.einsum("thd,htf->hdf", kpart, dup, preferred_element_type=F32)
    total = lax.psum(jnp.stack([ggate, gup, gdown], axis=1), "seq")
    norms = jnp.sqrt(jnp.sum(total * total, axis=(2, 3)))
    xmat = (total / (norms[:, :, None, None] + 1e-07)).astype(BF)
    result = newton_batch(xmat.reshape(head_count * 3, head_size, hidden), hidden)
    result = result.reshape(head_count, 3, head_size, hidden)
    return (applied, result[:, 0], result[:, 1], result[:, 2])


def sigmoid(x):
    return 0.5 * jnp.tanh(0.5 * x) + 0.5


def dot(a, b, dims=((1,), (0,))):
    return lax.dot_general(a, b, (dims, ((), ())), preferred_element_type=F32)


def applied_kernel(scale_one, scale_two, q_ref, wg_ref, wu_ref, wd_ref, out_ref):
    heads, size, _ = wg_ref.shape
    for head in range(heads):
        cols = slice(head * size, (head + 1) * size)
        q = q_ref[:, cols]
        gq = scale_one * dot(q, wg_ref[head])
        hq = (gq * sigmoid(gq) * dot(q, wu_ref[head])).astype(BF)
        out_ref[:, cols] = (scale_one * scale_two * dot(hq, wd_ref[head])).astype(BF)


def apply_queries(queries, w_gate, w_up, w_down):
    heads, size, hidden = w_gate.shape
    tokens = queries.shape[0]
    each = 4
    return pl.pallas_call(
        functools.partial(applied_kernel, size**-0.5, hidden**-0.5),
        grid=(heads // each,),
        out_shape=jax.ShapeDtypeStruct(queries.shape, BF),
        in_specs=[
            pl.BlockSpec((tokens, each * size), lambda h: (0, h)),
            pl.BlockSpec((each, size, hidden), lambda h: (h, 0, 0)),
            pl.BlockSpec((each, size, hidden), lambda h: (h, 0, 0)),
            pl.BlockSpec((each, hidden, size), lambda h: (h, 0, 0)),
        ],
        out_specs=pl.BlockSpec((tokens, each * size), lambda h: (0, h)),
        compiler_params=pltpu.CompilerParams(vmem_limit_bytes=VMEM_BYTES),
        cost_estimate=COST_APPLY,
        name="apply_queries",
    )(queries, w_gate, w_up, w_down)


def pack_kernel(size, k_ref, v_ref, rate_ref, *rest):
    out_ref = rest[-1]
    rates = jnp.transpose(rate_ref[...])
    for head in range(PLANE):
        cols = slice(head * size, (head + 1) * size)
        out_ref[head, 0] = k_ref[:, cols]
        out_ref[head, 1] = (rates[:, head : head + 1] * v_ref[:, cols].astype(F32)).astype(BF)


def pack_tokens(keys, values, rates, group, size, *follows):
    tokens = keys.shape[0]
    cols = PLANE * size
    return pl.pallas_call(
        functools.partial(pack_kernel, size),
        grid=(1,),
        out_shape=jax.ShapeDtypeStruct((PLANE, 2, tokens, size), BF),
        in_specs=[
            pl.BlockSpec((tokens, cols), lambda i: (0, group)),
            pl.BlockSpec((tokens, cols), lambda i: (0, group)),
            pl.BlockSpec((PLANE, tokens), lambda i: (group, 0)),
        ]
        + [ANY] * len(follows),
        out_specs=pl.BlockSpec((PLANE, 2, tokens, size), lambda i: (0, 0, 0, 0)),
        compiler_params=pltpu.CompilerParams(vmem_limit_bytes=VMEM_BYTES),
        cost_estimate=COST_PACK,
        name="pack_tokens",
    )(keys, values, rates, *follows)


def grads_kernel(group, scale_one, scale_two, where_ref, wg_ref, wu_ref, wd_ref, blocks, *rest):
    keep, *send = rest[-9 - SENDS : -8]
    held, total, final, wg_held, wu_held, wd_held, in_sem, sem = rest[-8:]
    head = group * PLANE + where_ref[0]
    weights = [
        pltpu.make_async_copy(ref.at[head], to, in_sem.at[PLANE + i])
        for i, (ref, to) in enumerate(((wg_ref, wg_held), (wu_ref, wu_held), (wd_ref, wd_held)))
    ]
    for copy in weights:
        copy.start()
    copies = [
        pltpu.make_async_copy(blocks.at[b], held.at[b], in_sem.at[b]) for b in range(PLANE)
    ]
    for copy in copies:
        copy.start()
    for copy in weights:
        copy.wait()
    wg, wu = wg_held[...], wu_held[...]
    wdt = jnp.transpose(wd_held[...])
    for b in range(PLANE):
        copies[b].wait()
        k, vr = held[b, 0], held[b, 1]
        gk = scale_one * dot(k, wg)
        uk = dot(k, wu)
        dh = dot(vr, wdt)
        sig = sigmoid(gk)
        act = gk * sig
        hk = (act * uk).astype(BF)
        dg = (dh * uk * (sig + act * (1.0 - sig))).astype(BF)
        du = (dh * act).astype(BF)
        kt, vt = jnp.transpose(k), jnp.transpose(vr)
        parts = (dot(kt, dg), dot(kt, du), dot(vt, hk))
        for i in range(3):
            if b == 0:
                total[i] = parts[i]
            else:
                total[i] += parts[i]
    both = -scale_one * scale_two
    final[0] = (both * scale_one * total[0]).astype(BF)
    final[1] = (both * total[1]).astype(BF)
    final[2] = (both * total[2]).astype(BF)
    odd = where_ref[4]
    pairs = [(final.at[odd], keep.at[0]), (final.at[2], keep.at[1])]
    each = SENDS // 2
    rows = final.shape[1] // each
    for i in range(each):
        pairs.append((final.at[1 - odd, pl.ds(i * rows, rows)], send[i]))
        pairs.append((final.at[2, pl.ds(i * rows, rows)], send[each + i]))
    run_copies(pairs, sem)


def head_grads(where, blocks, w_gate, w_up, w_down, group, *follows):
    _, size, hidden = w_gate.shape
    tokens = blocks.shape[2]
    return pl.pallas_call(
        functools.partial(grads_kernel, group, size**-0.5, hidden**-0.5),
        out_shape=[jax.ShapeDtypeStruct((2, size, hidden), BF)]
        + [jax.ShapeDtypeStruct((2 * size // SENDS, hidden), BF)] * SENDS,
        in_specs=[SMEM] + [HBM] * 3 + [ANY] * (1 + len(follows)),
        out_specs=[ANY] * (1 + SENDS),
        scratch_shapes=[
            pltpu.VMEM((PLANE, 2, tokens, size), BF),
            pltpu.VMEM((3, size, hidden), F32),
            pltpu.VMEM((3, size, hidden), BF),
            pltpu.VMEM((size, hidden), BF),
            pltpu.VMEM((size, hidden), BF),
            pltpu.VMEM((hidden, size), BF),
            pltpu.SemaphoreType.DMA((PLANE + 3,)),
            pltpu.SemaphoreType.DMA((2 + SENDS,)),
        ],
        compiler_params=pltpu.CompilerParams(vmem_limit_bytes=48 * 1024 * 1024),
        cost_estimate=COST_GRADS,
        name="head_grads",
    )(where, w_gate, w_up, w_down, blocks, *follows)


def combine_kernel(a_ref, *rest):
    parts, out_ref = rest[:SENDS], rest[-1]
    rows = parts[0].shape[0]
    each = out_ref.shape[1] // rows
    for i, part in enumerate(parts):
        at = (i // each, slice(i % each * rows, (i % each + 1) * rows))
        out_ref[at] = (a_ref[at].astype(F32) + part[...].astype(F32)).astype(BF)


def combine(a, parts, *follows):
    return pl.pallas_call(
        combine_kernel,
        out_shape=jax.ShapeDtypeStruct(a.shape, BF),
        in_specs=[VMEM] * (1 + SENDS) + [ANY] * len(follows),
        out_specs=VMEM,
        compiler_params=pltpu.CompilerParams(vmem_limit_bytes=8 * 1024 * 1024),
        cost_estimate=COST_ADD,
        name="add_partials",
    )(a, *parts, *follows)


def newton_kernel(where_ref, mine_ref, other_ref, *rest):
    out_ref, held = rest[-2:]
    size, width = held.shape
    half = size // 2
    mats = []
    for i in range(2):
        grad = mine_ref[i].astype(F32) + other_ref[i].astype(F32)
        norm = jnp.sqrt(jnp.sum(grad * grad))
        mats.append((grad / (norm + 1e-07)).astype(BF))
    for step in range(NS_STEPS):
        squares = [dot(x, x, ((1,), (1,))).astype(BF) for x in mats]
        mixes = [
            (-4.775 * a.astype(F32) + 2.0315 * dot(a, a)).astype(BF) for a in squares
        ]
        nexts = [3.4445 * x.astype(F32) + dot(b, x) for b, x in zip(mixes, mats)]
        if step == NS_STEPS - 1:
            nexts = [n * (0.2 * math.sqrt(width)) for n in nexts]
        mats = [n.astype(BF) for n in nexts]
    out_ref[:size] = mats[0]
    held[...] = mats[1]
    odd = where_ref[4]
    out_ref[size:] = held[pl.ds(pl.multiple_of(odd * half, half), half), :]


def newton(where, mine, other, *follows):
    _, size, hidden = mine.shape
    return pl.pallas_call(
        newton_kernel,
        out_shape=jax.ShapeDtypeStruct((size + size // 2, hidden), BF),
        in_specs=[SMEM] + [VMEM] * 2 + [ANY] * len(follows),
        out_specs=VMEM,
        scratch_shapes=[pltpu.VMEM((size, hidden), BF)],
        compiler_params=pltpu.CompilerParams(vmem_limit_bytes=20 * 1024 * 1024),
        cost_estimate=COST_NEWTON,
        name="newton_schulz",
    )(where, mine, other, *follows)


def run_copies(pairs, sem):
    copies = [pltpu.make_async_copy(a, b, sem.at[i]) for i, (a, b) in enumerate(pairs)]
    for copy in copies:
        copy.start()
    for copy in copies:
        copy.wait()


def place_kernel(count, size, where_ref, *rest):
    blocks, (gate, up, down, sem) = rest[:-4], rest[-4:]
    z, y, x, core = (where_ref[i] for i in range(1, 5))
    half = size // 2

    def put(parity):
        pairs = []
        for i, block in enumerate(blocks):
            group, flip, other, kind = i // 16, i // 8 % 2, i // 4 % 2, i % 4
            side, c = (1 - parity, 1 - core) if other else (parity, core)
            at = ((y, x), (y ^ (1 - c), x ^ c), (y ^ c, x ^ (1 - c)), (1 - y, 1 - x))[kind]
            head = group * PLANE + (lax.rem(z, 2) ^ flip) * 4 + at[0] * 2 + at[1]
            m0 = up if side else gate
            pairs.append((block.at[pl.ds(0, size)], m0.at[head]))
            pairs.append((block.at[pl.ds(size, half)], down.at[head, pl.ds(side * half, half)]))
        run_copies(pairs, sem)

    for parity in range(2):

        @pl.when(core == parity)
        def _():
            put(parity)


def place(where, blocks, shape):
    count = len(blocks)
    return pl.pallas_call(
        functools.partial(place_kernel, count, shape[1]),
        out_shape=[jax.ShapeDtypeStruct(shape, BF)] * 3,
        in_specs=[SMEM] + [ANY] * count,
        out_specs=[ANY] * 3,
        scratch_shapes=[pltpu.SemaphoreType.DMA((2 * count,))],
        compiler_params=pltpu.CompilerParams(vmem_limit_bytes=2 * 1024 * 1024),
        name="place_steps",
    )(where, *blocks)


def permutation(target):
    pairs = []
    for i in range(DEVICES):
        z, y, x, core = target(i // 8, i // 4 % 2, i // 2 % 2, i % 2)
        pairs.append((i, ((z * 2 + y) * 2 + x) * 2 + core))
    return pairs


CUBES = [
    [((2 * zhi + zlo) * 4 + yx) * 2 + core for zlo in range(2) for yx in range(4)]
    for zhi in range(2)
    for core in range(2)
]
Z_MOVES = [permutation(lambda z, y, x, c, s=s: (z ^ s, y, x, c)) for s in range(NZ)]
FIRST_MOVE = permutation(lambda z, y, x, c: (z, y ^ (1 - c), x ^ c, c))
SECOND_MOVE = permutation(lambda z, y, x, c: (z, y ^ c, x ^ (1 - c), c))
CORE_MOVE = permutation(lambda z, y, x, c: (z, y, x, 1 - c))


def move(array, pairs):
    return lax.ppermute(array, "seq", pairs)


def after(array, *others):
    return lax.optimization_barrier((array, *others))[0]


def per_device_fast(queries, keys, values, token_rates, w_gate, w_up, w_down):
    heads, size, hidden = w_gate.shape
    groups = heads // PLANE
    index = lax.axis_index("seq")
    z, core = index // 8, index % 2
    y, x = index // 4 % 2, index // 2 % 2
    where = jnp.stack([z % 2 * 4 + y * 2 + x, z, y, x, core]).astype(jnp.int32)

    packed = [pack_tokens(keys, values, token_rates, 0, size)]
    applied = apply_queries(queries, w_gate, w_up, w_down)
    for group in range(1, groups):
        packed.append(pack_tokens(keys, values, token_rates, group, size, applied))
    received = [
        lax.all_to_all(block, "seq", 0, 0, axis_index_groups=CUBES, tiled=True)
        for block in packed
    ]

    pairs, others, follow = [], [], ()
    for group in range(groups):
        keep, *send = head_grads(where, received[group], w_gate, w_up, w_down, group, *follow)
        pairs.append(combine(keep, [move(block, CORE_MOVE) for block in send], *others[-1:]))
        others.append(move(pairs[-1], Z_MOVES[2]))
        follow = pairs[-1:]
    blocks = []
    for group in range(groups):
        follow = pairs[group + 1 : group + 2]
        block = newton(where, pairs[group], others[group], *follow)
        for flip in range(2):
            if flip:
                block = move(block, Z_MOVES[1])
            one = move(block, FIRST_MOVE)
            two = move(block, SECOND_MOVE)
            three = move(one, SECOND_MOVE)
            mine = [block, one, two, three]
            blocks += mine + [move(b, CORE_MOVE) for b in mine]
    steps = place(where, blocks, w_gate.shape)
    return (applied, *steps)


def solution(mesh):
    in_specs = (
        P("seq", "head"),
        P("seq", "head"),
        P("seq", "head"),
        P("head", "seq"),
        P("head", None, None),
        P("head", None, None),
        P("head", None, None),
    )
    out_specs = (
        P("seq", "head"),
        P("head", None, None),
        P("head", None, None),
        P("head", None, None),
    )
    sizes = mesh.shape

    def per_device(*args):
        heads = args[4].shape[0]
        fast = sizes["seq"] == DEVICES and heads % PLANE == 0
        return (per_device_fast if fast else per_device_plain)(*args)

    return jax.shard_map(
        per_device, mesh=mesh, in_specs=in_specs, out_specs=out_specs, check_vma=False
    )
```

time: 712 us -> 169 us (0.24); the launches traced: 704 us -> 169 us
  waiting for transfers between devices: 369 us -> 75.6 us
  matrix products: 254 us -> 0 us
  Pallas kernels: 0 us -> 46.3 us
  starting transfers between devices: 0.04 us -> 42.8 us
  other arithmetic: 32.3 us -> 0 us
  local copies, waits for them, and re-layouts: 34.1 us -> 2.99 us
  between operations: 14.5 us -> 0.97 us
    psum x1 -> x0, waiting for transfers between devices: 369 us -> none  [per_device(): total = lax.psum(stacked, 'seq')]
    dot_general x18 -> x0, matrix products: 254 us -> none  [the longest x5 120 us: newton_batch(): jnp.einsum('mde,mef->mdf', bmat, xmat, preferred_element_type=jnp.float32)]
    pallas_call x0 -> x10, Pallas kernels: none -> 46.3 us  [the longest x2 16.8 us: head_grads(): pl.pallas_call(functools.partial(grads_kernel, group, size ** (-0.5), hid...]
    ppermute x0 -> x36, waiting for transfers between devices: none -> 41.3 us  [move(): return lax.ppermute(array, 'seq', pairs)]
    all_to_all x0 -> x2, waiting for transfers between devices: none -> 34.3 us  [per_device_fast(): lax.all_to_all(block, 'seq', 0, 0, axis_index_groups=CUBES, tiled=True)]
    ppermute x0 -> x36, starting transfers between devices: none -> 31.6 us  [move(): return lax.ppermute(array, 'seq', pairs)]
    another operation x1 -> x0, other arithmetic: 18 us -> none  [per_device(): stacked = jnp.stack([ggate, gup, gdown], axis=1)]
    unnamed x17 -> x4, local copies, waits for them, and re-layouts: 15 us -> 2.91 us
  transfers between devices with their start and end apart: 1 -> 38, of which waited for: 1 -> 15; matrix products, arithmetic and copies ran while one was open for 3% -> 0% of each run, Pallas kernels for 0% -> 20%
where the time goes in v2:
time: 169 us
  waiting for transfers between devices  75.6 us (45%)
  Pallas kernels  46.3 us (27%)
  starting transfers between devices  42.8 us (25%)
  local copies, waits for them, and re-layouts  2.99 us (2%)
    ppermute x36, waiting for transfers between devices, move(): return lax.ppermute(array, 'seq', pairs)  41.3 us
    all_to_all x2, waiting for transfers between devices, per_device_fast(): lax.all_to_all(block, 'seq', 0, 0, axis_index_groups=CUBES, tiled=True)  34.3 us
    ppermute x36, starting transfers between devices, move(): return lax.ppermute(array, 'seq', pairs)  31.6 us
    pallas_call x2, Pallas kernels, head_grads(): pl.pallas_call(functools.partial(grads_kernel, group, size ** (-0.5), hid...  16.8 us
    all_to_all x2, starting transfers between devices, per_device_fast(): lax.all_to_all(block, 'seq', 0, 0, axis_index_groups=CUBES, tiled=True)  11.3 us
    pallas_call x1, Pallas kernels, apply_queries(): pl.pallas_call(functools.partial(applied_kernel, size ** (-0.5), hidden *...  9.19 us
    pallas_call x2, Pallas kernels, newton(): pl.pallas_call(newton_kernel, out_shape=jax.ShapeDtypeStruct((size + size...  7.71 us
    pallas_call x2, Pallas kernels, pack_tokens(): pl.pallas_call(functools.partial(pack_kernel, size), grid=(1,), out_shape...  6.77 us
  transfers between devices with their start and end apart: 38, of which 15 were waited for; matrix products, arithmetic and copies ran while one was open for 0% of the time, Pallas kernels for 20%

profile of v2, /device:TPU:0, one launch (start us, length us, event | category | flops | bytes accessed | tf_op | source)
XLA Modules:
  0.0 168.7 jit_solution(9676901344287469790)
XLA Ops:
  0.6 3.4 %pack_tokens.2 = bf16[8,2,256,256]{3,2,1,0:T(8,128)(2,1)} custom-call(bf16[256,4096]{1,0:T(8,128)(2,1)} %k_ref.3, bf16[256,4096]{1,0:T(8,128)(2,1)} %v_ref.3, f32[16,256]{1,0:T(8,128)} %rate_ref.3), custom_call_target="tpu_custom_call" | custom-call | flops 1 | bytes 1 | tf_op jit(solution)/shard_map/pack_tokens/pallas_call | solution.py:137
  4.0 6.2 %all-to-all-start = ((bf16[8,2,256,256]{3,2,1,0:T(8,128)(2,1)}), bf16[8,2,256,256]{3,2,1,0:T(8,128)(2,1)S(1)}, u32[]{:S(2)}, u32[]{:S(2)}) async-start(bf16[8,2,256,256]{3,2,1,0:T(8,128)(2,1)} %pack_tokens.2), calls=%async_computation | async-start | bytes 4194304 | tf_op jit(solution)/shard_map/all_to_all | solution.py:374
  10.2 9.2 %apply_queries.1.rest_0_ = bf16[256,4096]{1,0:T(8,128)(2,1)} custom-call(bf16[256,4096]{1,0:T(8,128)(2,1)} %q_ref.1, bf16[16,256,512]{2,1,0:T(8,128)(2,1)} %wg_ref.5, bf16[16,256,512]{2,1,0:T(8,128)(2,1)} %wu_ref.5, bf16[16,512,256]{2,1,0:T(8,128)(2,1)} %wd_ref.5), custom_call_target="tpu_custom_call" | custom-call | flops 1 | bytes 1 | tf_op jit(solution)/shard_map/apply_queries/pallas_call | solution.py:108
  19.4 3.4 %pack_tokens.3 = bf16[8,2,256,256]{3,2,1,0:T(8,128)(2,1)} custom-call(bf16[256,4096]{1,0:T(8,128)(2,1)} %k_ref.3, bf16[256,4096]{1,0:T(8,128)(2,1)} %v_ref.3, f32[16,256]{1,0:T(8,128)} %rate_ref.3, bf16[256,4096]{1,0:T(8,128)(2,1)} %apply_queries.1.rest_0_), custom_call_target="tpu_custom_call" | custom-call | flops 1 | bytes 1 | tf_op jit(solution)/shard_map/pack_tokens/pallas_call | solution.py:137
  22.8 13.4 %all-to-all-done.blocks = bf16[8,2,256,256]{3,2,1,0:T(8,128)(2,1)S(1)} async-done(((bf16[8,2,256,256]{3,2,1,0:T(8,128)(2,1)}), bf16[8,2,256,256]{3,2,1,0:T(8,128)(2,1)S(1)}, u32[]{:S(2)}, u32[]{:S(2)}) %all-to-all-start) | async-done | bytes 2097184 | tf_op jit(solution)/shard_map/all_to_all | solution.py:374
  37.5 5.1 %all-to-all-start.1 = ((bf16[8,2,256,256]{3,2,1,0:T(8,128)(2,1)}), bf16[8,2,256,256]{3,2,1,0:T(8,128)(2,1)S(1)}, u32[]{:S(2)}, u32[]{:S(2)}) async-start(bf16[8,2,256,256]{3,2,1,0:T(8,128)(2,1)} %pack_tokens.3), calls=%async_computation.1 | async-start | bytes 4194304 | tf_op jit(solution)/shard_map/all_to_all | solution.py:374
  44.2 8.3 %head_grads.2 = (bf16[2,256,512]{2,1,0:T(8,128)(2,1)S(1)}, bf16[256,512]{1,0:T(8,128)(2,1)S(1)}, bf16[256,512]{1,0:T(8,128)(2,1)S(1)}) custom-call(s32[5]{0:T(128)S(1)} %stack.23.where_ref, bf16[16,256,512]{2,1,0:T(8,128)(2,1)} %wg_ref.5, bf16[16,256,512]{2,1,0:T(8,128)(2,1)} %wu_ref.5, bf16[16,512,256]{2,1,0:T(8,128)(2,1)} %wd_ref.5, ...), custom_call_target="tpu_custom_call" | custom-call | flops 1 | bytes 1 | tf_op jit(solution)/shard_map/head_grads/pallas_call | solution.py:208
  54.6 2.6 %collective-permute-start.2 = (bf16[2,256,512]{2,1,0:T(8,128)(2,1)S(1)}, bf16[2,256,512]{2,1,0:T(8,128)(2,1)S(1)}, u32[]{:S(2)}, u32[]{:S(2)}) collective-permute-start(bf16[2,256,512]{2,1,0:T(8,128)(2,1)S(1)} %add_partials.2.rest_0_.mine_ref), channel_id=1, source_target_pairs={{0,16},{1,17},{2,18},{3,19},{4,20},{5,21},{6,22},{7,23},{8,24},{9,... | collective-permute-start | bytes 1572872 | tf_op jit(solution)/shard_map/ppermute | solution.py:354
  57.3 20.9 %all-to-all-done.1.blocks = bf16[8,2,256,256]{3,2,1,0:T(8,128)(2,1)S(1)} async-done(((bf16[8,2,256,256]{3,2,1,0:T(8,128)(2,1)}), bf16[8,2,256,256]{3,2,1,0:T(8,128)(2,1)S(1)}, u32[]{:S(2)}, u32[]{:S(2)}) %all-to-all-start.1) | async-done | bytes 2097184 | tf_op jit(solution)/shard_map/all_to_all | solution.py:374
  78.2 8.5 %head_grads.3 = (bf16[2,256,512]{2,1,0:T(8,128)(2,1)S(1)}, bf16[256,512]{1,0:T(8,128)(2,1)S(1)}, bf16[256,512]{1,0:T(8,128)(2,1)S(1)}) custom-call(s32[5]{0:T(128)S(1)} %stack.23.where_ref, bf16[16,256,512]{2,1,0:T(8,128)(2,1)} %wg_ref.5, bf16[16,256,512]{2,1,0:T(8,128)(2,1)} %wu_ref.5, bf16[16,512,256]{2,1,0:T(8,128)(2,1)} %wd_ref.5, ...), custom_call_target="tpu_custom_call" | custom-call | flops 1 | bytes 1 | tf_op jit(solution)/shard_map/head_grads/pallas_call | solution.py:208
  88.8 3.9 %newton_schulz.2.rest_0_ = bf16[384,512]{1,0:T(8,128)(2,1)S(1)} custom-call(s32[5]{0:T(128)S(1)} %stack.23.where_ref, bf16[2,256,512]{2,1,0:T(8,128)(2,1)S(1)} %add_partials.2.rest_0_.mine_ref, bf16[2,256,512]{2,1,0:T(8,128)(2,1)S(1)} %collective-permute-done.2.rest_2_.other_ref, bf16[2,256,512]{2,1,0:T(8,128)(2,1)S(1)} %add_partials.3.rest_0_.mine_ref), custom_call_target="tpu_custom_call" | custom-call | flops 1 | bytes 1 | tf_op jit(solution)/shard_map/newton_schulz/pallas_call | solution.py:277
  93.7 3.5 %collective-permute-start.6 = (bf16[384,512]{1,0:T(8,128)(2,1)S(1)}, bf16[384,512]{1,0:T(8,128)(2,1)S(1)}, u32[]{:S(2)}, u32[]{:S(2)}) collective-permute-start(bf16[384,512]{1,0:T(8,128)(2,1)S(1)} %newton_schulz.2.rest_0_), channel_id=1, source_target_pairs={{0,2},{1,5},{2,0},{3,7},{4,6},{5,1},{6,4},{7,3},{8,10},{9,13},{10,... | collective-permute-start | bytes 1179656 | tf_op jit(solution)/shard_map/ppermute | solution.py:354
  98.7 11.4 %collective-permute-done.12.rest_8_ = bf16[384,512]{1,0:T(8,128)(2,1)S(1)} collective-permute-done((bf16[384,512]{1,0:T(8,128)(2,1)S(1)}, bf16[384,512]{1,0:T(8,128)(2,1)S(1)}, u32[]{:S(2)}, u32[]{:S(2)}) %collective-permute-start.12) | collective-permute-done | bytes 393248 | tf_op jit(solution)/shard_map/ppermute | solution.py:354
  110.0 3.5 %collective-permute-start.14 = (bf16[384,512]{1,0:T(8,128)(2,1)S(1)}, bf16[384,512]{1,0:T(8,128)(2,1)S(1)}, u32[]{:S(2)}, u32[]{:S(2)}) collective-permute-start(bf16[384,512]{1,0:T(8,128)(2,1)S(1)} %collective-permute-done.12.rest_8_), channel_id=1, source_target_pairs={{0,2},{1,5},{2,0},{3,7},{4,6},{5,1},{6,4},{7,3},{8,10},{9,13},{10,... | collective-permute-start | bytes 1179656 | tf_op jit(solution)/shard_map/ppermute | solution.py:354
  115.0 3.9 %collective-permute-done.20.other_ref = bf16[2,256,512]{2,1,0:T(8,128)(2,1)S(1)} collective-permute-done((bf16[2,256,512]{2,1,0:T(8,128)(2,1)S(1)}, bf16[2,256,512]{2,1,0:T(8,128)(2,1)S(1)}, u32[]{:S(2)}, u32[]{:S(2)}) %collective-permute-start.20) | collective-permute-done | bytes 524320 | tf_op jit(solution)/shard_map/ppermute | solution.py:354
  119.0 3.6 %collective-permute-start.7 = (bf16[384,512]{1,0:T(8,128)(2,1)S(1)}, bf16[384,512]{1,0:T(8,128)(2,1)S(1)}, u32[]{:S(2)}, u32[]{:S(2)}) collective-permute-start(bf16[384,512]{1,0:T(8,128)(2,1)S(1)} %collective-permute-done.5.rest_1_), channel_id=1, source_target_pairs={{0,2},{1,5},{2,0},{3,7},{4,6},{5,1},{6,4},{7,3},{8,10},{9,13},{10,... | collective-permute-start | bytes 1179656 | tf_op jit(solution)/shard_map/ppermute | solution.py:354
  122.5 3.9 %newton_schulz.3.rest_16_ = bf16[384,512]{1,0:T(8,128)(2,1)S(1)} custom-call(s32[5]{0:T(128)S(1)} %stack.23.where_ref, bf16[2,256,512]{2,1,0:T(8,128)(2,1)S(1)} %add_partials.3.rest_0_.mine_ref, bf16[2,256,512]{2,1,0:T(8,128)(2,1)S(1)} %collective-permute-done.20.other_ref), custom_call_target="tpu_custom_call" | custom-call | flops 1 | bytes 1 | tf_op jit(solution)/shard_map/newton_schulz/pallas_call | solution.py:277
  128.8 6.1 %collective-permute-done.28.rest_24_ = bf16[384,512]{1,0:T(8,128)(2,1)S(1)} collective-permute-done((bf16[384,512]{1,0:T(8,128)(2,1)S(1)}, bf16[384,512]{1,0:T(8,128)(2,1)S(1)}, u32[]{:S(2)}, u32[]{:S(2)}) %collective-permute-start.28) | collective-permute-done | bytes 393248 | tf_op jit(solution)/shard_map/ppermute | solution.py:354
  135.0 3.6 %collective-permute-start.15 = (bf16[384,512]{1,0:T(8,128)(2,1)S(1)}, bf16[384,512]{1,0:T(8,128)(2,1)S(1)}, u32[]{:S(2)}, u32[]{:S(2)}) collective-permute-start(bf16[384,512]{1,0:T(8,128)(2,1)S(1)} %collective-permute-done.13.rest_9_), channel_id=1, source_target_pairs={{0,2},{1,5},{2,0},{3,7},{4,6},{5,1},{6,4},{7,3},{8,10},{9,13},{10,... | collective-permute-start | bytes 1179656 | tf_op jit(solution)/shard_map/ppermute | solution.py:354
  141.1 6.1 %collective-permute-done.15.rest_11_ = bf16[384,512]{1,0:T(8,128)(2,1)S(1)} collective-permute-done((bf16[384,512]{1,0:T(8,128)(2,1)S(1)}, bf16[384,512]{1,0:T(8,128)(2,1)S(1)}, u32[]{:S(2)}, u32[]{:S(2)}) %collective-permute-start.15) | collective-permute-done | bytes 393248 | tf_op jit(solution)/shard_map/ppermute | solution.py:354
  147.7 2.5 %collective-permute-start.23 = (bf16[384,512]{1,0:T(8,128)(2,1)S(1)}, bf16[384,512]{1,0:T(8,128)(2,1)S(1)}, u32[]{:S(2)}, u32[]{:S(2)}) collective-permute-start(bf16[384,512]{1,0:T(8,128)(2,1)S(1)} %collective-permute-done.21.rest_17_), channel_id=1, source_target_pairs={{0,2},{1,5},{2,0},{3,7},{4,6},{5,1},{6,4},{7,3},{8,10},{9,13},{10,... | collective-permute-start | bytes 1179656 | tf_op jit(solution)/shard_map/ppermute | solution.py:354
  153.4 3.6 %collective-permute-done.23.rest_19_ = bf16[384,512]{1,0:T(8,128)(2,1)S(1)} collective-permute-done((bf16[384,512]{1,0:T(8,128)(2,1)S(1)}, bf16[384,512]{1,0:T(8,128)(2,1)S(1)}, u32[]{:S(2)}, u32[]{:S(2)}) %collective-permute-start.23) | collective-permute-done | bytes 393248 | tf_op jit(solution)/shard_map/ppermute | solution.py:354
  157.0 4.2 %collective-permute-done.31.rest_27_ = bf16[384,512]{1,0:T(8,128)(2,1)S(1)} collective-permute-done((bf16[384,512]{1,0:T(8,128)(2,1)S(1)}, bf16[384,512]{1,0:T(8,128)(2,1)S(1)}, u32[]{:S(2)}, u32[]{:S(2)}) %collective-permute-start.31) | collective-permute-done | bytes 393248 | tf_op jit(solution)/shard_map/ppermute | solution.py:354
  162.9 5.6 %place_steps.1 = (bf16[16,256,512]{2,1,0:T(8,128)(2,1)}, bf16[16,256,512]{2,1,0:T(8,128)(2,1)}, bf16[16,256,512]{2,1,0:T(8,128)(2,1)}) custom-call(s32[5]{0:T(128)S(1)} %stack.23.where_ref, bf16[384,512]{1,0:T(8,128)(2,1)S(1)} %newton_schulz.2.rest_0_, bf16[384,512]{1,0:T(8,128)(2,1)S(1)} %collective-permute-done.5.rest_1_, ...), custom_call_target="tpu_custom_call" | custom-call | tf_op jit(solution)/shard_map/place_steps/pallas_call | solution.py:323
  (67 shorter events, 21.3 us)
Async XLA Ops:
  4.0 32.1 %all-to-all-start = ((bf16[8,2,256,256]{3,2,1,0:T(8,128)(2,1)}), bf16[8,2,256,256]{3,2,1,0:T(8,128)(2,1)S(1)}, u32[]{:S(2)}, u32[]{:S(2)}) async-start(bf16[8,2,256,256]{3,2,1,0:T(8,128)(2,1)} %pack_tokens.2), calls=%async_computation | async-start | bytes 4194304 | tf_op jit(solution)/shard_map/all_to_all | solution.py:374
  37.5 40.7 %all-to-all-start.1 = ((bf16[8,2,256,256]{3,2,1,0:T(8,128)(2,1)}), bf16[8,2,256,256]{3,2,1,0:T(8,128)(2,1)S(1)}, u32[]{:S(2)}, u32[]{:S(2)}) async-start(bf16[8,2,256,256]{3,2,1,0:T(8,128)(2,1)} %pack_tokens.3), calls=%async_computation.1 | async-start | bytes 4194304 | tf_op jit(solution)/shard_map/all_to_all | solution.py:374
  54.6 34.1 %collective-permute-start.2 = (bf16[2,256,512]{2,1,0:T(8,128)(2,1)S(1)}, bf16[2,256,512]{2,1,0:T(8,128)(2,1)S(1)}, u32[]{:S(2)}, u32[]{:S(2)}) collective-permute-start(bf16[2,256,512]{2,1,0:T(8,128)(2,1)S(1)} %add_partials.2.rest_0_.mine_ref), channel_id=1, source_target_pairs={{0,16},{1,17},{2,18},{3,19},{4,20},{5,21},{6,22},{7,23},{8,24},{9,... | collective-permute-start | bytes 1572872 | tf_op jit(solution)/shard_map/ppermute | solution.py:354
  92.7 17.3 %collective-permute-start.12 = (bf16[384,512]{1,0:T(8,128)(2,1)S(1)}, bf16[384,512]{1,0:T(8,128)(2,1)S(1)}, u32[]{:S(2)}, u32[]{:S(2)}) collective-permute-start(bf16[384,512]{1,0:T(8,128)(2,1)S(1)} %newton_schulz.2.rest_0_), channel_id=1, source_target_pairs={{0,8},{1,9},{2,10},{3,11},{4,12},{5,13},{6,14},{7,15},{8,0},{9,1},... | collective-permute-start | bytes 1179656 | tf_op jit(solution)/shard_map/ppermute | solution.py:354
  92.8 26.2 %collective-permute-start.20 = (bf16[2,256,512]{2,1,0:T(8,128)(2,1)S(1)}, bf16[2,256,512]{2,1,0:T(8,128)(2,1)S(1)}, u32[]{:S(2)}, u32[]{:S(2)}) collective-permute-start(bf16[2,256,512]{2,1,0:T(8,128)(2,1)S(1)} %add_partials.3.rest_0_.mine_ref), channel_id=1, source_target_pairs={{0,16},{1,17},{2,18},{3,19},{4,20},{5,21},{6,22},{7,23},{8,24},{9,... | collective-permute-start | bytes 1572872 | tf_op jit(solution)/shard_map/ppermute | solution.py:354
  93.7 16.4 %collective-permute-start.8 = (bf16[384,512]{1,0:T(8,128)(2,1)S(1)}, bf16[384,512]{1,0:T(8,128)(2,1)S(1)}, u32[]{:S(2)}, u32[]{:S(2)}) collective-permute-start(bf16[384,512]{1,0:T(8,128)(2,1)S(1)} %newton_schulz.2.rest_0_), channel_id=1, source_target_pairs={{0,1},{1,0},{2,3},{3,2},{4,5},{5,4},{6,7},{7,6},{8,9},{9,8},{10,11... | collective-permute-start | bytes 1179656 | tf_op jit(solution)/shard_map/ppermute | solution.py:354
  93.7 19.9 %collective-permute-start.6 = (bf16[384,512]{1,0:T(8,128)(2,1)S(1)}, bf16[384,512]{1,0:T(8,128)(2,1)S(1)}, u32[]{:S(2)}, u32[]{:S(2)}) collective-permute-start(bf16[384,512]{1,0:T(8,128)(2,1)S(1)} %newton_schulz.2.rest_0_), channel_id=1, source_target_pairs={{0,2},{1,5},{2,0},{3,7},{4,6},{5,1},{6,4},{7,3},{8,10},{9,13},{10,... | collective-permute-start | bytes 1179656 | tf_op jit(solution)/shard_map/ppermute | solution.py:354
  97.2 17.8 %collective-permute-start.5 = (bf16[384,512]{1,0:T(8,128)(2,1)S(1)}, bf16[384,512]{1,0:T(8,128)(2,1)S(1)}, u32[]{:S(2)}, u32[]{:S(2)}) collective-permute-start(bf16[384,512]{1,0:T(8,128)(2,1)S(1)} %newton_schulz.2.rest_0_), channel_id=1, source_target_pairs={{0,4},{1,3},{2,6},{3,1},{4,0},{5,7},{6,2},{7,5},{8,12},{9,11},{10,... | collective-permute-start | bytes 1179656 | tf_op jit(solution)/shard_map/ppermute | solution.py:354
  110.0 9.0 %collective-permute-start.16 = (bf16[384,512]{1,0:T(8,128)(2,1)S(1)}, bf16[384,512]{1,0:T(8,128)(2,1)S(1)}, u32[]{:S(2)}, u32[]{:S(2)}) collective-permute-start(bf16[384,512]{1,0:T(8,128)(2,1)S(1)} %collective-permute-done.12.rest_8_), channel_id=1, source_target_pairs={{0,1},{1,0},{2,3},{3,2},{4,5},{5,4},{6,7},{7,6},{8,9},{9,8},{10,11... | collective-permute-start | bytes 1179656 | tf_op jit(solution)/shard_map/ppermute | solution.py:354
  110.0 16.4 %collective-permute-start.14 = (bf16[384,512]{1,0:T(8,128)(2,1)S(1)}, bf16[384,512]{1,0:T(8,128)(2,1)S(1)}, u32[]{:S(2)}, u32[]{:S(2)}) collective-permute-start(bf16[384,512]{1,0:T(8,128)(2,1)S(1)} %collective-permute-done.12.rest_8_), channel_id=1, source_target_pairs={{0,2},{1,5},{2,0},{3,7},{4,6},{5,1},{6,4},{7,3},{8,10},{9,13},{10,... | collective-permute-start | bytes 1179656 | tf_op jit(solution)/shard_map/ppermute | solution.py:354
  113.6 12.9 %collective-permute-start.13 = (bf16[384,512]{1,0:T(8,128)(2,1)S(1)}, bf16[384,512]{1,0:T(8,128)(2,1)S(1)}, u32[]{:S(2)}, u32[]{:S(2)}) collective-permute-start(bf16[384,512]{1,0:T(8,128)(2,1)S(1)} %collective-permute-done.12.rest_8_), channel_id=1, source_target_pairs={{0,4},{1,3},{2,6},{3,1},{4,0},{5,7},{6,2},{7,5},{8,12},{9,11},{10,... | collective-permute-start | bytes 1179656 | tf_op jit(solution)/shard_map/ppermute | solution.py:354
  115.0 11.6 %collective-permute-start.10 = (bf16[384,512]{1,0:T(8,128)(2,1)S(1)}, bf16[384,512]{1,0:T(8,128)(2,1)S(1)}, u32[]{:S(2)}, u32[]{:S(2)}) collective-permute-start(bf16[384,512]{1,0:T(8,128)(2,1)S(1)} %collective-permute-done.6.rest_2_), channel_id=1, source_target_pairs={{0,1},{1,0},{2,3},{3,2},{4,5},{5,4},{6,7},{7,6},{8,9},{9,8},{10,11... | collective-permute-start | bytes 1179656 | tf_op jit(solution)/shard_map/ppermute | solution.py:354
  119.0 9.3 %collective-permute-start.9 = (bf16[384,512]{1,0:T(8,128)(2,1)S(1)}, bf16[384,512]{1,0:T(8,128)(2,1)S(1)}, u32[]{:S(2)}, u32[]{:S(2)}) collective-permute-start(bf16[384,512]{1,0:T(8,128)(2,1)S(1)} %collective-permute-done.5.rest_1_), channel_id=1, source_target_pairs={{0,1},{1,0},{2,3},{3,2},{4,5},{5,4},{6,7},{7,6},{8,9},{9,8},{10,11... | collective-permute-start | bytes 1179656 | tf_op jit(solution)/shard_map/ppermute | solution.py:354
  119.0 9.9 %collective-permute-start.7 = (bf16[384,512]{1,0:T(8,128)(2,1)S(1)}, bf16[384,512]{1,0:T(8,128)(2,1)S(1)}, u32[]{:S(2)}, u32[]{:S(2)}) collective-permute-start(bf16[384,512]{1,0:T(8,128)(2,1)S(1)} %collective-permute-done.5.rest_1_), channel_id=1, source_target_pairs={{0,2},{1,5},{2,0},{3,7},{4,6},{5,1},{6,4},{7,3},{8,10},{9,13},{10,... | collective-permute-start | bytes 1179656 | tf_op jit(solution)/shard_map/ppermute | solution.py:354
  126.6 12.0 %collective-permute-start.22 = (bf16[384,512]{1,0:T(8,128)(2,1)S(1)}, bf16[384,512]{1,0:T(8,128)(2,1)S(1)}, u32[]{:S(2)}, u32[]{:S(2)}) collective-permute-start(bf16[384,512]{1,0:T(8,128)(2,1)S(1)} %newton_schulz.3.rest_16_), channel_id=1, source_target_pairs={{0,2},{1,5},{2,0},{3,7},{4,6},{5,1},{6,4},{7,3},{8,10},{9,13},{10,... | collective-permute-start | bytes 1179656 | tf_op jit(solution)/shard_map/ppermute | solution.py:354
  128.3 10.3 %collective-permute-start.21 = (bf16[384,512]{1,0:T(8,128)(2,1)S(1)}, bf16[384,512]{1,0:T(8,128)(2,1)S(1)}, u32[]{:S(2)}, u32[]{:S(2)}) collective-permute-start(bf16[384,512]{1,0:T(8,128)(2,1)S(1)} %newton_schulz.3.rest_16_), channel_id=1, source_target_pairs={{0,4},{1,3},{2,6},{3,1},{4,0},{5,7},{6,2},{7,5},{8,12},{9,11},{10,... | collective-permute-start | bytes 1179656 | tf_op jit(solution)/shard_map/ppermute | solution.py:354
  128.8 10.3 %collective-permute-start.18 = (bf16[384,512]{1,0:T(8,128)(2,1)S(1)}, bf16[384,512]{1,0:T(8,128)(2,1)S(1)}, u32[]{:S(2)}, u32[]{:S(2)}) collective-permute-start(bf16[384,512]{1,0:T(8,128)(2,1)S(1)} %collective-permute-done.14.rest_10_), channel_id=1, source_target_pairs={{0,1},{1,0},{2,3},{3,2},{4,5},{5,4},{6,7},{7,6},{8,9},{9,8},{10,11... | collective-permute-start | bytes 1179656 | tf_op jit(solution)/shard_map/ppermute | solution.py:354
  135.0 12.2 %collective-permute-start.15 = (bf16[384,512]{1,0:T(8,128)(2,1)S(1)}, bf16[384,512]{1,0:T(8,128)(2,1)S(1)}, u32[]{:S(2)}, u32[]{:S(2)}) collective-permute-start(bf16[384,512]{1,0:T(8,128)(2,1)S(1)} %collective-permute-done.13.rest_9_), channel_id=1, source_target_pairs={{0,2},{1,5},{2,0},{3,7},{4,6},{5,1},{6,4},{7,3},{8,10},{9,13},{10,... | collective-permute-start | bytes 1179656 | tf_op jit(solution)/shard_map/ppermute | solution.py:354
  138.6 8.6 %collective-permute-start.11 = (bf16[384,512]{1,0:T(8,128)(2,1)S(1)}, bf16[384,512]{1,0:T(8,128)(2,1)S(1)}, u32[]{:S(2)}, u32[]{:S(2)}) collective-permute-start(bf16[384,512]{1,0:T(8,128)(2,1)S(1)} %collective-permute-done.7.rest_3_), channel_id=1, source_target_pairs={{0,1},{1,0},{2,3},{3,2},{4,5},{5,4},{6,7},{7,6},{8,9},{9,8},{10,11... | collective-permute-start | bytes 1179656 | tf_op jit(solution)/shard_map/ppermute | solution.py:354
  138.6 9.1 %collective-permute-start.32 = (bf16[384,512]{1,0:T(8,128)(2,1)S(1)}, bf16[384,512]{1,0:T(8,128)(2,1)S(1)}, u32[]{:S(2)}, u32[]{:S(2)}) collective-permute-start(bf16[384,512]{1,0:T(8,128)(2,1)S(1)} %collective-permute-done.28.rest_24_), channel_id=1, source_target_pairs={{0,1},{1,0},{2,3},{3,2},{4,5},{5,4},{6,7},{7,6},{8,9},{9,8},{10,11... | collective-permute-start | bytes 1179656 | tf_op jit(solution)/shard_map/ppermute | solution.py:354
  139.1 11.8 %collective-permute-start.29 = (bf16[384,512]{1,0:T(8,128)(2,1)S(1)}, bf16[384,512]{1,0:T(8,128)(2,1)S(1)}, u32[]{:S(2)}, u32[]{:S(2)}) collective-permute-start(bf16[384,512]{1,0:T(8,128)(2,1)S(1)} %collective-permute-done.28.rest_24_), channel_id=1, source_target_pairs={{0,4},{1,3},{2,6},{3,1},{4,0},{5,7},{6,2},{7,5},{8,12},{9,11},{10,... | collective-permute-start | bytes 1179656 | tf_op jit(solution)/shard_map/ppermute | solution.py:354
  140.4 12.4 %collective-permute-start.30 = (bf16[384,512]{1,0:T(8,128)(2,1)S(1)}, bf16[384,512]{1,0:T(8,128)(2,1)S(1)}, u32[]{:S(2)}, u32[]{:S(2)}) collective-permute-start(bf16[384,512]{1,0:T(8,128)(2,1)S(1)} %collective-permute-done.28.rest_24_), channel_id=1, source_target_pairs={{0,2},{1,5},{2,0},{3,7},{4,6},{5,1},{6,4},{7,3},{8,10},{9,13},{10,... | collective-permute-start | bytes 1179656 | tf_op jit(solution)/shard_map/ppermute | solution.py:354
  147.7 9.3 %collective-permute-start.23 = (bf16[384,512]{1,0:T(8,128)(2,1)S(1)}, bf16[384,512]{1,0:T(8,128)(2,1)S(1)}, u32[]{:S(2)}, u32[]{:S(2)}) collective-permute-start(bf16[384,512]{1,0:T(8,128)(2,1)S(1)} %collective-permute-done.21.rest_17_), channel_id=1, source_target_pairs={{0,2},{1,5},{2,0},{3,7},{4,6},{5,1},{6,4},{7,3},{8,10},{9,13},{10,... | collective-permute-start | bytes 1179656 | tf_op jit(solution)/shard_map/ppermute | solution.py:354
  151.0 10.2 %collective-permute-start.31 = (bf16[384,512]{1,0:T(8,128)(2,1)S(1)}, bf16[384,512]{1,0:T(8,128)(2,1)S(1)}, u32[]{:S(2)}, u32[]{:S(2)}) collective-permute-start(bf16[384,512]{1,0:T(8,128)(2,1)S(1)} %collective-permute-done.29.rest_25_), channel_id=1, source_target_pairs={{0,2},{1,5},{2,0},{3,7},{4,6},{5,1},{6,4},{7,3},{8,10},{9,13},{10,... | collective-permute-start | bytes 1179656 | tf_op jit(solution)/shard_map/ppermute | solution.py:354
  (16 other events, 74.8 us)

commit v3 on v2

--- a/solution.py
+++ b/solution.py
@@ -32,7 +32,6 @@
 NZ = 4
 PLANE = 8
 DEVICES = NZ * PLANE
-SENDS = 2
 
 
 def newton_batch(xmat, width):
@@ -124,27 +123,32 @@
 
 def pack_kernel(size, k_ref, v_ref, rate_ref, *rest):
     out_ref = rest[-1]
+    step = pl.program_id(0)
+    lanes = lax.broadcasted_iota(jnp.int32, (rate_ref.shape[1], PLANE), 1)
     rates = jnp.transpose(rate_ref[...])
-    for head in range(PLANE):
-        cols = slice(head * size, (head + 1) * size)
-        out_ref[head, 0] = k_ref[:, cols]
-        out_ref[head, 1] = (rates[:, head : head + 1] * v_ref[:, cols].astype(F32)).astype(BF)
+    for i in range(out_ref.shape[0]):
+        cols = slice(i * size, (i + 1) * size)
+        here = lanes == step * out_ref.shape[0] + i
+        rate = jnp.sum(jnp.where(here, rates, 0.0), axis=1, keepdims=True)
+        out_ref[i, 0] = k_ref[:, cols]
+        out_ref[i, 1] = (rate * v_ref[:, cols].astype(F32)).astype(BF)
 
 
 def pack_tokens(keys, values, rates, group, size, *follows):
     tokens = keys.shape[0]
-    cols = PLANE * size
+    each = 4
+    steps = PLANE // each
     return pl.pallas_call(
         functools.partial(pack_kernel, size),
-        grid=(1,),
+        grid=(steps,),
         out_shape=jax.ShapeDtypeStruct((PLANE, 2, tokens, size), BF),
         in_specs=[
-            pl.BlockSpec((tokens, cols), lambda i: (0, group)),
-            pl.BlockSpec((tokens, cols), lambda i: (0, group)),
+            pl.BlockSpec((tokens, each * size), lambda i: (0, group * steps + i)),
+            pl.BlockSpec((tokens, each * size), lambda i: (0, group * steps + i)),
             pl.BlockSpec((PLANE, tokens), lambda i: (group, 0)),
         ]
         + [ANY] * len(follows),
-        out_specs=pl.BlockSpec((PLANE, 2, tokens, size), lambda i: (0, 0, 0, 0)),
+        out_specs=pl.BlockSpec((each, 2, tokens, size), lambda i: (i, 0, 0, 0)),
         compiler_params=pltpu.CompilerParams(vmem_limit_bytes=VMEM_BYTES),
         cost_estimate=COST_PACK,
         name="pack_tokens",
@@ -152,7 +156,7 @@
 
 
 def grads_kernel(group, scale_one, scale_two, where_ref, wg_ref, wu_ref, wd_ref, blocks, *rest):
-    keep, *send = rest[-9 - SENDS : -8]
+    keep, *send = rest[-12:-8]
     held, total, final, wg_held, wu_held, wd_held, in_sem, sem = rest[-8:]
     head = group * PLANE + where_ref[0]
     weights = [
@@ -161,8 +165,10 @@
     ]
     for copy in weights:
         copy.start()
+    tokens = held.shape[1] // PLANE
     copies = [
-        pltpu.make_async_copy(blocks.at[b], held.at[b], in_sem.at[b]) for b in range(PLANE)
+        pltpu.make_async_copy(blocks.at[b], held.at[:, pl.ds(b * tokens, tokens)], in_sem.at[b])
+        for b in range(PLANE)
     ]
     for copy in copies:
         copy.start()
@@ -170,9 +176,11 @@
         copy.wait()
     wg, wu = wg_held[...], wu_held[...]
     wdt = jnp.transpose(wd_held[...])
-    for b in range(PLANE):
+    for b in range(0, PLANE, 2):
         copies[b].wait()
-        k, vr = held[b, 0], held[b, 1]
+        copies[b + 1].wait()
+        rows = slice(b * tokens, (b + 2) * tokens)
+        k, vr = held[0, rows], held[1, rows]
         gk = scale_one * dot(k, wg)
         uk = dot(k, wu)
         dh = dot(vr, wdt)
@@ -192,14 +200,19 @@
     final[0] = (both * scale_one * total[0]).astype(BF)
     final[1] = (both * total[1]).astype(BF)
     final[2] = (both * total[2]).astype(BF)
-    odd = where_ref[4]
-    pairs = [(final.at[odd], keep.at[0]), (final.at[2], keep.at[1])]
-    each = SENDS // 2
-    rows = final.shape[1] // each
-    for i in range(each):
-        pairs.append((final.at[1 - odd, pl.ds(i * rows, rows)], send[i]))
-        pairs.append((final.at[2, pl.ds(i * rows, rows)], send[each + i]))
-    run_copies(pairs, sem)
+    core, half = where_ref[4], final.shape[1] // 2
+    mine = pl.ds(pl.multiple_of(core * half, half), half)
+    others = pl.ds(pl.multiple_of((1 - core) * half, half), half)
+    run_copies(
+        [
+            (final.at[1 - core, pl.ds(0, half)], send[0]),
+            (final.at[1 - core, pl.ds(half, half)], send[1]),
+            (final.at[2, others], send[2]),
+            (final.at[core], keep.at[pl.ds(0, 2 * half)]),
+            (final.at[2, mine], keep.at[pl.ds(2 * half, half)]),
+        ],
+        sem,
+    )
 
 
 def head_grads(where, blocks, w_gate, w_up, w_down, group, *follows):
@@ -207,19 +220,19 @@
     tokens = blocks.shape[2]
     return pl.pallas_call(
         functools.partial(grads_kernel, group, size**-0.5, hidden**-0.5),
-        out_shape=[jax.ShapeDtypeStruct((2, size, hidden), BF)]
-        + [jax.ShapeDtypeStruct((2 * size // SENDS, hidden), BF)] * SENDS,
+        out_shape=[jax.ShapeDtypeStruct((size + size // 2, hidden), BF)]
+        + [jax.ShapeDtypeStruct((size // 2, hidden), BF)] * 3,
         in_specs=[SMEM] + [HBM] * 3 + [ANY] * (1 + len(follows)),
-        out_specs=[ANY] * (1 + SENDS),
+        out_specs=[ANY] * 4,
         scratch_shapes=[
-            pltpu.VMEM((PLANE, 2, tokens, size), BF),
+            pltpu.VMEM((2, PLANE * tokens, size), BF),
             pltpu.VMEM((3, size, hidden), F32),
             pltpu.VMEM((3, size, hidden), BF),
             pltpu.VMEM((size, hidden), BF),
             pltpu.VMEM((size, hidden), BF),
             pltpu.VMEM((hidden, size), BF),
             pltpu.SemaphoreType.DMA((PLANE + 3,)),
-            pltpu.SemaphoreType.DMA((2 + SENDS,)),
+            pltpu.SemaphoreType.DMA((5,)),
         ],
         compiler_params=pltpu.CompilerParams(vmem_limit_bytes=48 * 1024 * 1024),
         cost_estimate=COST_GRADS,
@@ -227,34 +240,44 @@
     )(where, w_gate, w_up, w_down, blocks, *follows)
 
 
-def combine_kernel(a_ref, *rest):
-    parts, out_ref = rest[:SENDS], rest[-1]
-    rows = parts[0].shape[0]
-    each = out_ref.shape[1] // rows
-    for i, part in enumerate(parts):
-        at = (i // each, slice(i % each * rows, (i % each + 1) * rows))
-        out_ref[at] = (a_ref[at].astype(F32) + part[...].astype(F32)).astype(BF)
-
-
-def combine(a, parts, *follows):
+def combine_kernel(keep_ref, a_ref, b_ref, c_ref, *rest):
+    out_ref, part_ref = rest[-2:]
+    rows = part_ref.shape[0]
+    for i, ref in enumerate((a_ref, b_ref, c_ref)):
+        at = slice(i * rows, (i + 1) * rows)
+        total = (keep_ref[at].astype(F32) + ref[...].astype(F32)).astype(BF)
+        out_ref[at] = total
+    part_ref[...] = total
+
+
+def combine(keep, parts, *follows):
     return pl.pallas_call(
         combine_kernel,
-        out_shape=jax.ShapeDtypeStruct(a.shape, BF),
-        in_specs=[VMEM] * (1 + SENDS) + [ANY] * len(follows),
-        out_specs=VMEM,
+        out_shape=[
+            jax.ShapeDtypeStruct(keep.shape, BF),
+            jax.ShapeDtypeStruct(parts[-1].shape, BF),
+        ],
+        in_specs=[VMEM] * 4 + [ANY] * len(follows),
+        out_specs=[VMEM] * 2,
         compiler_params=pltpu.CompilerParams(vmem_limit_bytes=8 * 1024 * 1024),
         cost_estimate=COST_ADD,
         name="add_partials",
-    )(a, *parts, *follows)
-
-
-def newton_kernel(where_ref, mine_ref, other_ref, *rest):
-    out_ref, held = rest[-2:]
+    )(keep, *parts, *follows)
+
+
+def newton_kernel(where_ref, *rest):
+    mine_ref, other_ref, mine_sib, other_sib = rest[:4]
+    out_ref, total, held = rest[-3:]
     size, width = held.shape
     half = size // 2
+    core = where_ref[4]
+    mine = pl.ds(pl.multiple_of(core * half, half), half)
+    others = pl.ds(pl.multiple_of((1 - core) * half, half), half)
+    total[mine, :] = mine_ref[size:].astype(F32) + other_ref[size:].astype(F32)
+    total[others, :] = mine_sib[...].astype(F32) + other_sib[...].astype(F32)
     mats = []
-    for i in range(2):
-        grad = mine_ref[i].astype(F32) + other_ref[i].astype(F32)
+    main = mine_ref[:size].astype(F32) + other_ref[:size].astype(F32)
+    for grad in (main, total[...]):
         norm = jnp.sqrt(jnp.sum(grad * grad))
         mats.append((grad / (norm + 1e-07)).astype(BF))
     for step in range(NS_STEPS):
@@ -268,22 +291,22 @@
         mats = [n.astype(BF) for n in nexts]
     out_ref[:size] = mats[0]
     held[...] = mats[1]
-    odd = where_ref[4]
-    out_ref[size:] = held[pl.ds(pl.multiple_of(odd * half, half), half), :]
-
-
-def newton(where, mine, other, *follows):
-    _, size, hidden = mine.shape
+    out_ref[size:] = held[mine, :]
+
+
+def newton(where, parts, *follows):
+    rows, hidden = parts[0].shape
+    size = rows * 2 // 3
     return pl.pallas_call(
         newton_kernel,
-        out_shape=jax.ShapeDtypeStruct((size + size // 2, hidden), BF),
-        in_specs=[SMEM] + [VMEM] * 2 + [ANY] * len(follows),
+        out_shape=jax.ShapeDtypeStruct((rows, hidden), BF),
+        in_specs=[SMEM] + [VMEM] * len(parts) + [ANY] * len(follows),
         out_specs=VMEM,
-        scratch_shapes=[pltpu.VMEM((size, hidden), BF)],
+        scratch_shapes=[pltpu.VMEM((size, hidden), F32), pltpu.VMEM((size, hidden), BF)],
         compiler_params=pltpu.CompilerParams(vmem_limit_bytes=20 * 1024 * 1024),
         cost_estimate=COST_NEWTON,
         name="newton_schulz",
-    )(where, mine, other, *follows)
+    )(where, *parts, *follows)
 
 
 def run_copies(pairs, sem):
@@ -294,15 +317,15 @@
         copy.wait()
 
 
-def place_kernel(count, size, where_ref, *rest):
-    blocks, (gate, up, down, sem) = rest[:-4], rest[-4:]
+def place_kernel(group, which, size, where_ref, *rest):
+    blocks, (gate, up, down, sem) = rest[: len(which)], rest[-4:]
     z, y, x, core = (where_ref[i] for i in range(1, 5))
     half = size // 2
 
     def put(parity):
         pairs = []
-        for i, block in enumerate(blocks):
-            group, flip, other, kind = i // 16, i // 8 % 2, i // 4 % 2, i % 4
+        for i, block in zip(which, blocks):
+            flip, other, kind = i // 8, i // 4 % 2, i % 4
             side, c = (1 - parity, 1 - core) if other else (parity, core)
             at = ((y, x), (y ^ (1 - c), x ^ c), (y ^ c, x ^ (1 - c)), (1 - y, 1 - x))[kind]
             head = group * PLANE + (lax.rem(z, 2) ^ flip) * 4 + at[0] * 2 + at[1]
@@ -318,17 +341,19 @@
             put(parity)
 
 
-def place(where, blocks, shape):
+def place(where, blocks, steps, shape, group, which=tuple(range(16))):
     count = len(blocks)
     return pl.pallas_call(
-        functools.partial(place_kernel, count, shape[1]),
+        functools.partial(place_kernel, group, which, shape[1]),
         out_shape=[jax.ShapeDtypeStruct(shape, BF)] * 3,
-        in_specs=[SMEM] + [ANY] * count,
+        in_specs=[SMEM] + [VMEM] * count + [ANY] * len(steps),
         out_specs=[ANY] * 3,
         scratch_shapes=[pltpu.SemaphoreType.DMA((2 * count,))],
-        compiler_params=pltpu.CompilerParams(vmem_limit_bytes=2 * 1024 * 1024),
+        input_output_aliases={1 + count + i: i for i in range(len(steps))},
+        compiler_params=pltpu.CompilerParams(vmem_limit_bytes=16 * 1024 * 1024),
+        cost_estimate=COST_PLACE,
         name="place_steps",
-    )(where, *blocks)
+    )(where, *blocks, *steps)
 
 
 def permutation(target):
@@ -375,25 +400,42 @@
         for block in packed
     ]
 
-    pairs, others, follow = [], [], ()
-    for group in range(groups):
+    def summed(group, waits, *follow):
         keep, *send = head_grads(where, received[group], w_gate, w_up, w_down, group, *follow)
-        pairs.append(combine(keep, [move(block, CORE_MOVE) for block in send], *others[-1:]))
-        others.append(move(pairs[-1], Z_MOVES[2]))
-        follow = pairs[-1:]
-    blocks = []
-    for group in range(groups):
-        follow = pairs[group + 1 : group + 2]
-        block = newton(where, pairs[group], others[group], *follow)
-        for flip in range(2):
-            if flip:
-                block = move(block, Z_MOVES[1])
-            one = move(block, FIRST_MOVE)
-            two = move(block, SECOND_MOVE)
-            three = move(one, SECOND_MOVE)
-            mine = [block, one, two, three]
-            blocks += mine + [move(b, CORE_MOVE) for b in mine]
-    steps = place(where, blocks, w_gate.shape)
+        return combine(keep, [move(block, CORE_MOVE) for block in send], *waits)
+
+    def round_two(one, two, far):
+        return move(one, Z_MOVES[1]), move(two, FIRST_MOVE), move(far, SECOND_MOVE)
+
+    def with_sibling(*gathered):
+        return [*gathered] + [move(block, CORE_MOVE) for block in gathered]
+
+    mine, part = summed(0, ())
+    other = move(mine, Z_MOVES[2])
+    parts = (mine, other, move(part, CORE_MOVE), move(other[size:], CORE_MOVE))
+    mine_b, part_b = summed(1, (other,), mine)
+    other_b = move(mine_b, Z_MOVES[2])
+    near = newton(where, parts, mine_b)
+    one, two, far = (move(near, to) for to in (FIRST_MOVE, SECOND_MOVE, Z_MOVES[1]))
+    one, two, far, other_b = lax.optimization_barrier((one, two, far, other_b))
+    far_one, three, far_two = round_two(one, two, far)
+    parts = (mine_b, other_b, move(part_b, CORE_MOVE), move(other_b[size:], CORE_MOVE))
+    near_b = newton(where, parts)
+    near_b, three, far_two = lax.optimization_barrier((near_b, three, far_two))
+    far_three = move(far_one, SECOND_MOVE)
+    one_b, two_b, far_b = (move(near_b, to) for to in (FIRST_MOVE, SECOND_MOVE, Z_MOVES[1]))
+    blocks = with_sibling(near, one, two, three)
+    one, two, far_b, far_three = lax.optimization_barrier((one_b, two_b, far_b, far_three))
+    blocks += with_sibling(far, far_one, far_two, far_three)
+    steps = place(where, blocks, (), w_gate.shape, 0)
+    far_one, three, far_two = round_two(one, two, far_b)
+    far_one, three, far_two = lax.optimization_barrier((far_one, three, far_two))
+    far_three = move(far_one, SECOND_MOVE)
+    blocks = with_sibling(near_b, one, two, three) + with_sibling(far_b, far_one, far_two)
+    which = (*range(11), 12, 13, 14)
+    steps = place(where, blocks, steps, w_gate.shape, 1, which)
+    far_three, *steps = lax.optimization_barrier((far_three, *steps))
+    steps = place(where, with_sibling(far_three), steps, w_gate.shape, 1, (11, 15))
     return (applied, *steps)
 
 
@@ -417,7 +459,7 @@
 
     def per_device(*args):
         heads = args[4].shape[0]
-        fast = sizes["seq"] == DEVICES and heads % PLANE == 0
+        fast = sizes["seq"] == DEVICES and heads == 2 * PLANE
         return (per_device_fast if fast else per_device_plain)(*args)
 
     return jax.shard_map(

time: 169 us -> 165 us (0.976)
  starting transfers between devices: 42.8 us -> 37 us
    ppermute x36 -> x42, starting transfers between devices: 31.6 us -> 25.7 us  [move(): return lax.ppermute(array, 'seq', pairs)]
    ppermute x36 -> x42, waiting for transfers between devices: 41.3 us -> 43.8 us  [move(): return lax.ppermute(array, 'seq', pairs)]
    pallas_call x7 -> x9, Pallas kernels: 20.3 us -> 22 us  [the longest x3 8.1 us: place(): pl.pallas_call(functools.partial(place_kernel, group, which, shape[1]), o...]
  transfers between devices with their start and end apart: 38 -> 44, of which waited for: 15 -> 25; matrix products, arithmetic and copies ran while one was open for 0% -> 0% of each run, Pallas kernels for 20% -> 26%
where the time goes in v3:
time: 165 us; the launch traced here: 164 us
  waiting for transfers between devices  76.6 us (46%)
  Pallas kernels  46.9 us (28%)
  starting transfers between devices  37 us (22%)
  local copies, waits for them, and re-layouts  3.01 us (2%)
    ppermute x42, waiting for transfers between devices, move(): return lax.ppermute(array, 'seq', pairs)  43.8 us
    all_to_all x2, waiting for transfers between devices, per_device_fast(): lax.all_to_all(block, 'seq', 0, 0, axis_index_groups=CUBES, tiled=True)  32.8 us
    ppermute x42, starting transfers between devices, move(): return lax.ppermute(array, 'seq', pairs)  25.7 us
    pallas_call x2, Pallas kernels, head_grads(): pl.pallas_call(functools.partial(grads_kernel, group, size ** (-0.5), hid...  15.7 us
    all_to_all x2, starting transfers between devices, per_device_fast(): lax.all_to_all(block, 'seq', 0, 0, axis_index_groups=CUBES, tiled=True)  11.3 us
    pallas_call x1, Pallas kernels, apply_queries(): pl.pallas_call(functools.partial(applied_kernel, size ** (-0.5), hidden *...  9.19 us
    pallas_call x3, Pallas kernels, place(): pl.pallas_call(functools.partial(place_kernel, group, which, shape[1]), o...  8.1 us
    pallas_call x2, Pallas kernels, newton(): pl.pallas_call(newton_kernel, out_shape=jax.ShapeDtypeStruct((rows, hidde...  7.84 us
  transfers between devices with their start and end apart: 44, of which 25 were waited for; matrix products, arithmetic and copies ran while one was open for 0% of the time, Pallas kernels for 26%

profile of v3, /device:TPU:0, one launch (start us, length us, event | category | flops | bytes accessed | tf_op | source)
XLA Modules:
  0.0 164.5 jit_solution(5626048149438782527)
XLA Ops:
  0.6 2.9 %pack_tokens.3 = bf16[8,2,256,256]{3,2,1,0:T(8,128)(2,1)} custom-call(bf16[256,4096]{1,0:T(8,128)(2,1)} %k_ref.3, bf16[256,4096]{1,0:T(8,128)(2,1)} %v_ref.3, f32[16,256]{1,0:T(8,128)} %rate_ref.3), custom_call_target="tpu_custom_call" | custom-call | flops 1 | bytes 1 | tf_op jit(solution)/shard_map/pack_tokens/pallas_call | solution.py:141
  3.6 6.2 %all-to-all-start.1 = ((bf16[8,2,256,256]{3,2,1,0:T(8,128)(2,1)}), bf16[8,2,256,256]{3,2,1,0:T(8,128)(2,1)S(1)}, u32[]{:S(2)}, u32[]{:S(2)}) async-start(bf16[8,2,256,256]{3,2,1,0:T(8,128)(2,1)} %pack_tokens.3), calls=%async_computation.1 | async-start | bytes 4194304 | tf_op jit(solution)/shard_map/all_to_all | solution.py:399
  9.7 9.2 %apply_queries.1.rest_0_ = bf16[256,4096]{1,0:T(8,128)(2,1)} custom-call(bf16[256,4096]{1,0:T(8,128)(2,1)} %q_ref.1, bf16[16,256,512]{2,1,0:T(8,128)(2,1)} %wg_ref.5, bf16[16,256,512]{2,1,0:T(8,128)(2,1)} %wu_ref.5, bf16[16,512,256]{2,1,0:T(8,128)(2,1)} %wd_ref.5), custom_call_target="tpu_custom_call" | custom-call | flops 1 | bytes 1 | tf_op jit(solution)/shard_map/apply_queries/pallas_call | solution.py:107
  18.9 2.9 %pack_tokens.2 = bf16[8,2,256,256]{3,2,1,0:T(8,128)(2,1)} custom-call(bf16[256,4096]{1,0:T(8,128)(2,1)} %k_ref.3, bf16[256,4096]{1,0:T(8,128)(2,1)} %v_ref.3, f32[16,256]{1,0:T(8,128)} %rate_ref.3, bf16[256,4096]{1,0:T(8,128)(2,1)} %apply_queries.1.rest_0_), custom_call_target="tpu_custom_call" | custom-call | flops 1 | bytes 1 | tf_op jit(solution)/shard_map/pack_tokens/pallas_call | solution.py:141
  21.8 13.9 %all-to-all-done.1.blocks = bf16[8,2,256,256]{3,2,1,0:T(8,128)(2,1)S(1)} async-done(((bf16[8,2,256,256]{3,2,1,0:T(8,128)(2,1)}), bf16[8,2,256,256]{3,2,1,0:T(8,128)(2,1)S(1)}, u32[]{:S(2)}, u32[]{:S(2)}) %all-to-all-start.1) | async-done | bytes 2097184 | tf_op jit(solution)/shard_map/all_to_all | solution.py:399
  37.0 5.1 %all-to-all-start = ((bf16[8,2,256,256]{3,2,1,0:T(8,128)(2,1)}), bf16[8,2,256,256]{3,2,1,0:T(8,128)(2,1)S(1)}, u32[]{:S(2)}, u32[]{:S(2)}) async-start(bf16[8,2,256,256]{3,2,1,0:T(8,128)(2,1)} %pack_tokens.2), calls=%async_computation | async-start | bytes 4194304 | tf_op jit(solution)/shard_map/all_to_all | solution.py:399
  43.8 7.8 %head_grads.2 = (bf16[384,512]{1,0:T(8,128)(2,1)S(1)}, bf16[128,512]{1,0:T(8,128)(2,1)S(1)}, bf16[128,512]{1,0:T(8,128)(2,1)S(1)}, bf16[128,512]{1,0:T(8,128)(2,1)S(1)}) custom-call(s32[5]{0:T(128)S(1)} %stack.23.where_ref, bf16[16,256,512]{2,1,0:T(8,128)(2,1)} %wg_ref.5, bf16[16,256,512]{2,1,0:T(8,128)(2,1)} %wu_ref.5, bf16[16,512,256]{2,1,0:T(8,128)(2,1)} %wd_ref.5, ...), custom_call_target="tpu_custom_call" | custom-call | flops 1 | bytes 1 | tf_op jit(solution)/shard_map/head_grads/pallas_call | solution.py:221
  53.6 2.6 %collective-permute-start.6 = (bf16[384,512]{1,0:T(8,128)(2,1)S(1)}, bf16[384,512]{1,0:T(8,128)(2,1)S(1)}, u32[]{:S(2)}, u32[]{:S(2)}) collective-permute-start(bf16[384,512]{1,0:T(8,128)(2,1)S(1)} %get-tuple-element.47.rest_0_), channel_id=1, source_target_pairs={{0,16},{1,17},{2,18},{3,19},{4,20},{5,21},{6,22},{7,23},{8,24},{9,... | collective-permute-start | bytes 1179656 | tf_op jit(solution)/shard_map/ppermute | solution.py:379
  56.2 18.9 %all-to-all-done.blocks = bf16[8,2,256,256]{3,2,1,0:T(8,128)(2,1)S(1)} async-done(((bf16[8,2,256,256]{3,2,1,0:T(8,128)(2,1)}), bf16[8,2,256,256]{3,2,1,0:T(8,128)(2,1)S(1)}, u32[]{:S(2)}, u32[]{:S(2)}) %all-to-all-start) | async-done | bytes 2097184 | tf_op jit(solution)/shard_map/all_to_all | solution.py:399
  75.1 8.0 %head_grads.3 = (bf16[384,512]{1,0:T(8,128)(2,1)S(1)}, bf16[128,512]{1,0:T(8,128)(2,1)S(1)}, bf16[128,512]{1,0:T(8,128)(2,1)S(1)}, bf16[128,512]{1,0:T(8,128)(2,1)S(1)}) custom-call(s32[5]{0:T(128)S(1)} %stack.23.where_ref, bf16[16,256,512]{2,1,0:T(8,128)(2,1)} %wg_ref.5, bf16[16,256,512]{2,1,0:T(8,128)(2,1)} %wu_ref.5, bf16[16,512,256]{2,1,0:T(8,128)(2,1)} %wd_ref.5, ...), custom_call_target="tpu_custom_call" | custom-call | flops 1 | bytes 1 | tf_op jit(solution)/shard_map/head_grads/pallas_call | solution.py:221
  85.6 3.9 %newton_schulz.2.rest_0_ = bf16[384,512]{1,0:T(8,128)(2,1)S(1)} custom-call(s32[5]{0:T(128)S(1)} %stack.23.where_ref, bf16[384,512]{1,0:T(8,128)(2,1)S(1)} %get-tuple-element.47.rest_0_, bf16[384,512]{1,0:T(8,128)(2,1)S(1)} %collective-permute-done.6.rest_0_.rest_1_, bf16[128,512]{1,0:T(8,128)(2,1)S(1)} %collective-permute-done.7.rest_2_, ...), custom_call_target="tpu_custom_call" | custom-call | flops 1 | bytes 1 | tf_op jit(solution)/shard_map/newton_schulz/pallas_call | solution.py:300
  89.5 3.7 %collective-permute-start.10 = (bf16[384,512]{1,0:T(8,128)(2,1)S(1)}, bf16[384,512]{1,0:T(8,128)(2,1)S(1)}, u32[]{:S(2)}, u32[]{:S(2)}) collective-permute-start(bf16[384,512]{1,0:T(8,128)(2,1)S(1)} %newton_schulz.2.rest_0_), channel_id=1, source_target_pairs={{0,2},{1,5},{2,0},{3,7},{4,6},{5,1},{6,4},{7,3},{8,10},{9,13},{10,... | collective-permute-start | bytes 1179656 | tf_op jit(solution)/shard_map/ppermute | solution.py:379
  93.2 2.4 %collective-permute-start.11 = (bf16[384,512]{1,0:T(8,128)(2,1)S(1)}, bf16[384,512]{1,0:T(8,128)(2,1)S(1)}, u32[]{:S(2)}, u32[]{:S(2)}) collective-permute-start(bf16[384,512]{1,0:T(8,128)(2,1)S(1)} %newton_schulz.2.rest_0_), channel_id=1, source_target_pairs={{0,8},{1,9},{2,10},{3,11},{4,12},{5,13},{6,14},{7,15},{8,0},{9,1},... | collective-permute-start | bytes 1179656 | tf_op jit(solution)/shard_map/ppermute | solution.py:379
  97.1 8.5 %collective-permute-done.12.rest_1_ = bf16[384,512]{1,0:T(8,128)(2,1)S(1)} collective-permute-done((bf16[384,512]{1,0:T(8,128)(2,1)S(1)}, bf16[384,512]{1,0:T(8,128)(2,1)S(1)}, u32[]{:S(2)}, u32[]{:S(2)}) %collective-permute-start.12) | collective-permute-done | bytes 393248 | tf_op jit(solution)/shard_map/ppermute | solution.py:379
  105.6 4.8 %collective-permute-done.11.rest_8_ = bf16[384,512]{1,0:T(8,128)(2,1)S(1)} collective-permute-done((bf16[384,512]{1,0:T(8,128)(2,1)S(1)}, bf16[384,512]{1,0:T(8,128)(2,1)S(1)}, u32[]{:S(2)}, u32[]{:S(2)}) %collective-permute-start.11) | collective-permute-done | bytes 393248 | tf_op jit(solution)/shard_map/ppermute | solution.py:379
  111.4 3.5 %collective-permute-start.16 = (bf16[384,512]{1,0:T(8,128)(2,1)S(1)}, bf16[384,512]{1,0:T(8,128)(2,1)S(1)}, u32[]{:S(2)}, u32[]{:S(2)}) collective-permute-start(bf16[384,512]{1,0:T(8,128)(2,1)S(1)} %collective-permute-done.11.rest_8_), channel_id=1, source_target_pairs={{0,2},{1,5},{2,0},{3,7},{4,6},{5,1},{6,4},{7,3},{8,10},{9,13},{10,... | collective-permute-start | bytes 1179656 | tf_op jit(solution)/shard_map/ppermute | solution.py:379
  116.5 3.9 %newton_schulz.3.rest_0_ = bf16[384,512]{1,0:T(8,128)(2,1)S(1)} custom-call(s32[5]{0:T(128)S(1)} %stack.23.where_ref, bf16[384,512]{1,0:T(8,128)(2,1)S(1)} %get-tuple-element.52.rest_4_.rest_0_, bf16[384,512]{1,0:T(8,128)(2,1)S(1)} %collective-permute-done.12.rest_1_, bf16[128,512]{1,0:T(8,128)(2,1)S(1)} %collective-permute-done.13.rest_2_, ...), custom_call_target="tpu_custom_call" | custom-call | flops 1 | bytes 1 | tf_op jit(solution)/shard_map/newton_schulz/pallas_call | solution.py:300
  120.4 2.7 %collective-permute-done.16.rest_10_ = bf16[384,512]{1,0:T(8,128)(2,1)S(1)} collective-permute-done((bf16[384,512]{1,0:T(8,128)(2,1)S(1)}, bf16[384,512]{1,0:T(8,128)(2,1)S(1)}, u32[]{:S(2)}, u32[]{:S(2)}) %collective-permute-start.16) | collective-permute-done | bytes 393248 | tf_op jit(solution)/shard_map/ppermute | solution.py:379
  123.8 1.8 %collective-permute-start.18 = (bf16[384,512]{1,0:T(8,128)(2,1)S(1)}, bf16[384,512]{1,0:T(8,128)(2,1)S(1)}, u32[]{:S(2)}, u32[]{:S(2)}) collective-permute-start(bf16[384,512]{1,0:T(8,128)(2,1)S(1)} %newton_schulz.3.rest_0_), channel_id=1, source_target_pairs={{0,2},{1,5},{2,0},{3,7},{4,6},{5,1},{6,4},{7,3},{8,10},{9,13},{10,... | collective-permute-start | bytes 1179656 | tf_op jit(solution)/shard_map/ppermute | solution.py:379
  126.6 8.5 %collective-permute-done.17.rest_1_ = bf16[384,512]{1,0:T(8,128)(2,1)S(1)} collective-permute-done((bf16[384,512]{1,0:T(8,128)(2,1)S(1)}, bf16[384,512]{1,0:T(8,128)(2,1)S(1)}, u32[]{:S(2)}, u32[]{:S(2)}) %collective-permute-start.17) | collective-permute-done | bytes 393248 | tf_op jit(solution)/shard_map/ppermute | solution.py:379
  135.7 2.0 %collective-permute-done.21.rest_11_ = bf16[384,512]{1,0:T(8,128)(2,1)S(1)} collective-permute-done((bf16[384,512]{1,0:T(8,128)(2,1)S(1)}, bf16[384,512]{1,0:T(8,128)(2,1)S(1)}, u32[]{:S(2)}, u32[]{:S(2)}) %collective-permute-start.21) | collective-permute-done | bytes 393248 | tf_op jit(solution)/shard_map/ppermute | solution.py:379
  141.2 9.3 %collective-permute-done.22.rest_9_ = bf16[384,512]{1,0:T(8,128)(2,1)S(1)} collective-permute-done((bf16[384,512]{1,0:T(8,128)(2,1)S(1)}, bf16[384,512]{1,0:T(8,128)(2,1)S(1)}, u32[]{:S(2)}, u32[]{:S(2)}) %collective-permute-start.22) | collective-permute-done | bytes 393248 | tf_op jit(solution)/shard_map/ppermute | solution.py:379
  154.2 3.4 %place_steps.3 = (bf16[16,256,512]{2,1,0:T(8,128)(2,1)}, bf16[16,256,512]{2,1,0:T(8,128)(2,1)}, bf16[16,256,512]{2,1,0:T(8,128)(2,1)}) custom-call(s32[5]{0:T(128)S(1)} %stack.23.where_ref, bf16[384,512]{1,0:T(8,128)(2,1)S(1)} %newton_schulz.2.rest_0_, bf16[384,512]{1,0:T(8,128)(2,1)S(1)} %collective-permute-done.9.rest_1_, ...), custom_call_target="tpu_custom_call" | custom-call | flops 1 | bytes 1 | tf_op jit(solution)/shard_map/place_steps/pallas_call | solution.py:346
  157.7 3.2 %place_steps.4 = (bf16[16,256,512]{2,1,0:T(8,128)(2,1)}, bf16[16,256,512]{2,1,0:T(8,128)(2,1)}, bf16[16,256,512]{2,1,0:T(8,128)(2,1)}) custom-call(s32[5]{0:T(128)S(1)} %stack.23.where_ref, bf16[384,512]{1,0:T(8,128)(2,1)S(1)} %newton_schulz.3.rest_0_, ...), custom_call_target="tpu_custom_call", output_to_operand_aliasing={{0}: (15, {}), {1}: (16, {}), {2}: (17, {})} | custom-call | flops 1 | bytes 1 | tf_op jit(solution)/shard_map/place_steps/pallas_call | solution.py:346
  (83 shorter events, 24.5 us)
Async XLA Ops:
  3.6 32.1 %all-to-all-start.1 = ((bf16[8,2,256,256]{3,2,1,0:T(8,128)(2,1)}), bf16[8,2,256,256]{3,2,1,0:T(8,128)(2,1)S(1)}, u32[]{:S(2)}, u32[]{:S(2)}) async-start(bf16[8,2,256,256]{3,2,1,0:T(8,128)(2,1)} %pack_tokens.3), calls=%async_computation.1 | async-start | bytes 4194304 | tf_op jit(solution)/shard_map/all_to_all | solution.py:399
  37.0 38.1 %all-to-all-start = ((bf16[8,2,256,256]{3,2,1,0:T(8,128)(2,1)}), bf16[8,2,256,256]{3,2,1,0:T(8,128)(2,1)S(1)}, u32[]{:S(2)}, u32[]{:S(2)}) async-start(bf16[8,2,256,256]{3,2,1,0:T(8,128)(2,1)} %pack_tokens.2), calls=%async_computation | async-start | bytes 4194304 | tf_op jit(solution)/shard_map/all_to_all | solution.py:399
  53.6 30.6 %collective-permute-start.6 = (bf16[384,512]{1,0:T(8,128)(2,1)S(1)}, bf16[384,512]{1,0:T(8,128)(2,1)S(1)}, u32[]{:S(2)}, u32[]{:S(2)}) collective-permute-start(bf16[384,512]{1,0:T(8,128)(2,1)S(1)} %get-tuple-element.47.rest_0_), channel_id=1, source_target_pairs={{0,16},{1,17},{2,18},{3,19},{4,20},{5,21},{6,22},{7,23},{8,24},{9,... | collective-permute-start | bytes 1179656 | tf_op jit(solution)/shard_map/ppermute | solution.py:379
  85.1 20.4 %collective-permute-start.12 = (bf16[384,512]{1,0:T(8,128)(2,1)S(1)}, bf16[384,512]{1,0:T(8,128)(2,1)S(1)}, u32[]{:S(2)}, u32[]{:S(2)}) collective-permute-start(bf16[384,512]{1,0:T(8,128)(2,1)S(1)} %get-tuple-element.52.rest_4_.rest_0_), channel_id=1, source_target_pairs={{0,16},{1,17},{2,18},{3,19},{4,20},{5,21},{6,22},{7,23},{8,24},{9,... | collective-permute-start | bytes 1179656 | tf_op jit(solution)/shard_map/ppermute | solution.py:379
  89.5 16.0 %collective-permute-start.10 = (bf16[384,512]{1,0:T(8,128)(2,1)S(1)}, bf16[384,512]{1,0:T(8,128)(2,1)S(1)}, u32[]{:S(2)}, u32[]{:S(2)}) collective-permute-start(bf16[384,512]{1,0:T(8,128)(2,1)S(1)} %newton_schulz.2.rest_0_), channel_id=1, source_target_pairs={{0,2},{1,5},{2,0},{3,7},{4,6},{5,1},{6,4},{7,3},{8,10},{9,13},{10,... | collective-permute-start | bytes 1179656 | tf_op jit(solution)/shard_map/ppermute | solution.py:379
  93.2 17.1 %collective-permute-start.11 = (bf16[384,512]{1,0:T(8,128)(2,1)S(1)}, bf16[384,512]{1,0:T(8,128)(2,1)S(1)}, u32[]{:S(2)}, u32[]{:S(2)}) collective-permute-start(bf16[384,512]{1,0:T(8,128)(2,1)S(1)} %newton_schulz.2.rest_0_), channel_id=1, source_target_pairs={{0,8},{1,9},{2,10},{3,11},{4,12},{5,13},{6,14},{7,15},{8,0},{9,1},... | collective-permute-start | bytes 1179656 | tf_op jit(solution)/shard_map/ppermute | solution.py:379
  95.6 14.7 %collective-permute-start.9 = (bf16[384,512]{1,0:T(8,128)(2,1)S(1)}, bf16[384,512]{1,0:T(8,128)(2,1)S(1)}, u32[]{:S(2)}, u32[]{:S(2)}) collective-permute-start(bf16[384,512]{1,0:T(8,128)(2,1)S(1)} %newton_schulz.2.rest_0_), channel_id=1, source_target_pairs={{0,4},{1,3},{2,6},{3,1},{4,0},{5,7},{6,2},{7,5},{8,12},{9,11},{10,... | collective-permute-start | bytes 1179656 | tf_op jit(solution)/shard_map/ppermute | solution.py:379
  110.3 10.1 %collective-permute-start.15 = (bf16[384,512]{1,0:T(8,128)(2,1)S(1)}, bf16[384,512]{1,0:T(8,128)(2,1)S(1)}, u32[]{:S(2)}, u32[]{:S(2)}) collective-permute-start(bf16[384,512]{1,0:T(8,128)(2,1)S(1)} %collective-permute-done.10.rest_2_), channel_id=1, source_target_pairs={{0,4},{1,3},{2,6},{3,1},{4,0},{5,7},{6,2},{7,5},{8,12},{9,11},{10,... | collective-permute-start | bytes 1179656 | tf_op jit(solution)/shard_map/ppermute | solution.py:379
  111.4 11.7 %collective-permute-start.16 = (bf16[384,512]{1,0:T(8,128)(2,1)S(1)}, bf16[384,512]{1,0:T(8,128)(2,1)S(1)}, u32[]{:S(2)}, u32[]{:S(2)}) collective-permute-start(bf16[384,512]{1,0:T(8,128)(2,1)S(1)} %collective-permute-done.11.rest_8_), channel_id=1, source_target_pairs={{0,2},{1,5},{2,0},{3,7},{4,6},{5,1},{6,4},{7,3},{8,10},{9,13},{10,... | collective-permute-start | bytes 1179656 | tf_op jit(solution)/shard_map/ppermute | solution.py:379
  115.5 11.1 %collective-permute-start.20 = (bf16[384,512]{1,0:T(8,128)(2,1)S(1)}, bf16[384,512]{1,0:T(8,128)(2,1)S(1)}, u32[]{:S(2)}, u32[]{:S(2)}) collective-permute-start(bf16[384,512]{1,0:T(8,128)(2,1)S(1)} %collective-permute-done.9.rest_1_), channel_id=1, source_target_pairs={{0,8},{1,9},{2,10},{3,11},{4,12},{5,13},{6,14},{7,15},{8,0},{9,1},... | collective-permute-start | bytes 1179656 | tf_op jit(solution)/shard_map/ppermute | solution.py:379
  123.1 12.0 %collective-permute-start.17 = (bf16[384,512]{1,0:T(8,128)(2,1)S(1)}, bf16[384,512]{1,0:T(8,128)(2,1)S(1)}, u32[]{:S(2)}, u32[]{:S(2)}) collective-permute-start(bf16[384,512]{1,0:T(8,128)(2,1)S(1)} %newton_schulz.3.rest_0_), channel_id=1, source_target_pairs={{0,4},{1,3},{2,6},{3,1},{4,0},{5,7},{6,2},{7,5},{8,12},{9,11},{10,... | collective-permute-start | bytes 1179656 | tf_op jit(solution)/shard_map/ppermute | solution.py:379
  123.8 11.3 %collective-permute-start.18 = (bf16[384,512]{1,0:T(8,128)(2,1)S(1)}, bf16[384,512]{1,0:T(8,128)(2,1)S(1)}, u32[]{:S(2)}, u32[]{:S(2)}) collective-permute-start(bf16[384,512]{1,0:T(8,128)(2,1)S(1)} %newton_schulz.3.rest_0_), channel_id=1, source_target_pairs={{0,2},{1,5},{2,0},{3,7},{4,6},{5,1},{6,4},{7,3},{8,10},{9,13},{10,... | collective-permute-start | bytes 1179656 | tf_op jit(solution)/shard_map/ppermute | solution.py:379
  125.5 10.1 %collective-permute-start.19 = (bf16[384,512]{1,0:T(8,128)(2,1)S(1)}, bf16[384,512]{1,0:T(8,128)(2,1)S(1)}, u32[]{:S(2)}, u32[]{:S(2)}) collective-permute-start(bf16[384,512]{1,0:T(8,128)(2,1)S(1)} %newton_schulz.3.rest_0_), channel_id=1, source_target_pairs={{0,8},{1,9},{2,10},{3,11},{4,12},{5,13},{6,14},{7,15},{8,0},{9,1},... | collective-permute-start | bytes 1179656 | tf_op jit(solution)/shard_map/ppermute | solution.py:379
  126.6 11.1 %collective-permute-start.21 = (bf16[384,512]{1,0:T(8,128)(2,1)S(1)}, bf16[384,512]{1,0:T(8,128)(2,1)S(1)}, u32[]{:S(2)}, u32[]{:S(2)}) collective-permute-start(bf16[384,512]{1,0:T(8,128)(2,1)S(1)} %collective-permute-done.20.rest_9_), channel_id=1, source_target_pairs={{0,2},{1,5},{2,0},{3,7},{4,6},{5,1},{6,4},{7,3},{8,10},{9,13},{10,... | collective-permute-start | bytes 1179656 | tf_op jit(solution)/shard_map/ppermute | solution.py:379
  126.6 12.4 %collective-permute-start.33 = (bf16[384,512]{1,0:T(8,128)(2,1)S(1)}, bf16[384,512]{1,0:T(8,128)(2,1)S(1)}, u32[]{:S(2)}, u32[]{:S(2)}) collective-permute-start(bf16[384,512]{1,0:T(8,128)(2,1)S(1)} %newton_schulz.2.rest_0_), channel_id=1, source_target_pairs={{0,1},{1,0},{2,3},{3,2},{4,5},{5,4},{6,7},{7,6},{8,9},{9,8},{10,11... | collective-permute-start | bytes 1179656 | tf_op jit(solution)/shard_map/ppermute | solution.py:379
  139.0 11.5 %collective-permute-start.22 = (bf16[384,512]{1,0:T(8,128)(2,1)S(1)}, bf16[384,512]{1,0:T(8,128)(2,1)S(1)}, u32[]{:S(2)}, u32[]{:S(2)}) collective-permute-start(bf16[384,512]{1,0:T(8,128)(2,1)S(1)} %collective-permute-done.17.rest_1_), channel_id=1, source_target_pairs={{0,8},{1,9},{2,10},{3,11},{4,12},{5,13},{6,14},{7,15},{8,0},{9,1},... | collective-permute-start | bytes 1179656 | tf_op jit(solution)/shard_map/ppermute | solution.py:379
  139.1 11.8 %collective-permute-start.23 = (bf16[384,512]{1,0:T(8,128)(2,1)S(1)}, bf16[384,512]{1,0:T(8,128)(2,1)S(1)}, u32[]{:S(2)}, u32[]{:S(2)}) collective-permute-start(bf16[384,512]{1,0:T(8,128)(2,1)S(1)} %collective-permute-done.18.rest_2_), channel_id=1, source_target_pairs={{0,4},{1,3},{2,6},{3,1},{4,0},{5,7},{6,2},{7,5},{8,12},{9,11},{10,... | collective-permute-start | bytes 1179656 | tf_op jit(solution)/shard_map/ppermute | solution.py:379
  139.4 11.6 %collective-permute-start.24 = (bf16[384,512]{1,0:T(8,128)(2,1)S(1)}, bf16[384,512]{1,0:T(8,128)(2,1)S(1)}, u32[]{:S(2)}, u32[]{:S(2)}) collective-permute-start(bf16[384,512]{1,0:T(8,128)(2,1)S(1)} %collective-permute-done.19.rest_8_), channel_id=1, source_target_pairs={{0,2},{1,5},{2,0},{3,7},{4,6},{5,1},{6,4},{7,3},{8,10},{9,13},{10,... | collective-permute-start | bytes 1179656 | tf_op jit(solution)/shard_map/ppermute | solution.py:379
  140.5 10.9 %collective-permute-start.38 = (bf16[384,512]{1,0:T(8,128)(2,1)S(1)}, bf16[384,512]{1,0:T(8,128)(2,1)S(1)}, u32[]{:S(2)}, u32[]{:S(2)}) collective-permute-start(bf16[384,512]{1,0:T(8,128)(2,1)S(1)} %collective-permute-done.20.rest_9_), channel_id=1, source_target_pairs={{0,1},{1,0},{2,3},{3,2},{4,5},{5,4},{6,7},{7,6},{8,9},{9,8},{10,11... | collective-permute-start | bytes 1179656 | tf_op jit(solution)/shard_map/ppermute | solution.py:379
  140.9 10.7 %collective-permute-start.26 = (bf16[384,512]{1,0:T(8,128)(2,1)S(1)}, bf16[384,512]{1,0:T(8,128)(2,1)S(1)}, u32[]{:S(2)}, u32[]{:S(2)}) collective-permute-start(bf16[384,512]{1,0:T(8,128)(2,1)S(1)} %newton_schulz.3.rest_0_), channel_id=1, source_target_pairs={{0,1},{1,0},{2,3},{3,2},{4,5},{5,4},{6,7},{7,6},{8,9},{9,8},{10,11... | collective-permute-start | bytes 1179656 | tf_op jit(solution)/shard_map/ppermute | solution.py:379
  151.4 6.3 %collective-permute-start.30 = (bf16[384,512]{1,0:T(8,128)(2,1)S(1)}, bf16[384,512]{1,0:T(8,128)(2,1)S(1)}, u32[]{:S(2)}, u32[]{:S(2)}) collective-permute-start(bf16[384,512]{1,0:T(8,128)(2,1)S(1)} %collective-permute-done.19.rest_8_), channel_id=1, source_target_pairs={{0,1},{1,0},{2,3},{3,2},{4,5},{5,4},{6,7},{7,6},{8,9},{9,8},{10,11... | collective-permute-start | bytes 1179656 | tf_op jit(solution)/shard_map/ppermute | solution.py:379
  151.5 6.1 %collective-permute-start.29 = (bf16[384,512]{1,0:T(8,128)(2,1)S(1)}, bf16[384,512]{1,0:T(8,128)(2,1)S(1)}, u32[]{:S(2)}, u32[]{:S(2)}) collective-permute-start(bf16[384,512]{1,0:T(8,128)(2,1)S(1)} %collective-permute-done.23.rest_3_), channel_id=1, source_target_pairs={{0,1},{1,0},{2,3},{3,2},{4,5},{5,4},{6,7},{7,6},{8,9},{9,8},{10,11... | collective-permute-start | bytes 1179656 | tf_op jit(solution)/shard_map/ppermute | solution.py:379
  152.2 5.4 %collective-permute-start.31 = (bf16[384,512]{1,0:T(8,128)(2,1)S(1)}, bf16[384,512]{1,0:T(8,128)(2,1)S(1)}, u32[]{:S(2)}, u32[]{:S(2)}) collective-permute-start(bf16[384,512]{1,0:T(8,128)(2,1)S(1)} %collective-permute-done.22.rest_9_), channel_id=1, source_target_pairs={{0,1},{1,0},{2,3},{3,2},{4,5},{5,4},{6,7},{7,6},{8,9},{9,8},{10,11... | collective-permute-start | bytes 1179656 | tf_op jit(solution)/shard_map/ppermute | solution.py:379
  153.3 7.8 %collective-permute-start.25 = (bf16[384,512]{1,0:T(8,128)(2,1)S(1)}, bf16[384,512]{1,0:T(8,128)(2,1)S(1)}, u32[]{:S(2)}, u32[]{:S(2)}) collective-permute-start(bf16[384,512]{1,0:T(8,128)(2,1)S(1)} %collective-permute-done.22.rest_9_), channel_id=1, source_target_pairs={{0,2},{1,5},{2,0},{3,7},{4,6},{5,1},{6,4},{7,3},{8,10},{9,13},{10,... | collective-permute-start | bytes 1179656 | tf_op jit(solution)/shard_map/ppermute | solution.py:379
  (22 other events, 46.1 us)

commit v4 on v3

--- a/solution.py
+++ b/solution.py
@@ -417,15 +417,18 @@
     other_b = move(mine_b, Z_MOVES[2])
     near = newton(where, parts, mine_b)
     one, two, far = (move(near, to) for to in (FIRST_MOVE, SECOND_MOVE, Z_MOVES[1]))
-    one, two, far, other_b = lax.optimization_barrier((one, two, far, other_b))
-    far_one, three, far_two = round_two(one, two, far)
+    one, two, other_b = lax.optimization_barrier((one, two, other_b))
+    far_one, three = move(one, Z_MOVES[1]), move(two, FIRST_MOVE)
     parts = (mine_b, other_b, move(part_b, CORE_MOVE), move(other_b[size:], CORE_MOVE))
     near_b = newton(where, parts)
-    near_b, three, far_two = lax.optimization_barrier((near_b, three, far_two))
+    near_b, three, far = lax.optimization_barrier((near_b, three, far))
+    far_two = move(far, SECOND_MOVE)
     far_three = move(far_one, SECOND_MOVE)
     one_b, two_b, far_b = (move(near_b, to) for to in (FIRST_MOVE, SECOND_MOVE, Z_MOVES[1]))
     blocks = with_sibling(near, one, two, three)
-    one, two, far_b, far_three = lax.optimization_barrier((one_b, two_b, far_b, far_three))
+    one, two, far_b, far_two, far_three = lax.optimization_barrier(
+        (one_b, two_b, far_b, far_two, far_three)
+    )
     blocks += with_sibling(far, far_one, far_two, far_three)
     steps = place(where, blocks, (), w_gate.shape, 0)
     far_one, three, far_two = round_two(one, two, far_b)

time: 165 us -> 161 us (0.976)
  waiting for transfers between devices: 76.6 us -> 70.1 us
  starting transfers between devices: 37 us -> 39.7 us
    ppermute x42, waiting for transfers between devices: 43.8 us -> 37.3 us  [move(): return lax.ppermute(array, 'seq', pairs)]
    ppermute x42, starting transfers between devices: 25.7 us -> 28.4 us  [move(): return lax.ppermute(array, 'seq', pairs)]
  transfers between devices with their start and end apart: 44 -> 44, of which waited for: 25 -> 22; matrix products, arithmetic and copies ran while one was open for 0% -> 0% of each run, Pallas kernels for 26% -> 26%
where the time goes in v4:
time: 161 us
  waiting for transfers between devices  70.1 us (44%)
  Pallas kernels  46.9 us (29%)
  starting transfers between devices  39.7 us (25%)
  local copies, waits for them, and re-layouts  3.01 us (2%)
    ppermute x42, waiting for transfers between devices, move(): return lax.ppermute(array, 'seq', pairs)  37.3 us
    all_to_all x2, waiting for transfers between devices, per_device_fast(): lax.all_to_all(block, 'seq', 0, 0, axis_index_groups=CUBES, tiled=True)  32.8 us
    ppermute x42, starting transfers between devices, move(): return lax.ppermute(array, 'seq', pairs)  28.4 us
    pallas_call x2, Pallas kernels, head_grads(): pl.pallas_call(functools.partial(grads_kernel, group, size ** (-0.5), hid...  15.7 us
    all_to_all x2, starting transfers between devices, per_device_fast(): lax.all_to_all(block, 'seq', 0, 0, axis_index_groups=CUBES, tiled=True)  11.3 us
    pallas_call x1, Pallas kernels, apply_queries(): pl.pallas_call(functools.partial(applied_kernel, size ** (-0.5), hidden *...  9.19 us
    pallas_call x3, Pallas kernels, place(): pl.pallas_call(functools.partial(place_kernel, group, which, shape[1]), o...  8.1 us
    pallas_call x2, Pallas kernels, newton(): pl.pallas_call(newton_kernel, out_shape=jax.ShapeDtypeStruct((rows, hidde...  7.84 us
  transfers between devices with their start and end apart: 44, of which 22 were waited for; matrix products, arithmetic and copies ran while one was open for 0% of the time, Pallas kernels for 26%

profile of v4, /device:TPU:0, one launch (start us, length us, event | category | flops | bytes accessed | tf_op | source)
XLA Modules:
  0.0 160.6 jit_solution(11944398972868230105)
XLA Ops:
  0.6 2.9 %pack_tokens.3 = bf16[8,2,256,256]{3,2,1,0:T(8,128)(2,1)} custom-call(bf16[256,4096]{1,0:T(8,128)(2,1)} %k_ref.3, bf16[256,4096]{1,0:T(8,128)(2,1)} %v_ref.3, f32[16,256]{1,0:T(8,128)} %rate_ref.3), custom_call_target="tpu_custom_call" | custom-call | flops 1 | bytes 1 | tf_op jit(solution)/shard_map/pack_tokens/pallas_call | solution.py:141
  3.6 6.2 %all-to-all-start.1 = ((bf16[8,2,256,256]{3,2,1,0:T(8,128)(2,1)}), bf16[8,2,256,256]{3,2,1,0:T(8,128)(2,1)S(1)}, u32[]{:S(2)}, u32[]{:S(2)}) async-start(bf16[8,2,256,256]{3,2,1,0:T(8,128)(2,1)} %pack_tokens.3), calls=%async_computation.1 | async-start | bytes 4194304 | tf_op jit(solution)/shard_map/all_to_all | solution.py:399
  9.7 9.2 %apply_queries.1.rest_0_ = bf16[256,4096]{1,0:T(8,128)(2,1)} custom-call(bf16[256,4096]{1,0:T(8,128)(2,1)} %q_ref.1, bf16[16,256,512]{2,1,0:T(8,128)(2,1)} %wg_ref.5, bf16[16,256,512]{2,1,0:T(8,128)(2,1)} %wu_ref.5, bf16[16,512,256]{2,1,0:T(8,128)(2,1)} %wd_ref.5), custom_call_target="tpu_custom_call" | custom-call | flops 1 | bytes 1 | tf_op jit(solution)/shard_map/apply_queries/pallas_call | solution.py:107
  18.9 2.9 %pack_tokens.2 = bf16[8,2,256,256]{3,2,1,0:T(8,128)(2,1)} custom-call(bf16[256,4096]{1,0:T(8,128)(2,1)} %k_ref.3, bf16[256,4096]{1,0:T(8,128)(2,1)} %v_ref.3, f32[16,256]{1,0:T(8,128)} %rate_ref.3, bf16[256,4096]{1,0:T(8,128)(2,1)} %apply_queries.1.rest_0_), custom_call_target="tpu_custom_call" | custom-call | flops 1 | bytes 1 | tf_op jit(solution)/shard_map/pack_tokens/pallas_call | solution.py:141
  21.8 13.9 %all-to-all-done.1.blocks = bf16[8,2,256,256]{3,2,1,0:T(8,128)(2,1)S(1)} async-done(((bf16[8,2,256,256]{3,2,1,0:T(8,128)(2,1)}), bf16[8,2,256,256]{3,2,1,0:T(8,128)(2,1)S(1)}, u32[]{:S(2)}, u32[]{:S(2)}) %all-to-all-start.1) | async-done | bytes 2097184 | tf_op jit(solution)/shard_map/all_to_all | solution.py:399
  37.0 5.1 %all-to-all-start = ((bf16[8,2,256,256]{3,2,1,0:T(8,128)(2,1)}), bf16[8,2,256,256]{3,2,1,0:T(8,128)(2,1)S(1)}, u32[]{:S(2)}, u32[]{:S(2)}) async-start(bf16[8,2,256,256]{3,2,1,0:T(8,128)(2,1)} %pack_tokens.2), calls=%async_computation | async-start | bytes 4194304 | tf_op jit(solution)/shard_map/all_to_all | solution.py:399
  43.8 7.8 %head_grads.2 = (bf16[384,512]{1,0:T(8,128)(2,1)S(1)}, bf16[128,512]{1,0:T(8,128)(2,1)S(1)}, bf16[128,512]{1,0:T(8,128)(2,1)S(1)}, bf16[128,512]{1,0:T(8,128)(2,1)S(1)}) custom-call(s32[5]{0:T(128)S(1)} %stack.23.where_ref, bf16[16,256,512]{2,1,0:T(8,128)(2,1)} %wg_ref.5, bf16[16,256,512]{2,1,0:T(8,128)(2,1)} %wu_ref.5, bf16[16,512,256]{2,1,0:T(8,128)(2,1)} %wd_ref.5, ...), custom_call_target="tpu_custom_call" | custom-call | flops 1 | bytes 1 | tf_op jit(solution)/shard_map/head_grads/pallas_call | solution.py:221
  53.6 2.6 %collective-permute-start.6 = (bf16[384,512]{1,0:T(8,128)(2,1)S(1)}, bf16[384,512]{1,0:T(8,128)(2,1)S(1)}, u32[]{:S(2)}, u32[]{:S(2)}) collective-permute-start(bf16[384,512]{1,0:T(8,128)(2,1)S(1)} %get-tuple-element.47.rest_0_), channel_id=1, source_target_pairs={{0,16},{1,17},{2,18},{3,19},{4,20},{5,21},{6,22},{7,23},{8,24},{9,... | collective-permute-start | bytes 1179656 | tf_op jit(solution)/shard_map/ppermute | solution.py:379
  56.2 18.9 %all-to-all-done.blocks = bf16[8,2,256,256]{3,2,1,0:T(8,128)(2,1)S(1)} async-done(((bf16[8,2,256,256]{3,2,1,0:T(8,128)(2,1)}), bf16[8,2,256,256]{3,2,1,0:T(8,128)(2,1)S(1)}, u32[]{:S(2)}, u32[]{:S(2)}) %all-to-all-start) | async-done | bytes 2097184 | tf_op jit(solution)/shard_map/all_to_all | solution.py:399
  75.1 8.0 %head_grads.3 = (bf16[384,512]{1,0:T(8,128)(2,1)S(1)}, bf16[128,512]{1,0:T(8,128)(2,1)S(1)}, bf16[128,512]{1,0:T(8,128)(2,1)S(1)}, bf16[128,512]{1,0:T(8,128)(2,1)S(1)}) custom-call(s32[5]{0:T(128)S(1)} %stack.23.where_ref, bf16[16,256,512]{2,1,0:T(8,128)(2,1)} %wg_ref.5, bf16[16,256,512]{2,1,0:T(8,128)(2,1)} %wu_ref.5, bf16[16,512,256]{2,1,0:T(8,128)(2,1)} %wd_ref.5, ...), custom_call_target="tpu_custom_call" | custom-call | flops 1 | bytes 1 | tf_op jit(solution)/shard_map/head_grads/pallas_call | solution.py:221
  85.6 3.9 %newton_schulz.2.rest_0_ = bf16[384,512]{1,0:T(8,128)(2,1)S(1)} custom-call(s32[5]{0:T(128)S(1)} %stack.23.where_ref, bf16[384,512]{1,0:T(8,128)(2,1)S(1)} %get-tuple-element.47.rest_0_, bf16[384,512]{1,0:T(8,128)(2,1)S(1)} %collective-permute-done.6.rest_0_.rest_1_, bf16[128,512]{1,0:T(8,128)(2,1)S(1)} %collective-permute-done.7.rest_2_, ...), custom_call_target="tpu_custom_call" | custom-call | flops 1 | bytes 1 | tf_op jit(solution)/shard_map/newton_schulz/pallas_call | solution.py:300
  89.5 3.7 %collective-permute-start.10 = (bf16[384,512]{1,0:T(8,128)(2,1)S(1)}, bf16[384,512]{1,0:T(8,128)(2,1)S(1)}, u32[]{:S(2)}, u32[]{:S(2)}) collective-permute-start(bf16[384,512]{1,0:T(8,128)(2,1)S(1)} %newton_schulz.2.rest_0_), channel_id=1, source_target_pairs={{0,2},{1,5},{2,0},{3,7},{4,6},{5,1},{6,4},{7,3},{8,10},{9,13},{10,... | collective-permute-start | bytes 1179656 | tf_op jit(solution)/shard_map/ppermute | solution.py:379
  94.7 2.4 %collective-permute-start.15 = (bf16[384,512]{1,0:T(8,128)(2,1)S(1)}, bf16[384,512]{1,0:T(8,128)(2,1)S(1)}, u32[]{:S(2)}, u32[]{:S(2)}) collective-permute-start(bf16[384,512]{1,0:T(8,128)(2,1)S(1)} %newton_schulz.2.rest_0_), channel_id=1, source_target_pairs={{0,8},{1,9},{2,10},{3,11},{4,12},{5,13},{6,14},{7,15},{8,0},{9,1},... | collective-permute-start | bytes 1179656 | tf_op jit(solution)/shard_map/ppermute | solution.py:379
  97.1 8.5 %collective-permute-done.11.rest_1_ = bf16[384,512]{1,0:T(8,128)(2,1)S(1)} collective-permute-done((bf16[384,512]{1,0:T(8,128)(2,1)S(1)}, bf16[384,512]{1,0:T(8,128)(2,1)S(1)}, u32[]{:S(2)}, u32[]{:S(2)}) %collective-permute-start.11) | collective-permute-done | bytes 393248 | tf_op jit(solution)/shard_map/ppermute | solution.py:379
  106.6 2.2 %collective-permute-start.12 = (bf16[128,512]{1,0:T(8,128)(2,1)S(1)}, bf16[128,512]{1,0:T(8,128)(2,1)S(1)}, u32[]{:S(2)}, u32[]{:S(2)}) collective-permute-start(bf16[128,512]{1,0:T(8,128)(2,1)S(1)} %get-tuple-element.55), channel_id=1, source_target_pairs={{0,1},{1,0},{2,3},{3,2},{4,5},{5,4},{6,7},{7,6},{8,9},{9,8},{10,11... | collective-permute-start | bytes 393224 | tf_op jit(solution)/shard_map/ppermute | solution.py:379
  110.2 3.9 %newton_schulz.3.rest_0_ = bf16[384,512]{1,0:T(8,128)(2,1)S(1)} custom-call(s32[5]{0:T(128)S(1)} %stack.23.where_ref, bf16[384,512]{1,0:T(8,128)(2,1)S(1)} %get-tuple-element.52.rest_4_.rest_0_, bf16[384,512]{1,0:T(8,128)(2,1)S(1)} %collective-permute-done.11.rest_1_, bf16[128,512]{1,0:T(8,128)(2,1)S(1)} %collective-permute-done.12.rest_2_, ...), custom_call_target="tpu_custom_call" | custom-call | flops 1 | bytes 1 | tf_op jit(solution)/shard_map/newton_schulz/pallas_call | solution.py:300
  115.7 2.6 %collective-permute-start.17 = (bf16[384,512]{1,0:T(8,128)(2,1)S(1)}, bf16[384,512]{1,0:T(8,128)(2,1)S(1)}, u32[]{:S(2)}, u32[]{:S(2)}) collective-permute-start(bf16[384,512]{1,0:T(8,128)(2,1)S(1)} %newton_schulz.3.rest_0_), channel_id=1, source_target_pairs={{0,2},{1,5},{2,0},{3,7},{4,6},{5,1},{6,4},{7,3},{8,10},{9,13},{10,... | collective-permute-start | bytes 1179656 | tf_op jit(solution)/shard_map/ppermute | solution.py:379
  118.5 3.9 %collective-permute-done.20.rest_9_ = bf16[384,512]{1,0:T(8,128)(2,1)S(1)} collective-permute-done((bf16[384,512]{1,0:T(8,128)(2,1)S(1)}, bf16[384,512]{1,0:T(8,128)(2,1)S(1)}, u32[]{:S(2)}, u32[]{:S(2)}) %collective-permute-start.20) | collective-permute-done | bytes 393248 | tf_op jit(solution)/shard_map/ppermute | solution.py:379
  123.2 1.9 %collective-permute-done.16.rest_1_ = bf16[384,512]{1,0:T(8,128)(2,1)S(1)} collective-permute-done((bf16[384,512]{1,0:T(8,128)(2,1)S(1)}, bf16[384,512]{1,0:T(8,128)(2,1)S(1)}, u32[]{:S(2)}, u32[]{:S(2)}) %collective-permute-start.16) | collective-permute-done | bytes 393248 | tf_op jit(solution)/shard_map/ppermute | solution.py:379
  126.3 4.4 %collective-permute-done.18.rest_8_ = bf16[384,512]{1,0:T(8,128)(2,1)S(1)} collective-permute-done((bf16[384,512]{1,0:T(8,128)(2,1)S(1)}, bf16[384,512]{1,0:T(8,128)(2,1)S(1)}, u32[]{:S(2)}, u32[]{:S(2)}) %collective-permute-start.18) | collective-permute-done | bytes 393248 | tf_op jit(solution)/shard_map/ppermute | solution.py:379
  131.2 3.0 %collective-permute-done.21.rest_11_ = bf16[384,512]{1,0:T(8,128)(2,1)S(1)} collective-permute-done((bf16[384,512]{1,0:T(8,128)(2,1)S(1)}, bf16[384,512]{1,0:T(8,128)(2,1)S(1)}, u32[]{:S(2)}, u32[]{:S(2)}) %collective-permute-start.21) | collective-permute-done | bytes 393248 | tf_op jit(solution)/shard_map/ppermute | solution.py:379
  138.2 7.8 %collective-permute-done.22.rest_9_ = bf16[384,512]{1,0:T(8,128)(2,1)S(1)} collective-permute-done((bf16[384,512]{1,0:T(8,128)(2,1)S(1)}, bf16[384,512]{1,0:T(8,128)(2,1)S(1)}, u32[]{:S(2)}, u32[]{:S(2)}) %collective-permute-start.22) | collective-permute-done | bytes 393248 | tf_op jit(solution)/shard_map/ppermute | solution.py:379
  150.5 3.4 %place_steps.3 = (bf16[16,256,512]{2,1,0:T(8,128)(2,1)}, bf16[16,256,512]{2,1,0:T(8,128)(2,1)}, bf16[16,256,512]{2,1,0:T(8,128)(2,1)}) custom-call(s32[5]{0:T(128)S(1)} %stack.23.where_ref, bf16[384,512]{1,0:T(8,128)(2,1)S(1)} %newton_schulz.2.rest_0_, bf16[384,512]{1,0:T(8,128)(2,1)S(1)} %collective-permute-done.9.rest_1_, ...), custom_call_target="tpu_custom_call" | custom-call | flops 1 | bytes 1 | tf_op jit(solution)/shard_map/place_steps/pallas_call | solution.py:346
  154.0 3.2 %place_steps.4 = (bf16[16,256,512]{2,1,0:T(8,128)(2,1)}, bf16[16,256,512]{2,1,0:T(8,128)(2,1)}, bf16[16,256,512]{2,1,0:T(8,128)(2,1)}) custom-call(s32[5]{0:T(128)S(1)} %stack.23.where_ref, bf16[384,512]{1,0:T(8,128)(2,1)S(1)} %newton_schulz.3.rest_0_, ...), custom_call_target="tpu_custom_call", output_to_operand_aliasing={{0}: (15, {}), {1}: (16, {}), {2}: (17, {})} | custom-call | flops 1 | bytes 1 | tf_op jit(solution)/shard_map/place_steps/pallas_call | solution.py:346
  (83 shorter events, 27.3 us)
Async XLA Ops:
  3.6 32.1 %all-to-all-start.1 = ((bf16[8,2,256,256]{3,2,1,0:T(8,128)(2,1)}), bf16[8,2,256,256]{3,2,1,0:T(8,128)(2,1)S(1)}, u32[]{:S(2)}, u32[]{:S(2)}) async-start(bf16[8,2,256,256]{3,2,1,0:T(8,128)(2,1)} %pack_tokens.3), calls=%async_computation.1 | async-start | bytes 4194304 | tf_op jit(solution)/shard_map/all_to_all | solution.py:399
  37.0 38.1 %all-to-all-start = ((bf16[8,2,256,256]{3,2,1,0:T(8,128)(2,1)}), bf16[8,2,256,256]{3,2,1,0:T(8,128)(2,1)S(1)}, u32[]{:S(2)}, u32[]{:S(2)}) async-start(bf16[8,2,256,256]{3,2,1,0:T(8,128)(2,1)} %pack_tokens.2), calls=%async_computation | async-start | bytes 4194304 | tf_op jit(solution)/shard_map/all_to_all | solution.py:399
  53.6 30.6 %collective-permute-start.6 = (bf16[384,512]{1,0:T(8,128)(2,1)S(1)}, bf16[384,512]{1,0:T(8,128)(2,1)S(1)}, u32[]{:S(2)}, u32[]{:S(2)}) collective-permute-start(bf16[384,512]{1,0:T(8,128)(2,1)S(1)} %get-tuple-element.47.rest_0_), channel_id=1, source_target_pairs={{0,16},{1,17},{2,18},{3,19},{4,20},{5,21},{6,22},{7,23},{8,24},{9,... | collective-permute-start | bytes 1179656 | tf_op jit(solution)/shard_map/ppermute | solution.py:379
  85.1 20.4 %collective-permute-start.11 = (bf16[384,512]{1,0:T(8,128)(2,1)S(1)}, bf16[384,512]{1,0:T(8,128)(2,1)S(1)}, u32[]{:S(2)}, u32[]{:S(2)}) collective-permute-start(bf16[384,512]{1,0:T(8,128)(2,1)S(1)} %get-tuple-element.52.rest_4_.rest_0_), channel_id=1, source_target_pairs={{0,16},{1,17},{2,18},{3,19},{4,20},{5,21},{6,22},{7,23},{8,24},{9,... | collective-permute-start | bytes 1179656 | tf_op jit(solution)/shard_map/ppermute | solution.py:379
  89.5 16.0 %collective-permute-start.10 = (bf16[384,512]{1,0:T(8,128)(2,1)S(1)}, bf16[384,512]{1,0:T(8,128)(2,1)S(1)}, u32[]{:S(2)}, u32[]{:S(2)}) collective-permute-start(bf16[384,512]{1,0:T(8,128)(2,1)S(1)} %newton_schulz.2.rest_0_), channel_id=1, source_target_pairs={{0,2},{1,5},{2,0},{3,7},{4,6},{5,1},{6,4},{7,3},{8,10},{9,13},{10,... | collective-permute-start | bytes 1179656 | tf_op jit(solution)/shard_map/ppermute | solution.py:379
  93.2 12.3 %collective-permute-start.9 = (bf16[384,512]{1,0:T(8,128)(2,1)S(1)}, bf16[384,512]{1,0:T(8,128)(2,1)S(1)}, u32[]{:S(2)}, u32[]{:S(2)}) collective-permute-start(bf16[384,512]{1,0:T(8,128)(2,1)S(1)} %newton_schulz.2.rest_0_), channel_id=1, source_target_pairs={{0,4},{1,3},{2,6},{3,1},{4,0},{5,7},{6,2},{7,5},{8,12},{9,11},{10,... | collective-permute-start | bytes 1179656 | tf_op jit(solution)/shard_map/ppermute | solution.py:379
  94.7 19.4 %collective-permute-start.15 = (bf16[384,512]{1,0:T(8,128)(2,1)S(1)}, bf16[384,512]{1,0:T(8,128)(2,1)S(1)}, u32[]{:S(2)}, u32[]{:S(2)}) collective-permute-start(bf16[384,512]{1,0:T(8,128)(2,1)S(1)} %newton_schulz.2.rest_0_), channel_id=1, source_target_pairs={{0,8},{1,9},{2,10},{3,11},{4,12},{5,13},{6,14},{7,15},{8,0},{9,1},... | collective-permute-start | bytes 1179656 | tf_op jit(solution)/shard_map/ppermute | solution.py:379
  105.6 8.6 %collective-permute-start.14 = (bf16[384,512]{1,0:T(8,128)(2,1)S(1)}, bf16[384,512]{1,0:T(8,128)(2,1)S(1)}, u32[]{:S(2)}, u32[]{:S(2)}) collective-permute-start(bf16[384,512]{1,0:T(8,128)(2,1)S(1)} %collective-permute-done.10.rest_2_), channel_id=1, source_target_pairs={{0,4},{1,3},{2,6},{3,1},{4,0},{5,7},{6,2},{7,5},{8,12},{9,11},{10,... | collective-permute-start | bytes 1179656 | tf_op jit(solution)/shard_map/ppermute | solution.py:379
  108.9 13.5 %collective-permute-start.20 = (bf16[384,512]{1,0:T(8,128)(2,1)S(1)}, bf16[384,512]{1,0:T(8,128)(2,1)S(1)}, u32[]{:S(2)}, u32[]{:S(2)}) collective-permute-start(bf16[384,512]{1,0:T(8,128)(2,1)S(1)} %collective-permute-done.9.rest_1_), channel_id=1, source_target_pairs={{0,8},{1,9},{2,10},{3,11},{4,12},{5,13},{6,14},{7,15},{8,0},{9,1},... | collective-permute-start | bytes 1179656 | tf_op jit(solution)/shard_map/ppermute | solution.py:379
  114.1 11.0 %collective-permute-start.16 = (bf16[384,512]{1,0:T(8,128)(2,1)S(1)}, bf16[384,512]{1,0:T(8,128)(2,1)S(1)}, u32[]{:S(2)}, u32[]{:S(2)}) collective-permute-start(bf16[384,512]{1,0:T(8,128)(2,1)S(1)} %newton_schulz.3.rest_0_), channel_id=1, source_target_pairs={{0,4},{1,3},{2,6},{3,1},{4,0},{5,7},{6,2},{7,5},{8,12},{9,11},{10,... | collective-permute-start | bytes 1179656 | tf_op jit(solution)/shard_map/ppermute | solution.py:379
  115.7 10.1 %collective-permute-start.17 = (bf16[384,512]{1,0:T(8,128)(2,1)S(1)}, bf16[384,512]{1,0:T(8,128)(2,1)S(1)}, u32[]{:S(2)}, u32[]{:S(2)}) collective-permute-start(bf16[384,512]{1,0:T(8,128)(2,1)S(1)} %newton_schulz.3.rest_0_), channel_id=1, source_target_pairs={{0,2},{1,5},{2,0},{3,7},{4,6},{5,1},{6,4},{7,3},{8,10},{9,13},{10,... | collective-permute-start | bytes 1179656 | tf_op jit(solution)/shard_map/ppermute | solution.py:379
  118.3 12.4 %collective-permute-start.18 = (bf16[384,512]{1,0:T(8,128)(2,1)S(1)}, bf16[384,512]{1,0:T(8,128)(2,1)S(1)}, u32[]{:S(2)}, u32[]{:S(2)}) collective-permute-start(bf16[384,512]{1,0:T(8,128)(2,1)S(1)} %newton_schulz.3.rest_0_), channel_id=1, source_target_pairs={{0,8},{1,9},{2,10},{3,11},{4,12},{5,13},{6,14},{7,15},{8,0},{9,1},... | collective-permute-start | bytes 1179656 | tf_op jit(solution)/shard_map/ppermute | solution.py:379
  118.3 12.4 %collective-permute-start.19 = (bf16[384,512]{1,0:T(8,128)(2,1)S(1)}, bf16[384,512]{1,0:T(8,128)(2,1)S(1)}, u32[]{:S(2)}, u32[]{:S(2)}) collective-permute-start(bf16[384,512]{1,0:T(8,128)(2,1)S(1)} %collective-permute-done.15.rest_8_), channel_id=1, source_target_pairs={{0,2},{1,5},{2,0},{3,7},{4,6},{5,1},{6,4},{7,3},{8,10},{9,13},{10,... | collective-permute-start | bytes 1179656 | tf_op jit(solution)/shard_map/ppermute | solution.py:379
  122.4 11.8 %collective-permute-start.21 = (bf16[384,512]{1,0:T(8,128)(2,1)S(1)}, bf16[384,512]{1,0:T(8,128)(2,1)S(1)}, u32[]{:S(2)}, u32[]{:S(2)}) collective-permute-start(bf16[384,512]{1,0:T(8,128)(2,1)S(1)} %collective-permute-done.20.rest_9_), channel_id=1, source_target_pairs={{0,2},{1,5},{2,0},{3,7},{4,6},{5,1},{6,4},{7,3},{8,10},{9,13},{10,... | collective-permute-start | bytes 1179656 | tf_op jit(solution)/shard_map/ppermute | solution.py:379
  125.2 9.3 %collective-permute-start.33 = (bf16[384,512]{1,0:T(8,128)(2,1)S(1)}, bf16[384,512]{1,0:T(8,128)(2,1)S(1)}, u32[]{:S(2)}, u32[]{:S(2)}) collective-permute-start(bf16[384,512]{1,0:T(8,128)(2,1)S(1)} %newton_schulz.2.rest_0_), channel_id=1, source_target_pairs={{0,1},{1,0},{2,3},{3,2},{4,5},{5,4},{6,7},{7,6},{8,9},{9,8},{10,11... | collective-permute-start | bytes 1179656 | tf_op jit(solution)/shard_map/ppermute | solution.py:379
  125.8 8.9 %collective-permute-start.34 = (bf16[384,512]{1,0:T(8,128)(2,1)S(1)}, bf16[384,512]{1,0:T(8,128)(2,1)S(1)}, u32[]{:S(2)}, u32[]{:S(2)}) collective-permute-start(bf16[384,512]{1,0:T(8,128)(2,1)S(1)} %collective-permute-done.9.rest_1_), channel_id=1, source_target_pairs={{0,1},{1,0},{2,3},{3,2},{4,5},{5,4},{6,7},{7,6},{8,9},{9,8},{10,11... | collective-permute-start | bytes 1179656 | tf_op jit(solution)/shard_map/ppermute | solution.py:379
  134.7 11.3 %collective-permute-start.22 = (bf16[384,512]{1,0:T(8,128)(2,1)S(1)}, bf16[384,512]{1,0:T(8,128)(2,1)S(1)}, u32[]{:S(2)}, u32[]{:S(2)}) collective-permute-start(bf16[384,512]{1,0:T(8,128)(2,1)S(1)} %collective-permute-done.16.rest_1_), channel_id=1, source_target_pairs={{0,8},{1,9},{2,10},{3,11},{4,12},{5,13},{6,14},{7,15},{8,0},{9,1},... | collective-permute-start | bytes 1179656 | tf_op jit(solution)/shard_map/ppermute | solution.py:379
  135.3 11.7 %collective-permute-start.23 = (bf16[384,512]{1,0:T(8,128)(2,1)S(1)}, bf16[384,512]{1,0:T(8,128)(2,1)S(1)}, u32[]{:S(2)}, u32[]{:S(2)}) collective-permute-start(bf16[384,512]{1,0:T(8,128)(2,1)S(1)} %collective-permute-done.17.rest_2_), channel_id=1, source_target_pairs={{0,4},{1,3},{2,6},{3,1},{4,0},{5,7},{6,2},{7,5},{8,12},{9,11},{10,... | collective-permute-start | bytes 1179656 | tf_op jit(solution)/shard_map/ppermute | solution.py:379
  136.6 10.4 %collective-permute-start.24 = (bf16[384,512]{1,0:T(8,128)(2,1)S(1)}, bf16[384,512]{1,0:T(8,128)(2,1)S(1)}, u32[]{:S(2)}, u32[]{:S(2)}) collective-permute-start(bf16[384,512]{1,0:T(8,128)(2,1)S(1)} %collective-permute-done.18.rest_8_), channel_id=1, source_target_pairs={{0,2},{1,5},{2,0},{3,7},{4,6},{5,1},{6,4},{7,3},{8,10},{9,13},{10,... | collective-permute-start | bytes 1179656 | tf_op jit(solution)/shard_map/ppermute | solution.py:379
  137.7 9.8 %collective-permute-start.26 = (bf16[384,512]{1,0:T(8,128)(2,1)S(1)}, bf16[384,512]{1,0:T(8,128)(2,1)S(1)}, u32[]{:S(2)}, u32[]{:S(2)}) collective-permute-start(bf16[384,512]{1,0:T(8,128)(2,1)S(1)} %newton_schulz.3.rest_0_), channel_id=1, source_target_pairs={{0,1},{1,0},{2,3},{3,2},{4,5},{5,4},{6,7},{7,6},{8,9},{9,8},{10,11... | collective-permute-start | bytes 1179656 | tf_op jit(solution)/shard_map/ppermute | solution.py:379
  137.7 9.9 %collective-permute-start.39 = (bf16[384,512]{1,0:T(8,128)(2,1)S(1)}, bf16[384,512]{1,0:T(8,128)(2,1)S(1)}, u32[]{:S(2)}, u32[]{:S(2)}) collective-permute-start(bf16[384,512]{1,0:T(8,128)(2,1)S(1)} %collective-permute-done.19.rest_10_), channel_id=1, source_target_pairs={{0,1},{1,0},{2,3},{3,2},{4,5},{5,4},{6,7},{7,6},{8,9},{9,8},{10,11... | collective-permute-start | bytes 1179656 | tf_op jit(solution)/shard_map/ppermute | solution.py:379
  147.6 6.4 %collective-permute-start.30 = (bf16[384,512]{1,0:T(8,128)(2,1)S(1)}, bf16[384,512]{1,0:T(8,128)(2,1)S(1)}, u32[]{:S(2)}, u32[]{:S(2)}) collective-permute-start(bf16[384,512]{1,0:T(8,128)(2,1)S(1)} %collective-permute-done.18.rest_8_), channel_id=1, source_target_pairs={{0,1},{1,0},{2,3},{3,2},{4,5},{5,4},{6,7},{7,6},{8,9},{9,8},{10,11... | collective-permute-start | bytes 1179656 | tf_op jit(solution)/shard_map/ppermute | solution.py:379
  147.6 6.3 %collective-permute-start.29 = (bf16[384,512]{1,0:T(8,128)(2,1)S(1)}, bf16[384,512]{1,0:T(8,128)(2,1)S(1)}, u32[]{:S(2)}, u32[]{:S(2)}) collective-permute-start(bf16[384,512]{1,0:T(8,128)(2,1)S(1)} %collective-permute-done.23.rest_3_), channel_id=1, source_target_pairs={{0,1},{1,0},{2,3},{3,2},{4,5},{5,4},{6,7},{7,6},{8,9},{9,8},{10,11... | collective-permute-start | bytes 1179656 | tf_op jit(solution)/shard_map/ppermute | solution.py:379
  149.3 7.9 %collective-permute-start.25 = (bf16[384,512]{1,0:T(8,128)(2,1)S(1)}, bf16[384,512]{1,0:T(8,128)(2,1)S(1)}, u32[]{:S(2)}, u32[]{:S(2)}) collective-permute-start(bf16[384,512]{1,0:T(8,128)(2,1)S(1)} %collective-permute-done.22.rest_9_), channel_id=1, source_target_pairs={{0,2},{1,5},{2,0},{3,7},{4,6},{5,1},{6,4},{7,3},{8,10},{9,13},{10,... | collective-permute-start | bytes 1179656 | tf_op jit(solution)/shard_map/ppermute | solution.py:379
  (22 other events, 55.2 us)

commit v5 on v4

--- a/solution.py
+++ b/solution.py
@@ -149,38 +149,20 @@
         ]
         + [ANY] * len(follows),
         out_specs=pl.BlockSpec((each, 2, tokens, size), lambda i: (i, 0, 0, 0)),
-        compiler_params=pltpu.CompilerParams(vmem_limit_bytes=VMEM_BYTES),
+        compiler_params=pltpu.CompilerParams(vmem_limit_bytes=16 * 1024 * 1024 if group else VMEM_BYTES),
         cost_estimate=COST_PACK,
         name="pack_tokens",
     )(keys, values, rates, *follows)
 
 
-def grads_kernel(group, scale_one, scale_two, where_ref, wg_ref, wu_ref, wd_ref, blocks, *rest):
-    keep, *send = rest[-12:-8]
-    held, total, final, wg_held, wu_held, wd_held, in_sem, sem = rest[-8:]
-    head = group * PLANE + where_ref[0]
-    weights = [
-        pltpu.make_async_copy(ref.at[head], to, in_sem.at[PLANE + i])
-        for i, (ref, to) in enumerate(((wg_ref, wg_held), (wu_ref, wu_held), (wd_ref, wd_held)))
-    ]
-    for copy in weights:
-        copy.start()
-    tokens = held.shape[1] // PLANE
-    copies = [
-        pltpu.make_async_copy(blocks.at[b], held.at[:, pl.ds(b * tokens, tokens)], in_sem.at[b])
-        for b in range(PLANE)
-    ]
-    for copy in copies:
-        copy.start()
-    for copy in weights:
-        copy.wait()
-    wg, wu = wg_held[...], wu_held[...]
-    wdt = jnp.transpose(wd_held[...])
+def grads_kernel(scale_one, scale_two, where_ref, wg_ref, wu_ref, wd_ref, blocks, *rest):
+    keep, *send = rest[-7:-3]
+    total, final, sem = rest[-3:]
+    wg, wu = wg_ref[...], wu_ref[...]
+    wdt = jnp.transpose(wd_ref[...])
     for b in range(0, PLANE, 2):
-        copies[b].wait()
-        copies[b + 1].wait()
-        rows = slice(b * tokens, (b + 2) * tokens)
-        k, vr = held[0, rows], held[1, rows]
+        k = blocks[b : b + 2, 0].reshape(2 * blocks.shape[2], blocks.shape[3])
+        vr = blocks[b : b + 2, 1].reshape(2 * blocks.shape[2], blocks.shape[3])
         gk = scale_one * dot(k, wg)
         uk = dot(k, wu)
         dh = dot(vr, wdt)
@@ -215,29 +197,23 @@
     )
 
 
-def head_grads(where, blocks, w_gate, w_up, w_down, group, *follows):
-    _, size, hidden = w_gate.shape
-    tokens = blocks.shape[2]
-    return pl.pallas_call(
-        functools.partial(grads_kernel, group, size**-0.5, hidden**-0.5),
+def head_grads(where, blocks, weights, *follows):
+    size, hidden = weights[0].shape
+    return pl.pallas_call(
+        functools.partial(grads_kernel, size**-0.5, hidden**-0.5),
         out_shape=[jax.ShapeDtypeStruct((size + size // 2, hidden), BF)]
         + [jax.ShapeDtypeStruct((size // 2, hidden), BF)] * 3,
-        in_specs=[SMEM] + [HBM] * 3 + [ANY] * (1 + len(follows)),
+        in_specs=[SMEM] + [VMEM] * 4 + [ANY] * len(follows),
         out_specs=[ANY] * 4,
         scratch_shapes=[
-            pltpu.VMEM((2, PLANE * tokens, size), BF),
             pltpu.VMEM((3, size, hidden), F32),
             pltpu.VMEM((3, size, hidden), BF),
-            pltpu.VMEM((size, hidden), BF),
-            pltpu.VMEM((size, hidden), BF),
-            pltpu.VMEM((hidden, size), BF),
-            pltpu.SemaphoreType.DMA((PLANE + 3,)),
             pltpu.SemaphoreType.DMA((5,)),
         ],
-        compiler_params=pltpu.CompilerParams(vmem_limit_bytes=48 * 1024 * 1024),
+        compiler_params=pltpu.CompilerParams(vmem_limit_bytes=24 * 1024 * 1024),
         cost_estimate=COST_GRADS,
         name="head_grads",
-    )(where, w_gate, w_up, w_down, blocks, *follows)
+    )(where, *weights, blocks, *follows)
 
 
 def combine_kernel(keep_ref, a_ref, b_ref, c_ref, *rest):
@@ -393,15 +369,18 @@
 
     packed = [pack_tokens(keys, values, token_rates, 0, size)]
     applied = apply_queries(queries, w_gate, w_up, w_down)
-    for group in range(1, groups):
-        packed.append(pack_tokens(keys, values, token_rates, group, size, applied))
+    weights = [
+        [lax.dynamic_index_in_dim(w, g * PLANE + where[0], 0, False) for w in (w_gate, w_up, w_down)]
+        for g in range(groups)
+    ]
+    packed.append(pack_tokens(keys, values, token_rates, 1, size, applied, *weights[0], *weights[1]))
     received = [
         lax.all_to_all(block, "seq", 0, 0, axis_index_groups=CUBES, tiled=True)
         for block in packed
     ]
 
     def summed(group, waits, *follow):
-        keep, *send = head_grads(where, received[group], w_gate, w_up, w_down, group, *follow)
+        keep, *send = head_grads(where, received[group], weights[group], *follow)
         return combine(keep, [move(block, CORE_MOVE) for block in send], *waits)
 
     def round_two(one, two, far):

time: 161 us -> 159 us (0.988)
  waiting for transfers between devices: 70.1 us -> 64.1 us
  local copies, waits for them, and re-layouts: 3.01 us -> 8.73 us
  Pallas kernels: 46.9 us -> 44 us
    all_to_all x2, waiting for transfers between devices: 32.8 us -> 28.6 us  [per_device_fast(): lax.all_to_all(block, 'seq', 0, 0, axis_index_groups=CUBES, tiled=True)]
    unnamed x4 -> x14, local copies, waits for them, and re-layouts: 2.91 us -> 6.15 us
    squeeze x0 -> x2, local copies, waits for them, and re-layouts: none -> 2.48 us  [per_device_fast(): lax.dynamic_index_in_dim(w, g * PLANE + where[0], 0, False)]
    pallas_call x2, Pallas kernels: 15.7 us -> 13.6 us  [head_grads(): pl.pallas_call(functools.partial(grads_kernel, size ** (-0.5), hidden **...]
    pallas_call x2, Pallas kernels: 5.83 us -> 3.92 us  [pack_tokens(): pl.pallas_call(functools.partial(pack_kernel, size), grid=(steps,), out_s...]
    ppermute x42, waiting for transfers between devices: 37.3 us -> 35.5 us  [move(): return lax.ppermute(array, 'seq', pairs)]
  transfers between devices with their start and end apart: 44 -> 44, of which waited for: 22 -> 21; matrix products, arithmetic and copies ran while one was open for 0% -> 2% of each run, Pallas kernels for 26% -> 25%
where the time goes in v5:
time: 159 us
  waiting for transfers between devices  64.1 us (40%)
  Pallas kernels  44 us (28%)
  starting transfers between devices  41 us (26%)
  local copies, waits for them, and re-layouts  8.73 us (5%)
    ppermute x42, waiting for transfers between devices, move(): return lax.ppermute(array, 'seq', pairs)  35.5 us
    ppermute x42, starting transfers between devices, move(): return lax.ppermute(array, 'seq', pairs)  29.7 us
    all_to_all x2, waiting for transfers between devices, per_device_fast(): lax.all_to_all(block, 'seq', 0, 0, axis_index_groups=CUBES, tiled=True)  28.6 us
    pallas_call x2, Pallas kernels, head_grads(): pl.pallas_call(functools.partial(grads_kernel, size ** (-0.5), hidden **...  13.6 us
    all_to_all x2, starting transfers between devices, per_device_fast(): lax.all_to_all(block, 'seq', 0, 0, axis_index_groups=CUBES, tiled=True)  11.3 us
    pallas_call x1, Pallas kernels, apply_queries(): pl.pallas_call(functools.partial(applied_kernel, size ** (-0.5), hidden *...  9.2 us
    pallas_call x2, Pallas kernels, newton(): pl.pallas_call(newton_kernel, out_shape=jax.ShapeDtypeStruct((rows, hidde...  8.3 us
    pallas_call x3, Pallas kernels, place(): pl.pallas_call(functools.partial(place_kernel, group, which, shape[1]), o...  8.1 us
  transfers between devices with their start and end apart: 44, of which 21 were waited for; matrix products, arithmetic and copies ran while one was open for 2% of the time, Pallas kernels for 25%

profile of v5, /device:TPU:0, one launch (start us, length us, event | category | flops | bytes accessed | tf_op | source)
XLA Modules:
  0.0 158.9 jit_solution(15484187258173016080)
XLA Ops:
  0.6 3.0 %pack_tokens.3 = bf16[8,2,256,256]{3,2,1,0:T(8,128)(2,1)} custom-call(bf16[256,4096]{1,0:T(8,128)(2,1)} %k_ref.3, bf16[256,4096]{1,0:T(8,128)(2,1)} %v_ref.3, f32[16,256]{1,0:T(8,128)} %rate_ref.3), custom_call_target="tpu_custom_call" | custom-call | flops 1 | bytes 1 | tf_op jit(solution)/shard_map/pack_tokens/pallas_call | solution.py:141
  3.6 6.2 %all-to-all-start.1 = ((bf16[8,2,256,256]{3,2,1,0:T(8,128)(2,1)}), bf16[8,2,256,256]{3,2,1,0:T(8,128)(2,1)}, u32[]{:S(2)}, u32[]{:S(2)}) async-start(bf16[8,2,256,256]{3,2,1,0:T(8,128)(2,1)} %pack_tokens.3), calls=%async_computation.1 | async-start | bytes 4194304 | tf_op jit(solution)/shard_map/all_to_all | solution.py:378
  9.8 9.2 %apply_queries.1.rest_0_ = bf16[256,4096]{1,0:T(8,128)(2,1)} custom-call(bf16[256,4096]{1,0:T(8,128)(2,1)} %q_ref.1, bf16[16,256,512]{2,1,0:T(8,128)(2,1)} %wg_ref.1, bf16[16,256,512]{2,1,0:T(8,128)(2,1)} %wu_ref.1, bf16[16,512,256]{2,1,0:T(8,128)(2,1)} %wd_ref.1), custom_call_target="tpu_custom_call" | custom-call | flops 1 | bytes 1 | tf_op jit(solution)/shard_map/apply_queries/pallas_call | solution.py:107
  23.1 1.6 %copy-done.3 = bf16[256,4096]{1,0:T(8,128)(2,1)S(1)} copy-done((bf16[256,4096]{1,0:T(8,128)(2,1)S(1)}, bf16[256,4096]{1,0:T(8,128)(2,1)}, u32[]{:S(2)}) %copy-start.3) | copy-done | bytes 2097176
  27.7 8.2 %all-to-all-done.1.blocks = bf16[8,2,256,256]{3,2,1,0:T(8,128)(2,1)} async-done(((bf16[8,2,256,256]{3,2,1,0:T(8,128)(2,1)}), bf16[8,2,256,256]{3,2,1,0:T(8,128)(2,1)}, u32[]{:S(2)}, u32[]{:S(2)}) %all-to-all-start.1) | async-done | bytes 2097184 | tf_op jit(solution)/shard_map/all_to_all | solution.py:378
  35.9 5.1 %all-to-all-start = ((bf16[8,2,256,256]{3,2,1,0:T(8,128)(2,1)}), bf16[8,2,256,256]{3,2,1,0:T(8,128)(2,1)S(1)}, u32[]{:S(2)}, u32[]{:S(2)}) async-start(bf16[8,2,256,256]{3,2,1,0:T(8,128)(2,1)} %copy-done.2), calls=%async_computation | async-start | bytes 4194304 | tf_op jit(solution)/shard_map/all_to_all | solution.py:378
  41.1 7.2 %head_grads.2 = (bf16[384,512]{1,0:T(8,128)(2,1)S(1)}, bf16[128,512]{1,0:T(8,128)(2,1)S(1)}, bf16[128,512]{1,0:T(8,128)(2,1)S(1)}, bf16[128,512]{1,0:T(8,128)(2,1)S(1)}) custom-call(s32[5]{0:T(128)S(1)} %stack.23.where_ref, bf16[256,512]{1,0:T(8,128)(2,1)S(1)} %get-tuple-element.89.rest_1_.wg_ref, bf16[256,512]{1,0:T(8,128)(2,1)S(1)} %get-tuple-element.84.rest_2_.wu_ref, ...), custom_call_target="tpu_custom_call" | custom-call | flops 1 | bytes 1 | tf_op jit(solution)/shard_map/head_grads/pallas_call | solution.py:202
  51.0 2.6 %collective-permute-start.6 = (bf16[384,512]{1,0:T(8,128)(2,1)}, bf16[384,512]{1,0:T(8,128)(2,1)S(1)}, u32[]{:S(2)}, u32[]{:S(2)}) collective-permute-start(bf16[384,512]{1,0:T(8,128)(2,1)} %get-tuple-element.47.rest_0_), channel_id=1, source_target_pairs={{0,16},{1,17},{2,18},{3,19},{4,20},{5,21},{6,22},{7,23},{8,24},{9,... | collective-permute-start | bytes 1179656 | tf_op jit(solution)/shard_map/ppermute | solution.py:355
  53.6 20.4 %all-to-all-done.blocks = bf16[8,2,256,256]{3,2,1,0:T(8,128)(2,1)S(1)} async-done(((bf16[8,2,256,256]{3,2,1,0:T(8,128)(2,1)}), bf16[8,2,256,256]{3,2,1,0:T(8,128)(2,1)S(1)}, u32[]{:S(2)}, u32[]{:S(2)}) %all-to-all-start) | async-done | bytes 2097184 | tf_op jit(solution)/shard_map/all_to_all | solution.py:378
  75.0 6.4 %head_grads.3 = (bf16[384,512]{1,0:T(8,128)(2,1)S(1)}, bf16[128,512]{1,0:T(8,128)(2,1)S(1)}, bf16[128,512]{1,0:T(8,128)(2,1)S(1)}, bf16[128,512]{1,0:T(8,128)(2,1)S(1)}) custom-call(s32[5]{0:T(128)S(1)} %stack.23.where_ref, bf16[256,512]{1,0:T(8,128)(2,1)S(1)} %copy-done.5, bf16[256,512]{1,0:T(8,128)(2,1)S(1)} %get-tuple-element.85.rest_5_.wu_ref, ...), custom_call_target="tpu_custom_call" | custom-call | flops 1 | bytes 1 | tf_op jit(solution)/shard_map/head_grads/pallas_call | solution.py:202
  84.0 4.4 %newton_schulz.2.rest_0_ = bf16[384,512]{1,0:T(8,128)(2,1)S(1)} custom-call(s32[5]{0:T(128)S(1)} %stack.23.where_ref, bf16[384,512]{1,0:T(8,128)(2,1)} %get-tuple-element.47.rest_0_, bf16[384,512]{1,0:T(8,128)(2,1)S(1)} %collective-permute-done.6.rest_0_.rest_1_, bf16[128,512]{1,0:T(8,128)(2,1)S(1)} %collective-permute-done.7.rest_2_, ...), custom_call_target="tpu_custom_call" | custom-call | flops 1 | bytes 1 | tf_op jit(solution)/shard_map/newton_schulz/pallas_call | solution.py:276
  88.4 3.6 %collective-permute-start.10 = (bf16[384,512]{1,0:T(8,128)(2,1)S(1)}, bf16[384,512]{1,0:T(8,128)(2,1)S(1)}, u32[]{:S(2)}, u32[]{:S(2)}) collective-permute-start(bf16[384,512]{1,0:T(8,128)(2,1)S(1)} %newton_schulz.2.rest_0_), channel_id=1, source_target_pairs={{0,2},{1,5},{2,0},{3,7},{4,6},{5,1},{6,4},{7,3},{8,10},{9,13},{10,... | collective-permute-start | bytes 1179656 | tf_op jit(solution)/shard_map/ppermute | solution.py:355
  93.4 2.4 %collective-permute-start.15 = (bf16[384,512]{1,0:T(8,128)(2,1)S(1)}, bf16[384,512]{1,0:T(8,128)(2,1)S(1)}, u32[]{:S(2)}, u32[]{:S(2)}) collective-permute-start(bf16[384,512]{1,0:T(8,128)(2,1)S(1)} %newton_schulz.2.rest_0_), channel_id=1, source_target_pairs={{0,8},{1,9},{2,10},{3,11},{4,12},{5,13},{6,14},{7,15},{8,0},{9,1},... | collective-permute-start | bytes 1179656 | tf_op jit(solution)/shard_map/ppermute | solution.py:355
  95.8 8.0 %collective-permute-done.11.rest_1_ = bf16[384,512]{1,0:T(8,128)(2,1)S(1)} collective-permute-done((bf16[384,512]{1,0:T(8,128)(2,1)S(1)}, bf16[384,512]{1,0:T(8,128)(2,1)S(1)}, u32[]{:S(2)}, u32[]{:S(2)}) %collective-permute-start.11) | collective-permute-done | bytes 393248 | tf_op jit(solution)/shard_map/ppermute | solution.py:355
  103.8 1.7 %collective-permute-start.14 = (bf16[384,512]{1,0:T(8,128)(2,1)S(1)}, bf16[384,512]{1,0:T(8,128)(2,1)S(1)}, u32[]{:S(2)}, u32[]{:S(2)}) collective-permute-start(bf16[384,512]{1,0:T(8,128)(2,1)S(1)} %collective-permute-done.10.rest_2_), channel_id=1, source_target_pairs={{0,4},{1,3},{2,6},{3,1},{4,0},{5,7},{6,2},{7,5},{8,12},{9,11},{10,... | collective-permute-start | bytes 1179656 | tf_op jit(solution)/shard_map/ppermute | solution.py:355
  108.4 3.9 %newton_schulz.3.rest_0_ = bf16[384,512]{1,0:T(8,128)(2,1)S(1)} custom-call(s32[5]{0:T(128)S(1)} %stack.23.where_ref, bf16[384,512]{1,0:T(8,128)(2,1)S(1)} %get-tuple-element.52.rest_4_.rest_0_, bf16[384,512]{1,0:T(8,128)(2,1)S(1)} %collective-permute-done.11.rest_1_, bf16[128,512]{1,0:T(8,128)(2,1)S(1)} %collective-permute-done.12.rest_2_, ...), custom_call_target="tpu_custom_call" | custom-call | flops 1 | bytes 1 | tf_op jit(solution)/shard_map/newton_schulz/pallas_call | solution.py:276
  113.9 2.6 %collective-permute-start.17 = (bf16[384,512]{1,0:T(8,128)(2,1)S(1)}, bf16[384,512]{1,0:T(8,128)(2,1)S(1)}, u32[]{:S(2)}, u32[]{:S(2)}) collective-permute-start(bf16[384,512]{1,0:T(8,128)(2,1)S(1)} %newton_schulz.3.rest_0_), channel_id=1, source_target_pairs={{0,2},{1,5},{2,0},{3,7},{4,6},{5,1},{6,4},{7,3},{8,10},{9,13},{10,... | collective-permute-start | bytes 1179656 | tf_op jit(solution)/shard_map/ppermute | solution.py:355
  116.7 3.9 %collective-permute-done.20.rest_9_ = bf16[384,512]{1,0:T(8,128)(2,1)S(1)} collective-permute-done((bf16[384,512]{1,0:T(8,128)(2,1)S(1)}, bf16[384,512]{1,0:T(8,128)(2,1)S(1)}, u32[]{:S(2)}, u32[]{:S(2)}) %collective-permute-start.20) | collective-permute-done | bytes 393248 | tf_op jit(solution)/shard_map/ppermute | solution.py:355
  120.6 1.8 %collective-permute-start.21 = (bf16[384,512]{1,0:T(8,128)(2,1)S(1)}, bf16[384,512]{1,0:T(8,128)(2,1)S(1)}, u32[]{:S(2)}, u32[]{:S(2)}) collective-permute-start(bf16[384,512]{1,0:T(8,128)(2,1)S(1)} %collective-permute-done.20.rest_9_), channel_id=1, source_target_pairs={{0,2},{1,5},{2,0},{3,7},{4,6},{5,1},{6,4},{7,3},{8,10},{9,13},{10,... | collective-permute-start | bytes 1179656 | tf_op jit(solution)/shard_map/ppermute | solution.py:355
  124.6 4.4 %collective-permute-done.18.rest_8_ = bf16[384,512]{1,0:T(8,128)(2,1)S(1)} collective-permute-done((bf16[384,512]{1,0:T(8,128)(2,1)S(1)}, bf16[384,512]{1,0:T(8,128)(2,1)S(1)}, u32[]{:S(2)}, u32[]{:S(2)}) %collective-permute-start.18) | collective-permute-done | bytes 393248 | tf_op jit(solution)/shard_map/ppermute | solution.py:355
  129.5 3.0 %collective-permute-done.21.rest_11_ = bf16[384,512]{1,0:T(8,128)(2,1)S(1)} collective-permute-done((bf16[384,512]{1,0:T(8,128)(2,1)S(1)}, bf16[384,512]{1,0:T(8,128)(2,1)S(1)}, u32[]{:S(2)}, u32[]{:S(2)}) %collective-permute-start.21) | collective-permute-done | bytes 393248 | tf_op jit(solution)/shard_map/ppermute | solution.py:355
  136.5 7.8 %collective-permute-done.22.rest_9_ = bf16[384,512]{1,0:T(8,128)(2,1)S(1)} collective-permute-done((bf16[384,512]{1,0:T(8,128)(2,1)S(1)}, bf16[384,512]{1,0:T(8,128)(2,1)S(1)}, u32[]{:S(2)}, u32[]{:S(2)}) %collective-permute-start.22) | collective-permute-done | bytes 393248 | tf_op jit(solution)/shard_map/ppermute | solution.py:355
  148.8 3.4 %place_steps.3 = (bf16[16,256,512]{2,1,0:T(8,128)(2,1)}, bf16[16,256,512]{2,1,0:T(8,128)(2,1)}, bf16[16,256,512]{2,1,0:T(8,128)(2,1)}) custom-call(s32[5]{0:T(128)S(1)} %stack.23.where_ref, bf16[384,512]{1,0:T(8,128)(2,1)S(1)} %newton_schulz.2.rest_0_, bf16[384,512]{1,0:T(8,128)(2,1)S(1)} %collective-permute-done.9.rest_1_, ...), custom_call_target="tpu_custom_call" | custom-call | flops 1 | bytes 1 | tf_op jit(solution)/shard_map/place_steps/pallas_call | solution.py:322
  152.3 3.2 %place_steps.4 = (bf16[16,256,512]{2,1,0:T(8,128)(2,1)}, bf16[16,256,512]{2,1,0:T(8,128)(2,1)}, bf16[16,256,512]{2,1,0:T(8,128)(2,1)}) custom-call(s32[5]{0:T(128)S(1)} %stack.23.where_ref, bf16[384,512]{1,0:T(8,128)(2,1)S(1)} %newton_schulz.3.rest_0_, ...), custom_call_target="tpu_custom_call", output_to_operand_aliasing={{0}: (15, {}), {1}: (16, {}), {2}: (17, {})} | custom-call | flops 1 | bytes 1 | tf_op jit(solution)/shard_map/place_steps/pallas_call | solution.py:322
  (95 shorter events, 34.0 us)
Async XLA Ops:
  3.6 32.2 %all-to-all-start.1 = ((bf16[8,2,256,256]{3,2,1,0:T(8,128)(2,1)}), bf16[8,2,256,256]{3,2,1,0:T(8,128)(2,1)}, u32[]{:S(2)}, u32[]{:S(2)}) async-start(bf16[8,2,256,256]{3,2,1,0:T(8,128)(2,1)} %pack_tokens.3), calls=%async_computation.1 | async-start | bytes 4194304 | tf_op jit(solution)/shard_map/all_to_all | solution.py:378
  35.9 38.1 %all-to-all-start = ((bf16[8,2,256,256]{3,2,1,0:T(8,128)(2,1)}), bf16[8,2,256,256]{3,2,1,0:T(8,128)(2,1)S(1)}, u32[]{:S(2)}, u32[]{:S(2)}) async-start(bf16[8,2,256,256]{3,2,1,0:T(8,128)(2,1)} %copy-done.2), calls=%async_computation | async-start | bytes 4194304 | tf_op jit(solution)/shard_map/all_to_all | solution.py:378
  51.0 31.4 %collective-permute-start.6 = (bf16[384,512]{1,0:T(8,128)(2,1)}, bf16[384,512]{1,0:T(8,128)(2,1)S(1)}, u32[]{:S(2)}, u32[]{:S(2)}) collective-permute-start(bf16[384,512]{1,0:T(8,128)(2,1)} %get-tuple-element.47.rest_0_), channel_id=1, source_target_pairs={{0,16},{1,17},{2,18},{3,19},{4,20},{5,21},{6,22},{7,23},{8,24},{9,... | collective-permute-start | bytes 1179656 | tf_op jit(solution)/shard_map/ppermute | solution.py:355
  83.4 20.4 %collective-permute-start.11 = (bf16[384,512]{1,0:T(8,128)(2,1)S(1)}, bf16[384,512]{1,0:T(8,128)(2,1)S(1)}, u32[]{:S(2)}, u32[]{:S(2)}) collective-permute-start(bf16[384,512]{1,0:T(8,128)(2,1)S(1)} %get-tuple-element.52.rest_4_.rest_0_), channel_id=1, source_target_pairs={{0,16},{1,17},{2,18},{3,19},{4,20},{5,21},{6,22},{7,23},{8,24},{9,... | collective-permute-start | bytes 1179656 | tf_op jit(solution)/shard_map/ppermute | solution.py:355
  88.4 15.4 %collective-permute-start.10 = (bf16[384,512]{1,0:T(8,128)(2,1)S(1)}, bf16[384,512]{1,0:T(8,128)(2,1)S(1)}, u32[]{:S(2)}, u32[]{:S(2)}) collective-permute-start(bf16[384,512]{1,0:T(8,128)(2,1)S(1)} %newton_schulz.2.rest_0_), channel_id=1, source_target_pairs={{0,2},{1,5},{2,0},{3,7},{4,6},{5,1},{6,4},{7,3},{8,10},{9,13},{10,... | collective-permute-start | bytes 1179656 | tf_op jit(solution)/shard_map/ppermute | solution.py:355
  92.0 11.8 %collective-permute-start.9 = (bf16[384,512]{1,0:T(8,128)(2,1)S(1)}, bf16[384,512]{1,0:T(8,128)(2,1)S(1)}, u32[]{:S(2)}, u32[]{:S(2)}) collective-permute-start(bf16[384,512]{1,0:T(8,128)(2,1)S(1)} %newton_schulz.2.rest_0_), channel_id=1, source_target_pairs={{0,4},{1,3},{2,6},{3,1},{4,0},{5,7},{6,2},{7,5},{8,12},{9,11},{10,... | collective-permute-start | bytes 1179656 | tf_op jit(solution)/shard_map/ppermute | solution.py:355
  93.4 19.0 %collective-permute-start.15 = (bf16[384,512]{1,0:T(8,128)(2,1)S(1)}, bf16[384,512]{1,0:T(8,128)(2,1)S(1)}, u32[]{:S(2)}, u32[]{:S(2)}) collective-permute-start(bf16[384,512]{1,0:T(8,128)(2,1)S(1)} %newton_schulz.2.rest_0_), channel_id=1, source_target_pairs={{0,8},{1,9},{2,10},{3,11},{4,12},{5,13},{6,14},{7,15},{8,0},{9,1},... | collective-permute-start | bytes 1179656 | tf_op jit(solution)/shard_map/ppermute | solution.py:355
  103.8 8.6 %collective-permute-start.14 = (bf16[384,512]{1,0:T(8,128)(2,1)S(1)}, bf16[384,512]{1,0:T(8,128)(2,1)S(1)}, u32[]{:S(2)}, u32[]{:S(2)}) collective-permute-start(bf16[384,512]{1,0:T(8,128)(2,1)S(1)} %collective-permute-done.10.rest_2_), channel_id=1, source_target_pairs={{0,4},{1,3},{2,6},{3,1},{4,0},{5,7},{6,2},{7,5},{8,12},{9,11},{10,... | collective-permute-start | bytes 1179656 | tf_op jit(solution)/shard_map/ppermute | solution.py:355
  107.1 13.5 %collective-permute-start.20 = (bf16[384,512]{1,0:T(8,128)(2,1)S(1)}, bf16[384,512]{1,0:T(8,128)(2,1)S(1)}, u32[]{:S(2)}, u32[]{:S(2)}) collective-permute-start(bf16[384,512]{1,0:T(8,128)(2,1)S(1)} %collective-permute-done.9.rest_1_), channel_id=1, source_target_pairs={{0,8},{1,9},{2,10},{3,11},{4,12},{5,13},{6,14},{7,15},{8,0},{9,1},... | collective-permute-start | bytes 1179656 | tf_op jit(solution)/shard_map/ppermute | solution.py:355
  112.4 11.0 %collective-permute-start.16 = (bf16[384,512]{1,0:T(8,128)(2,1)S(1)}, bf16[384,512]{1,0:T(8,128)(2,1)S(1)}, u32[]{:S(2)}, u32[]{:S(2)}) collective-permute-start(bf16[384,512]{1,0:T(8,128)(2,1)S(1)} %newton_schulz.3.rest_0_), channel_id=1, source_target_pairs={{0,4},{1,3},{2,6},{3,1},{4,0},{5,7},{6,2},{7,5},{8,12},{9,11},{10,... | collective-permute-start | bytes 1179656 | tf_op jit(solution)/shard_map/ppermute | solution.py:355
  113.9 10.1 %collective-permute-start.17 = (bf16[384,512]{1,0:T(8,128)(2,1)S(1)}, bf16[384,512]{1,0:T(8,128)(2,1)S(1)}, u32[]{:S(2)}, u32[]{:S(2)}) collective-permute-start(bf16[384,512]{1,0:T(8,128)(2,1)S(1)} %newton_schulz.3.rest_0_), channel_id=1, source_target_pairs={{0,2},{1,5},{2,0},{3,7},{4,6},{5,1},{6,4},{7,3},{8,10},{9,13},{10,... | collective-permute-start | bytes 1179656 | tf_op jit(solution)/shard_map/ppermute | solution.py:355
  116.6 12.4 %collective-permute-start.18 = (bf16[384,512]{1,0:T(8,128)(2,1)S(1)}, bf16[384,512]{1,0:T(8,128)(2,1)S(1)}, u32[]{:S(2)}, u32[]{:S(2)}) collective-permute-start(bf16[384,512]{1,0:T(8,128)(2,1)S(1)} %newton_schulz.3.rest_0_), channel_id=1, source_target_pairs={{0,8},{1,9},{2,10},{3,11},{4,12},{5,13},{6,14},{7,15},{8,0},{9,1},... | collective-permute-start | bytes 1179656 | tf_op jit(solution)/shard_map/ppermute | solution.py:355
  116.6 12.4 %collective-permute-start.19 = (bf16[384,512]{1,0:T(8,128)(2,1)S(1)}, bf16[384,512]{1,0:T(8,128)(2,1)S(1)}, u32[]{:S(2)}, u32[]{:S(2)}) collective-permute-start(bf16[384,512]{1,0:T(8,128)(2,1)S(1)} %collective-permute-done.15.rest_8_), channel_id=1, source_target_pairs={{0,2},{1,5},{2,0},{3,7},{4,6},{5,1},{6,4},{7,3},{8,10},{9,13},{10,... | collective-permute-start | bytes 1179656 | tf_op jit(solution)/shard_map/ppermute | solution.py:355
  120.6 11.8 %collective-permute-start.21 = (bf16[384,512]{1,0:T(8,128)(2,1)S(1)}, bf16[384,512]{1,0:T(8,128)(2,1)S(1)}, u32[]{:S(2)}, u32[]{:S(2)}) collective-permute-start(bf16[384,512]{1,0:T(8,128)(2,1)S(1)} %collective-permute-done.20.rest_9_), channel_id=1, source_target_pairs={{0,2},{1,5},{2,0},{3,7},{4,6},{5,1},{6,4},{7,3},{8,10},{9,13},{10,... | collective-permute-start | bytes 1179656 | tf_op jit(solution)/shard_map/ppermute | solution.py:355
  123.4 9.3 %collective-permute-start.33 = (bf16[384,512]{1,0:T(8,128)(2,1)S(1)}, bf16[384,512]{1,0:T(8,128)(2,1)S(1)}, u32[]{:S(2)}, u32[]{:S(2)}) collective-permute-start(bf16[384,512]{1,0:T(8,128)(2,1)S(1)} %newton_schulz.2.rest_0_), channel_id=1, source_target_pairs={{0,1},{1,0},{2,3},{3,2},{4,5},{5,4},{6,7},{7,6},{8,9},{9,8},{10,11... | collective-permute-start | bytes 1179656 | tf_op jit(solution)/shard_map/ppermute | solution.py:355
  124.0 8.9 %collective-permute-start.34 = (bf16[384,512]{1,0:T(8,128)(2,1)S(1)}, bf16[384,512]{1,0:T(8,128)(2,1)S(1)}, u32[]{:S(2)}, u32[]{:S(2)}) collective-permute-start(bf16[384,512]{1,0:T(8,128)(2,1)S(1)} %collective-permute-done.9.rest_1_), channel_id=1, source_target_pairs={{0,1},{1,0},{2,3},{3,2},{4,5},{5,4},{6,7},{7,6},{8,9},{9,8},{10,11... | collective-permute-start | bytes 1179656 | tf_op jit(solution)/shard_map/ppermute | solution.py:355
  133.0 11.3 %collective-permute-start.22 = (bf16[384,512]{1,0:T(8,128)(2,1)S(1)}, bf16[384,512]{1,0:T(8,128)(2,1)S(1)}, u32[]{:S(2)}, u32[]{:S(2)}) collective-permute-start(bf16[384,512]{1,0:T(8,128)(2,1)S(1)} %collective-permute-done.16.rest_1_), channel_id=1, source_target_pairs={{0,8},{1,9},{2,10},{3,11},{4,12},{5,13},{6,14},{7,15},{8,0},{9,1},... | collective-permute-start | bytes 1179656 | tf_op jit(solution)/shard_map/ppermute | solution.py:355
  133.5 11.8 %collective-permute-start.23 = (bf16[384,512]{1,0:T(8,128)(2,1)S(1)}, bf16[384,512]{1,0:T(8,128)(2,1)S(1)}, u32[]{:S(2)}, u32[]{:S(2)}) collective-permute-start(bf16[384,512]{1,0:T(8,128)(2,1)S(1)} %collective-permute-done.17.rest_2_), channel_id=1, source_target_pairs={{0,4},{1,3},{2,6},{3,1},{4,0},{5,7},{6,2},{7,5},{8,12},{9,11},{10,... | collective-permute-start | bytes 1179656 | tf_op jit(solution)/shard_map/ppermute | solution.py:355
  134.9 10.4 %collective-permute-start.24 = (bf16[384,512]{1,0:T(8,128)(2,1)S(1)}, bf16[384,512]{1,0:T(8,128)(2,1)S(1)}, u32[]{:S(2)}, u32[]{:S(2)}) collective-permute-start(bf16[384,512]{1,0:T(8,128)(2,1)S(1)} %collective-permute-done.18.rest_8_), channel_id=1, source_target_pairs={{0,2},{1,5},{2,0},{3,7},{4,6},{5,1},{6,4},{7,3},{8,10},{9,13},{10,... | collective-permute-start | bytes 1179656 | tf_op jit(solution)/shard_map/ppermute | solution.py:355
  136.0 9.9 %collective-permute-start.26 = (bf16[384,512]{1,0:T(8,128)(2,1)S(1)}, bf16[384,512]{1,0:T(8,128)(2,1)S(1)}, u32[]{:S(2)}, u32[]{:S(2)}) collective-permute-start(bf16[384,512]{1,0:T(8,128)(2,1)S(1)} %newton_schulz.3.rest_0_), channel_id=1, source_target_pairs={{0,1},{1,0},{2,3},{3,2},{4,5},{5,4},{6,7},{7,6},{8,9},{9,8},{10,11... | collective-permute-start | bytes 1179656 | tf_op jit(solution)/shard_map/ppermute | solution.py:355
  136.0 9.9 %collective-permute-start.39 = (bf16[384,512]{1,0:T(8,128)(2,1)S(1)}, bf16[384,512]{1,0:T(8,128)(2,1)S(1)}, u32[]{:S(2)}, u32[]{:S(2)}) collective-permute-start(bf16[384,512]{1,0:T(8,128)(2,1)S(1)} %collective-permute-done.19.rest_10_), channel_id=1, source_target_pairs={{0,1},{1,0},{2,3},{3,2},{4,5},{5,4},{6,7},{7,6},{8,9},{9,8},{10,11... | collective-permute-start | bytes 1179656 | tf_op jit(solution)/shard_map/ppermute | solution.py:355
  145.8 6.4 %collective-permute-start.30 = (bf16[384,512]{1,0:T(8,128)(2,1)S(1)}, bf16[384,512]{1,0:T(8,128)(2,1)S(1)}, u32[]{:S(2)}, u32[]{:S(2)}) collective-permute-start(bf16[384,512]{1,0:T(8,128)(2,1)S(1)} %collective-permute-done.18.rest_8_), channel_id=1, source_target_pairs={{0,1},{1,0},{2,3},{3,2},{4,5},{5,4},{6,7},{7,6},{8,9},{9,8},{10,11... | collective-permute-start | bytes 1179656 | tf_op jit(solution)/shard_map/ppermute | solution.py:355
  145.9 6.3 %collective-permute-start.29 = (bf16[384,512]{1,0:T(8,128)(2,1)S(1)}, bf16[384,512]{1,0:T(8,128)(2,1)S(1)}, u32[]{:S(2)}, u32[]{:S(2)}) collective-permute-start(bf16[384,512]{1,0:T(8,128)(2,1)S(1)} %collective-permute-done.23.rest_3_), channel_id=1, source_target_pairs={{0,1},{1,0},{2,3},{3,2},{4,5},{5,4},{6,7},{7,6},{8,9},{9,8},{10,11... | collective-permute-start | bytes 1179656 | tf_op jit(solution)/shard_map/ppermute | solution.py:355
  147.6 7.9 %collective-permute-start.25 = (bf16[384,512]{1,0:T(8,128)(2,1)S(1)}, bf16[384,512]{1,0:T(8,128)(2,1)S(1)}, u32[]{:S(2)}, u32[]{:S(2)}) collective-permute-start(bf16[384,512]{1,0:T(8,128)(2,1)S(1)} %collective-permute-done.22.rest_9_), channel_id=1, source_target_pairs={{0,2},{1,5},{2,0},{3,7},{4,6},{5,1},{6,4},{7,3},{8,10},{9,13},{10,... | collective-permute-start | bytes 1179656 | tf_op jit(solution)/shard_map/ppermute | solution.py:355
  (27 other events, 72.6 us)

commit v6 on v5

--- a/solution.py
+++ b/solution.py
@@ -155,11 +155,10 @@
     )(keys, values, rates, *follows)
 
 
-def grads_kernel(scale_one, scale_two, where_ref, wg_ref, wu_ref, wd_ref, blocks, *rest):
+def grads_kernel(scale_one, scale_two, where_ref, w_ref, blocks, *rest):
     keep, *send = rest[-7:-3]
     total, final, sem = rest[-3:]
-    wg, wu = wg_ref[...], wu_ref[...]
-    wdt = jnp.transpose(wd_ref[...])
+    wg, wu, wdt = w_ref[0], w_ref[1], w_ref[2]
     for b in range(0, PLANE, 2):
         k = blocks[b : b + 2, 0].reshape(2 * blocks.shape[2], blocks.shape[3])
         vr = blocks[b : b + 2, 1].reshape(2 * blocks.shape[2], blocks.shape[3])
@@ -198,12 +197,12 @@
 
 
 def head_grads(where, blocks, weights, *follows):
-    size, hidden = weights[0].shape
+    _, size, hidden = weights[0].shape
     return pl.pallas_call(
         functools.partial(grads_kernel, size**-0.5, hidden**-0.5),
         out_shape=[jax.ShapeDtypeStruct((size + size // 2, hidden), BF)]
         + [jax.ShapeDtypeStruct((size // 2, hidden), BF)] * 3,
-        in_specs=[SMEM] + [VMEM] * 4 + [ANY] * len(follows),
+        in_specs=[SMEM] + [VMEM] * 2 + [ANY] * len(follows),
         out_specs=[ANY] * 4,
         scratch_shapes=[
             pltpu.VMEM((3, size, hidden), F32),
@@ -369,10 +368,13 @@
 
     packed = [pack_tokens(keys, values, token_rates, 0, size)]
     applied = apply_queries(queries, w_gate, w_up, w_down)
-    weights = [
-        [lax.dynamic_index_in_dim(w, g * PLANE + where[0], 0, False) for w in (w_gate, w_up, w_down)]
-        for g in range(groups)
-    ]
+    weights = []
+    for group in range(groups):
+        gate, up, down = (
+            lax.dynamic_index_in_dim(w, group * PLANE + where[0], 0, False)
+            for w in (w_gate, w_up, w_down)
+        )
+        weights.append((jnp.stack([gate, up, jnp.transpose(down)]),))
     packed.append(pack_tokens(keys, values, token_rates, 1, size, applied, *weights[0], *weights[1]))
     received = [
         lax.all_to_all(block, "seq", 0, 0, axis_index_groups=CUBES, tiled=True)

time: 159 us -> 159 us (level)
  waiting for transfers between devices: 64.1 us -> 61.6 us
    all_to_all x2, waiting for transfers between devices: 28.6 us -> 25.7 us  [per_device_fast(): lax.all_to_all(block, 'seq', 0, 0, axis_index_groups=CUBES, tiled=True)]
    dynamic_slice x0 -> x4, local copies, waits for them, and re-layouts: none -> 2.61 us  [per_device_fast(): lax.dynamic_index_in_dim(w, group * PLANE + where[0], 0, False)]
    squeeze x2 -> x0, local copies, waits for them, and re-layouts: 2.48 us -> none  [per_device_fast(): lax.dynamic_index_in_dim(w, g * PLANE + where[0], 0, False)]
  transfers between devices with their start and end apart: 44 -> 44, of which waited for: 21 -> 22; matrix products, arithmetic and copies ran while one was open for 2% -> 2% of each run, Pallas kernels for 25% -> 25%
where the time goes in v6:
time: 159 us; the launch traced here: 158 us
  waiting for transfers between devices  61.6 us (39%)
  Pallas kernels  44.2 us (28%)
  starting transfers between devices  40.6 us (26%)
  local copies, waits for them, and re-layouts  9.48 us (6%)
    ppermute x42, waiting for transfers between devices, move(): return lax.ppermute(array, 'seq', pairs)  35.9 us
    ppermute x42, starting transfers between devices, move(): return lax.ppermute(array, 'seq', pairs)  29.3 us
    all_to_all x2, waiting for transfers between devices, per_device_fast(): lax.all_to_all(block, 'seq', 0, 0, axis_index_groups=CUBES, tiled=True)  25.7 us
    pallas_call x2, Pallas kernels, head_grads(): pl.pallas_call(functools.partial(grads_kernel, size ** (-0.5), hidden **...  13.6 us
    all_to_all x2, starting transfers between devices, per_device_fast(): lax.all_to_all(block, 'seq', 0, 0, axis_index_groups=CUBES, tiled=True)  11.3 us
    pallas_call x1, Pallas kernels, apply_queries(): pl.pallas_call(functools.partial(applied_kernel, size ** (-0.5), hidden *...  9.34 us
    pallas_call x2, Pallas kernels, newton(): pl.pallas_call(newton_kernel, out_shape=jax.ShapeDtypeStruct((rows, hidde...  8.3 us
    pallas_call x3, Pallas kernels, place(): pl.pallas_call(functools.partial(place_kernel, group, which, shape[1]), o...  8.1 us
  transfers between devices with their start and end apart: 44, of which 22 were waited for; matrix products, arithmetic and copies ran while one was open for 2% of the time, Pallas kernels for 25%

profile of v6, /device:TPU:0, one launch (start us, length us, event | category | flops | bytes accessed | tf_op | source)
XLA Modules:
  0.0 158.0 jit_solution(15532249130632231165)
XLA Ops:
  0.6 3.0 %pack_tokens.3 = bf16[8,2,256,256]{3,2,1,0:T(8,128)(2,1)} custom-call(bf16[256,4096]{1,0:T(8,128)(2,1)} %k_ref.3, bf16[256,4096]{1,0:T(8,128)(2,1)} %v_ref.3, f32[16,256]{1,0:T(8,128)} %rate_ref.3), custom_call_target="tpu_custom_call" | custom-call | flops 1 | bytes 1 | tf_op jit(solution)/shard_map/pack_tokens/pallas_call | solution.py:141
  3.6 6.2 %all-to-all-start.1 = ((bf16[8,2,256,256]{3,2,1,0:T(8,128)(2,1)}), bf16[8,2,256,256]{3,2,1,0:T(8,128)(2,1)}, u32[]{:S(2)}, u32[]{:S(2)}) async-start(bf16[8,2,256,256]{3,2,1,0:T(8,128)(2,1)} %pack_tokens.3), calls=%async_computation.1 | async-start | bytes 4194304 | tf_op jit(solution)/shard_map/all_to_all | solution.py:380
  13.5 9.3 %apply_queries.1.rest_0_ = bf16[256,4096]{1,0:T(8,128)(2,1)} custom-call(bf16[256,4096]{1,0:T(8,128)(2,1)} %q_ref.1, bf16[16,256,512]{2,1,0:T(8,128)(2,1)} %wg_ref.1, bf16[16,256,512]{2,1,0:T(8,128)(2,1)} %wu_ref.1, bf16[16,512,256]{2,1,0:T(8,128)(2,1)} %wd_ref.1), custom_call_target="tpu_custom_call" | custom-call | flops 1 | bytes 1 | tf_op jit(solution)/shard_map/apply_queries/pallas_call | solution.py:107
  24.5 1.6 %copy-done.3 = bf16[256,4096]{1,0:T(8,128)(2,1)S(1)} copy-done((bf16[256,4096]{1,0:T(8,128)(2,1)S(1)}, bf16[256,4096]{1,0:T(8,128)(2,1)}, u32[]{:S(2)}) %copy-start.3) | copy-done | bytes 2097176
  29.4 6.4 %all-to-all-done.1.blocks = bf16[8,2,256,256]{3,2,1,0:T(8,128)(2,1)} async-done(((bf16[8,2,256,256]{3,2,1,0:T(8,128)(2,1)}), bf16[8,2,256,256]{3,2,1,0:T(8,128)(2,1)}, u32[]{:S(2)}, u32[]{:S(2)}) %all-to-all-start.1) | async-done | bytes 2097184 | tf_op jit(solution)/shard_map/all_to_all | solution.py:380
  35.9 5.1 %all-to-all-start = ((bf16[8,2,256,256]{3,2,1,0:T(8,128)(2,1)}), bf16[8,2,256,256]{3,2,1,0:T(8,128)(2,1)S(1)}, u32[]{:S(2)}, u32[]{:S(2)}) async-start(bf16[8,2,256,256]{3,2,1,0:T(8,128)(2,1)} %copy-done.2), calls=%async_computation | async-start | bytes 4194304 | tf_op jit(solution)/shard_map/all_to_all | solution.py:380
  42.2 7.2 %head_grads.2 = (bf16[384,512]{1,0:T(8,128)(2,1)S(1)}, bf16[128,512]{1,0:T(8,128)(2,1)S(1)}, bf16[128,512]{1,0:T(8,128)(2,1)S(1)}, bf16[128,512]{1,0:T(8,128)(2,1)S(1)}) custom-call(s32[5]{0:T(128)S(1)} %stack.39.where_ref, bf16[3,256,512]{2,1,0:T(8,128)(2,1)S(1)} %copy-done.5, bf16[8,2,256,256]{3,2,1,0:T(8,128)(2,1)} %all-to-all-done.1.blocks), custom_call_target="tpu_custom_call" | custom-call | flops 1 | bytes 1 | tf_op jit(solution)/shard_map/head_grads/pallas_call | solution.py:201
  52.1 2.6 %collective-permute-start.6 = (bf16[384,512]{1,0:T(8,128)(2,1)}, bf16[384,512]{1,0:T(8,128)(2,1)S(1)}, u32[]{:S(2)}, u32[]{:S(2)}) collective-permute-start(bf16[384,512]{1,0:T(8,128)(2,1)} %get-tuple-element.47.rest_0_), channel_id=1, source_target_pairs={{0,16},{1,17},{2,18},{3,19},{4,20},{5,21},{6,22},{7,23},{8,24},{9,... | collective-permute-start | bytes 1179656 | tf_op jit(solution)/shard_map/ppermute | solution.py:354
  54.7 19.3 %all-to-all-done.blocks = bf16[8,2,256,256]{3,2,1,0:T(8,128)(2,1)S(1)} async-done(((bf16[8,2,256,256]{3,2,1,0:T(8,128)(2,1)}), bf16[8,2,256,256]{3,2,1,0:T(8,128)(2,1)S(1)}, u32[]{:S(2)}, u32[]{:S(2)}) %all-to-all-start) | async-done | bytes 2097184 | tf_op jit(solution)/shard_map/all_to_all | solution.py:380
  74.0 6.4 %head_grads.3 = (bf16[384,512]{1,0:T(8,128)(2,1)S(1)}, bf16[128,512]{1,0:T(8,128)(2,1)S(1)}, bf16[128,512]{1,0:T(8,128)(2,1)S(1)}, bf16[128,512]{1,0:T(8,128)(2,1)S(1)}) custom-call(s32[5]{0:T(128)S(1)} %stack.39.where_ref, bf16[3,256,512]{2,1,0:T(8,128)(2,1)S(1)} %pad_maximum_fusion.rest_2_.w_ref, bf16[8,2,256,256]{3,2,1,0:T(8,128)(2,1)S(1)} %all-to-all-done.blocks, ...), custom_call_target="tpu_custom_call" | custom-call | flops 1 | bytes 1 | tf_op jit(solution)/shard_map/head_grads/pallas_call | solution.py:201
  83.0 4.4 %newton_schulz.2.rest_0_ = bf16[384,512]{1,0:T(8,128)(2,1)S(1)} custom-call(s32[5]{0:T(128)S(1)} %stack.39.where_ref, bf16[384,512]{1,0:T(8,128)(2,1)} %get-tuple-element.47.rest_0_, bf16[384,512]{1,0:T(8,128)(2,1)S(1)} %collective-permute-done.6.rest_0_.rest_1_, bf16[128,512]{1,0:T(8,128)(2,1)S(1)} %collective-permute-done.7.rest_2_, ...), custom_call_target="tpu_custom_call" | custom-call | flops 1 | bytes 1 | tf_op jit(solution)/shard_map/newton_schulz/pallas_call | solution.py:275
  87.4 3.7 %collective-permute-start.10 = (bf16[384,512]{1,0:T(8,128)(2,1)S(1)}, bf16[384,512]{1,0:T(8,128)(2,1)S(1)}, u32[]{:S(2)}, u32[]{:S(2)}) collective-permute-start(bf16[384,512]{1,0:T(8,128)(2,1)S(1)} %newton_schulz.2.rest_0_), channel_id=1, source_target_pairs={{0,2},{1,5},{2,0},{3,7},{4,6},{5,1},{6,4},{7,3},{8,10},{9,13},{10,... | collective-permute-start | bytes 1179656 | tf_op jit(solution)/shard_map/ppermute | solution.py:354
  92.5 2.4 %collective-permute-start.15 = (bf16[384,512]{1,0:T(8,128)(2,1)S(1)}, bf16[384,512]{1,0:T(8,128)(2,1)S(1)}, u32[]{:S(2)}, u32[]{:S(2)}) collective-permute-start(bf16[384,512]{1,0:T(8,128)(2,1)S(1)} %newton_schulz.2.rest_0_), channel_id=1, source_target_pairs={{0,8},{1,9},{2,10},{3,11},{4,12},{5,13},{6,14},{7,15},{8,0},{9,1},... | collective-permute-start | bytes 1179656 | tf_op jit(solution)/shard_map/ppermute | solution.py:354
  94.9 8.0 %collective-permute-done.11.rest_1_ = bf16[384,512]{1,0:T(8,128)(2,1)S(1)} collective-permute-done((bf16[384,512]{1,0:T(8,128)(2,1)S(1)}, bf16[384,512]{1,0:T(8,128)(2,1)S(1)}, u32[]{:S(2)}, u32[]{:S(2)}) %collective-permute-start.11) | collective-permute-done | bytes 393248 | tf_op jit(solution)/shard_map/ppermute | solution.py:354
  104.1 2.0 %collective-permute-start.12 = (bf16[128,512]{1,0:T(8,128)(2,1)S(1)}, bf16[128,512]{1,0:T(8,128)(2,1)S(1)}, u32[]{:S(2)}, u32[]{:S(2)}) collective-permute-start(bf16[128,512]{1,0:T(8,128)(2,1)S(1)} %get-tuple-element.55), channel_id=1, source_target_pairs={{0,1},{1,0},{2,3},{3,2},{4,5},{5,4},{6,7},{7,6},{8,9},{9,8},{10,11... | collective-permute-start | bytes 393224 | tf_op jit(solution)/shard_map/ppermute | solution.py:354
  107.5 3.9 %newton_schulz.3.rest_0_ = bf16[384,512]{1,0:T(8,128)(2,1)S(1)} custom-call(s32[5]{0:T(128)S(1)} %stack.39.where_ref, bf16[384,512]{1,0:T(8,128)(2,1)S(1)} %get-tuple-element.52.rest_4_.rest_0_, bf16[384,512]{1,0:T(8,128)(2,1)S(1)} %collective-permute-done.11.rest_1_, bf16[128,512]{1,0:T(8,128)(2,1)S(1)} %collective-permute-done.12.rest_2_, ...), custom_call_target="tpu_custom_call" | custom-call | flops 1 | bytes 1 | tf_op jit(solution)/shard_map/newton_schulz/pallas_call | solution.py:275
  113.0 2.6 %collective-permute-start.17 = (bf16[384,512]{1,0:T(8,128)(2,1)S(1)}, bf16[384,512]{1,0:T(8,128)(2,1)S(1)}, u32[]{:S(2)}, u32[]{:S(2)}) collective-permute-start(bf16[384,512]{1,0:T(8,128)(2,1)S(1)} %newton_schulz.3.rest_0_), channel_id=1, source_target_pairs={{0,2},{1,5},{2,0},{3,7},{4,6},{5,1},{6,4},{7,3},{8,10},{9,13},{10,... | collective-permute-start | bytes 1179656 | tf_op jit(solution)/shard_map/ppermute | solution.py:354
  115.8 3.9 %collective-permute-done.20.rest_9_ = bf16[384,512]{1,0:T(8,128)(2,1)S(1)} collective-permute-done((bf16[384,512]{1,0:T(8,128)(2,1)S(1)}, bf16[384,512]{1,0:T(8,128)(2,1)S(1)}, u32[]{:S(2)}, u32[]{:S(2)}) %collective-permute-start.20) | collective-permute-done | bytes 393248 | tf_op jit(solution)/shard_map/ppermute | solution.py:354
  119.7 1.8 %collective-permute-start.21 = (bf16[384,512]{1,0:T(8,128)(2,1)S(1)}, bf16[384,512]{1,0:T(8,128)(2,1)S(1)}, u32[]{:S(2)}, u32[]{:S(2)}) collective-permute-start(bf16[384,512]{1,0:T(8,128)(2,1)S(1)} %collective-permute-done.20.rest_9_), channel_id=1, source_target_pairs={{0,2},{1,5},{2,0},{3,7},{4,6},{5,1},{6,4},{7,3},{8,10},{9,13},{10,... | collective-permute-start | bytes 1179656 | tf_op jit(solution)/shard_map/ppermute | solution.py:354
  123.7 4.4 %collective-permute-done.18.rest_8_ = bf16[384,512]{1,0:T(8,128)(2,1)S(1)} collective-permute-done((bf16[384,512]{1,0:T(8,128)(2,1)S(1)}, bf16[384,512]{1,0:T(8,128)(2,1)S(1)}, u32[]{:S(2)}, u32[]{:S(2)}) %collective-permute-start.18) | collective-permute-done | bytes 393248 | tf_op jit(solution)/shard_map/ppermute | solution.py:354
  128.6 3.0 %collective-permute-done.21.rest_11_ = bf16[384,512]{1,0:T(8,128)(2,1)S(1)} collective-permute-done((bf16[384,512]{1,0:T(8,128)(2,1)S(1)}, bf16[384,512]{1,0:T(8,128)(2,1)S(1)}, u32[]{:S(2)}, u32[]{:S(2)}) %collective-permute-start.21) | collective-permute-done | bytes 393248 | tf_op jit(solution)/shard_map/ppermute | solution.py:354
  135.6 7.8 %collective-permute-done.22.rest_9_ = bf16[384,512]{1,0:T(8,128)(2,1)S(1)} collective-permute-done((bf16[384,512]{1,0:T(8,128)(2,1)S(1)}, bf16[384,512]{1,0:T(8,128)(2,1)S(1)}, u32[]{:S(2)}, u32[]{:S(2)}) %collective-permute-start.22) | collective-permute-done | bytes 393248 | tf_op jit(solution)/shard_map/ppermute | solution.py:354
  147.9 3.4 %place_steps.3 = (bf16[16,256,512]{2,1,0:T(8,128)(2,1)}, bf16[16,256,512]{2,1,0:T(8,128)(2,1)}, bf16[16,256,512]{2,1,0:T(8,128)(2,1)}) custom-call(s32[5]{0:T(128)S(1)} %stack.39.where_ref, bf16[384,512]{1,0:T(8,128)(2,1)S(1)} %newton_schulz.2.rest_0_, bf16[384,512]{1,0:T(8,128)(2,1)S(1)} %collective-permute-done.9.rest_1_, ...), custom_call_target="tpu_custom_call" | custom-call | flops 1 | bytes 1 | tf_op jit(solution)/shard_map/place_steps/pallas_call | solution.py:321
  151.4 3.2 %place_steps.4 = (bf16[16,256,512]{2,1,0:T(8,128)(2,1)}, bf16[16,256,512]{2,1,0:T(8,128)(2,1)}, bf16[16,256,512]{2,1,0:T(8,128)(2,1)}) custom-call(s32[5]{0:T(128)S(1)} %stack.39.where_ref, bf16[384,512]{1,0:T(8,128)(2,1)S(1)} %newton_schulz.3.rest_0_, ...), custom_call_target="tpu_custom_call", output_to_operand_aliasing={{0}: (15, {}), {1}: (16, {}), {2}: (17, {})} | custom-call | flops 1 | bytes 1 | tf_op jit(solution)/shard_map/place_steps/pallas_call | solution.py:321
  (99 shorter events, 35.3 us)
Async XLA Ops:
  3.6 32.2 %all-to-all-start.1 = ((bf16[8,2,256,256]{3,2,1,0:T(8,128)(2,1)}), bf16[8,2,256,256]{3,2,1,0:T(8,128)(2,1)}, u32[]{:S(2)}, u32[]{:S(2)}) async-start(bf16[8,2,256,256]{3,2,1,0:T(8,128)(2,1)} %pack_tokens.3), calls=%async_computation.1 | async-start | bytes 4194304 | tf_op jit(solution)/shard_map/all_to_all | solution.py:380
  35.9 38.1 %all-to-all-start = ((bf16[8,2,256,256]{3,2,1,0:T(8,128)(2,1)}), bf16[8,2,256,256]{3,2,1,0:T(8,128)(2,1)S(1)}, u32[]{:S(2)}, u32[]{:S(2)}) async-start(bf16[8,2,256,256]{3,2,1,0:T(8,128)(2,1)} %copy-done.2), calls=%async_computation | async-start | bytes 4194304 | tf_op jit(solution)/shard_map/all_to_all | solution.py:380
  52.1 29.4 %collective-permute-start.6 = (bf16[384,512]{1,0:T(8,128)(2,1)}, bf16[384,512]{1,0:T(8,128)(2,1)S(1)}, u32[]{:S(2)}, u32[]{:S(2)}) collective-permute-start(bf16[384,512]{1,0:T(8,128)(2,1)} %get-tuple-element.47.rest_0_), channel_id=1, source_target_pairs={{0,16},{1,17},{2,18},{3,19},{4,20},{5,21},{6,22},{7,23},{8,24},{9,... | collective-permute-start | bytes 1179656 | tf_op jit(solution)/shard_map/ppermute | solution.py:354
  82.5 20.4 %collective-permute-start.11 = (bf16[384,512]{1,0:T(8,128)(2,1)S(1)}, bf16[384,512]{1,0:T(8,128)(2,1)S(1)}, u32[]{:S(2)}, u32[]{:S(2)}) collective-permute-start(bf16[384,512]{1,0:T(8,128)(2,1)S(1)} %get-tuple-element.52.rest_4_.rest_0_), channel_id=1, source_target_pairs={{0,16},{1,17},{2,18},{3,19},{4,20},{5,21},{6,22},{7,23},{8,24},{9,... | collective-permute-start | bytes 1179656 | tf_op jit(solution)/shard_map/ppermute | solution.py:354
  87.4 15.5 %collective-permute-start.10 = (bf16[384,512]{1,0:T(8,128)(2,1)S(1)}, bf16[384,512]{1,0:T(8,128)(2,1)S(1)}, u32[]{:S(2)}, u32[]{:S(2)}) collective-permute-start(bf16[384,512]{1,0:T(8,128)(2,1)S(1)} %newton_schulz.2.rest_0_), channel_id=1, source_target_pairs={{0,2},{1,5},{2,0},{3,7},{4,6},{5,1},{6,4},{7,3},{8,10},{9,13},{10,... | collective-permute-start | bytes 1179656 | tf_op jit(solution)/shard_map/ppermute | solution.py:354
  91.1 11.8 %collective-permute-start.9 = (bf16[384,512]{1,0:T(8,128)(2,1)S(1)}, bf16[384,512]{1,0:T(8,128)(2,1)S(1)}, u32[]{:S(2)}, u32[]{:S(2)}) collective-permute-start(bf16[384,512]{1,0:T(8,128)(2,1)S(1)} %newton_schulz.2.rest_0_), channel_id=1, source_target_pairs={{0,4},{1,3},{2,6},{3,1},{4,0},{5,7},{6,2},{7,5},{8,12},{9,11},{10,... | collective-permute-start | bytes 1179656 | tf_op jit(solution)/shard_map/ppermute | solution.py:354
  92.5 18.9 %collective-permute-start.15 = (bf16[384,512]{1,0:T(8,128)(2,1)S(1)}, bf16[384,512]{1,0:T(8,128)(2,1)S(1)}, u32[]{:S(2)}, u32[]{:S(2)}) collective-permute-start(bf16[384,512]{1,0:T(8,128)(2,1)S(1)} %newton_schulz.2.rest_0_), channel_id=1, source_target_pairs={{0,8},{1,9},{2,10},{3,11},{4,12},{5,13},{6,14},{7,15},{8,0},{9,1},... | collective-permute-start | bytes 1179656 | tf_op jit(solution)/shard_map/ppermute | solution.py:354
  102.9 8.6 %collective-permute-start.14 = (bf16[384,512]{1,0:T(8,128)(2,1)S(1)}, bf16[384,512]{1,0:T(8,128)(2,1)S(1)}, u32[]{:S(2)}, u32[]{:S(2)}) collective-permute-start(bf16[384,512]{1,0:T(8,128)(2,1)S(1)} %collective-permute-done.10.rest_2_), channel_id=1, source_target_pairs={{0,4},{1,3},{2,6},{3,1},{4,0},{5,7},{6,2},{7,5},{8,12},{9,11},{10,... | collective-permute-start | bytes 1179656 | tf_op jit(solution)/shard_map/ppermute | solution.py:354
  106.2 13.5 %collective-permute-start.20 = (bf16[384,512]{1,0:T(8,128)(2,1)S(1)}, bf16[384,512]{1,0:T(8,128)(2,1)S(1)}, u32[]{:S(2)}, u32[]{:S(2)}) collective-permute-start(bf16[384,512]{1,0:T(8,128)(2,1)S(1)} %collective-permute-done.9.rest_1_), channel_id=1, source_target_pairs={{0,8},{1,9},{2,10},{3,11},{4,12},{5,13},{6,14},{7,15},{8,0},{9,1},... | collective-permute-start | bytes 1179656 | tf_op jit(solution)/shard_map/ppermute | solution.py:354
  111.5 11.0 %collective-permute-start.16 = (bf16[384,512]{1,0:T(8,128)(2,1)S(1)}, bf16[384,512]{1,0:T(8,128)(2,1)S(1)}, u32[]{:S(2)}, u32[]{:S(2)}) collective-permute-start(bf16[384,512]{1,0:T(8,128)(2,1)S(1)} %newton_schulz.3.rest_0_), channel_id=1, source_target_pairs={{0,4},{1,3},{2,6},{3,1},{4,0},{5,7},{6,2},{7,5},{8,12},{9,11},{10,... | collective-permute-start | bytes 1179656 | tf_op jit(solution)/shard_map/ppermute | solution.py:354
  113.0 10.1 %collective-permute-start.17 = (bf16[384,512]{1,0:T(8,128)(2,1)S(1)}, bf16[384,512]{1,0:T(8,128)(2,1)S(1)}, u32[]{:S(2)}, u32[]{:S(2)}) collective-permute-start(bf16[384,512]{1,0:T(8,128)(2,1)S(1)} %newton_schulz.3.rest_0_), channel_id=1, source_target_pairs={{0,2},{1,5},{2,0},{3,7},{4,6},{5,1},{6,4},{7,3},{8,10},{9,13},{10,... | collective-permute-start | bytes 1179656 | tf_op jit(solution)/shard_map/ppermute | solution.py:354
  115.7 12.4 %collective-permute-start.18 = (bf16[384,512]{1,0:T(8,128)(2,1)S(1)}, bf16[384,512]{1,0:T(8,128)(2,1)S(1)}, u32[]{:S(2)}, u32[]{:S(2)}) collective-permute-start(bf16[384,512]{1,0:T(8,128)(2,1)S(1)} %newton_schulz.3.rest_0_), channel_id=1, source_target_pairs={{0,8},{1,9},{2,10},{3,11},{4,12},{5,13},{6,14},{7,15},{8,0},{9,1},... | collective-permute-start | bytes 1179656 | tf_op jit(solution)/shard_map/ppermute | solution.py:354
  115.7 12.4 %collective-permute-start.19 = (bf16[384,512]{1,0:T(8,128)(2,1)S(1)}, bf16[384,512]{1,0:T(8,128)(2,1)S(1)}, u32[]{:S(2)}, u32[]{:S(2)}) collective-permute-start(bf16[384,512]{1,0:T(8,128)(2,1)S(1)} %collective-permute-done.15.rest_8_), channel_id=1, source_target_pairs={{0,2},{1,5},{2,0},{3,7},{4,6},{5,1},{6,4},{7,3},{8,10},{9,13},{10,... | collective-permute-start | bytes 1179656 | tf_op jit(solution)/shard_map/ppermute | solution.py:354
  119.7 11.8 %collective-permute-start.21 = (bf16[384,512]{1,0:T(8,128)(2,1)S(1)}, bf16[384,512]{1,0:T(8,128)(2,1)S(1)}, u32[]{:S(2)}, u32[]{:S(2)}) collective-permute-start(bf16[384,512]{1,0:T(8,128)(2,1)S(1)} %collective-permute-done.20.rest_9_), channel_id=1, source_target_pairs={{0,2},{1,5},{2,0},{3,7},{4,6},{5,1},{6,4},{7,3},{8,10},{9,13},{10,... | collective-permute-start | bytes 1179656 | tf_op jit(solution)/shard_map/ppermute | solution.py:354
  122.5 9.3 %collective-permute-start.33 = (bf16[384,512]{1,0:T(8,128)(2,1)S(1)}, bf16[384,512]{1,0:T(8,128)(2,1)S(1)}, u32[]{:S(2)}, u32[]{:S(2)}) collective-permute-start(bf16[384,512]{1,0:T(8,128)(2,1)S(1)} %newton_schulz.2.rest_0_), channel_id=1, source_target_pairs={{0,1},{1,0},{2,3},{3,2},{4,5},{5,4},{6,7},{7,6},{8,9},{9,8},{10,11... | collective-permute-start | bytes 1179656 | tf_op jit(solution)/shard_map/ppermute | solution.py:354
  123.1 8.9 %collective-permute-start.34 = (bf16[384,512]{1,0:T(8,128)(2,1)S(1)}, bf16[384,512]{1,0:T(8,128)(2,1)S(1)}, u32[]{:S(2)}, u32[]{:S(2)}) collective-permute-start(bf16[384,512]{1,0:T(8,128)(2,1)S(1)} %collective-permute-done.9.rest_1_), channel_id=1, source_target_pairs={{0,1},{1,0},{2,3},{3,2},{4,5},{5,4},{6,7},{7,6},{8,9},{9,8},{10,11... | collective-permute-start | bytes 1179656 | tf_op jit(solution)/shard_map/ppermute | solution.py:354
  132.1 11.3 %collective-permute-start.22 = (bf16[384,512]{1,0:T(8,128)(2,1)S(1)}, bf16[384,512]{1,0:T(8,128)(2,1)S(1)}, u32[]{:S(2)}, u32[]{:S(2)}) collective-permute-start(bf16[384,512]{1,0:T(8,128)(2,1)S(1)} %collective-permute-done.16.rest_1_), channel_id=1, source_target_pairs={{0,8},{1,9},{2,10},{3,11},{4,12},{5,13},{6,14},{7,15},{8,0},{9,1},... | collective-permute-start | bytes 1179656 | tf_op jit(solution)/shard_map/ppermute | solution.py:354
  132.6 11.7 %collective-permute-start.23 = (bf16[384,512]{1,0:T(8,128)(2,1)S(1)}, bf16[384,512]{1,0:T(8,128)(2,1)S(1)}, u32[]{:S(2)}, u32[]{:S(2)}) collective-permute-start(bf16[384,512]{1,0:T(8,128)(2,1)S(1)} %collective-permute-done.17.rest_2_), channel_id=1, source_target_pairs={{0,4},{1,3},{2,6},{3,1},{4,0},{5,7},{6,2},{7,5},{8,12},{9,11},{10,... | collective-permute-start | bytes 1179656 | tf_op jit(solution)/shard_map/ppermute | solution.py:354
  134.0 10.4 %collective-permute-start.24 = (bf16[384,512]{1,0:T(8,128)(2,1)S(1)}, bf16[384,512]{1,0:T(8,128)(2,1)S(1)}, u32[]{:S(2)}, u32[]{:S(2)}) collective-permute-start(bf16[384,512]{1,0:T(8,128)(2,1)S(1)} %collective-permute-done.18.rest_8_), channel_id=1, source_target_pairs={{0,2},{1,5},{2,0},{3,7},{4,6},{5,1},{6,4},{7,3},{8,10},{9,13},{10,... | collective-permute-start | bytes 1179656 | tf_op jit(solution)/shard_map/ppermute | solution.py:354
  135.1 9.8 %collective-permute-start.26 = (bf16[384,512]{1,0:T(8,128)(2,1)S(1)}, bf16[384,512]{1,0:T(8,128)(2,1)S(1)}, u32[]{:S(2)}, u32[]{:S(2)}) collective-permute-start(bf16[384,512]{1,0:T(8,128)(2,1)S(1)} %newton_schulz.3.rest_0_), channel_id=1, source_target_pairs={{0,1},{1,0},{2,3},{3,2},{4,5},{5,4},{6,7},{7,6},{8,9},{9,8},{10,11... | collective-permute-start | bytes 1179656 | tf_op jit(solution)/shard_map/ppermute | solution.py:354
  135.1 9.9 %collective-permute-start.39 = (bf16[384,512]{1,0:T(8,128)(2,1)S(1)}, bf16[384,512]{1,0:T(8,128)(2,1)S(1)}, u32[]{:S(2)}, u32[]{:S(2)}) collective-permute-start(bf16[384,512]{1,0:T(8,128)(2,1)S(1)} %collective-permute-done.19.rest_10_), channel_id=1, source_target_pairs={{0,1},{1,0},{2,3},{3,2},{4,5},{5,4},{6,7},{7,6},{8,9},{9,8},{10,11... | collective-permute-start | bytes 1179656 | tf_op jit(solution)/shard_map/ppermute | solution.py:354
  144.9 6.4 %collective-permute-start.30 = (bf16[384,512]{1,0:T(8,128)(2,1)S(1)}, bf16[384,512]{1,0:T(8,128)(2,1)S(1)}, u32[]{:S(2)}, u32[]{:S(2)}) collective-permute-start(bf16[384,512]{1,0:T(8,128)(2,1)S(1)} %collective-permute-done.18.rest_8_), channel_id=1, source_target_pairs={{0,1},{1,0},{2,3},{3,2},{4,5},{5,4},{6,7},{7,6},{8,9},{9,8},{10,11... | collective-permute-start | bytes 1179656 | tf_op jit(solution)/shard_map/ppermute | solution.py:354
  145.0 6.4 %collective-permute-start.29 = (bf16[384,512]{1,0:T(8,128)(2,1)S(1)}, bf16[384,512]{1,0:T(8,128)(2,1)S(1)}, u32[]{:S(2)}, u32[]{:S(2)}) collective-permute-start(bf16[384,512]{1,0:T(8,128)(2,1)S(1)} %collective-permute-done.23.rest_3_), channel_id=1, source_target_pairs={{0,1},{1,0},{2,3},{3,2},{4,5},{5,4},{6,7},{7,6},{8,9},{9,8},{10,11... | collective-permute-start | bytes 1179656 | tf_op jit(solution)/shard_map/ppermute | solution.py:354
  146.7 7.9 %collective-permute-start.25 = (bf16[384,512]{1,0:T(8,128)(2,1)S(1)}, bf16[384,512]{1,0:T(8,128)(2,1)S(1)}, u32[]{:S(2)}, u32[]{:S(2)}) collective-permute-start(bf16[384,512]{1,0:T(8,128)(2,1)S(1)} %collective-permute-done.22.rest_9_), channel_id=1, source_target_pairs={{0,2},{1,5},{2,0},{3,7},{4,6},{5,1},{6,4},{7,3},{8,10},{9,13},{10,... | collective-permute-start | bytes 1179656 | tf_op jit(solution)/shard_map/ppermute | solution.py:354
  (27 other events, 77.7 us)
